TPU v7x, 32 devices: a whole 2x2x4 slice. The times are simulated.
32 devices in a mesh: grp: 4 (over y, x), fsdp: 8 (over z, core).
Axes of the slice: x: 2, y: 2, z: 4, core: 2. Of those that a mesh axis runs over, the one named last changes fastest.
Arguments:
- hidden: bfloat16 [64, 257, 1024], P(('grp', 'fsdp')), may hold values from -6 to 6
- ln1_gain: float32 [1024], replicated, may hold values from 0.25 to 1.75
- w_qkv: bfloat16 [1024, 3072], P('fsdp'), may hold values from -0.1875 to 0.1875
- w_out: bfloat16 [1024, 1024], P('fsdp'), may hold values from -0.1875 to 0.1875
- ln2_gain: float32 [1024], replicated, may hold values from 0.25 to 1.75
- w_up: bfloat16 [1024, 4096], P('fsdp'), may hold values from -0.1875 to 0.1875
- w_down: bfloat16 [4096, 1024], P('fsdp'), may hold values from -0.09375 to 0.09375
- post_gain: float32 [1024], replicated, may hold values from 0.25 to 1.75
- w_proj: bfloat16 [1024, 256], replicated, may hold values from -0.1875 to 0.1875
- table: float32 [32, 2048, 256], P(('grp', 'fsdp')), may hold values from -6 to 6
- accum: float32 [32, 2048, 256], P(('grp', 'fsdp')), may hold values from 0.1 to 4
- place: int32 [32], replicated, may hold values from 0 to 31, each once
- lookup_table: int32 [4096, 1], P(('grp', 'fsdp')), may hold values from 0 to 31; in each aligned block of 128 rows (0 to 127, 128 to 255, ...) at most 8 rows name the same one
- lookup_row: int32 [4096], P(('grp', 'fsdp')), may hold values from 0 to 2047
Outputs:
- table_new: float32 [32, 2048, 256], P(('grp', 'fsdp'))
- accum_new: float32 [32, 2048, 256], P(('grp', 'fsdp'))
- content_grad: float32 [64, 256], P(('grp', 'fsdp'))
- proj_grad: float32 [1024, 256], P(('grp', 'fsdp'))
Inputs may be any that keep to these rules, and one draw needn't show every extreme that they name: `lookup_table`: within the lookups of one device (aligned blocks of 128), no table is named more than 8 times, a bound that some block reaches. `place`: every device holds exactly one table.
All inputs are finite; a program needn't handle non-finite values.
Results may differ from a plain program's by a relative error of at most 0.0044.
Values may be sent and summed in bfloat16 or wider, within the bound.
No kernel may reach another device: no remote copies, remote signals or barrier semaphores. Data moves between devices by JAX's collectives and lax.ppermute only.
A program may use at most 192 MiB of HBM per device.

v0:
```python
import functools
import math

import jax
import jax.numpy as jnp
from jax import lax
from jax.experimental import pallas as pl
from jax.experimental.pallas import tpu as pltpu
from jax.sharding import PartitionSpec as P

HEADS = 16
LOOK_IMG = 64
CORES = 2
LANES = 128
MIB = 1 << 20

epsilon = 1e-06
learn_rate = 0.5
bf16 = jnp.bfloat16
f32 = jnp.float32
BOTH = ("grp", "fsdp")

VMEM = pl.BlockSpec(memory_space=pltpu.VMEM)
SMEM = pl.BlockSpec(memory_space=pltpu.SMEM)
ANY = pl.BlockSpec(memory_space=pl.ANY)


def norm_rows(values, gain):
    center = jnp.mean(values, axis=-1, keepdims=True)
    shifted = values - center
    spread = jnp.mean(shifted * shifted, axis=-1, keepdims=True)
    return shifted * lax.rsqrt(spread + epsilon) * gain


def spread_shards(shards, grp, fsdp, turn):
    chips = fsdp // CORES
    both = tuple(BOTH)

    def moved(value, target):
        pairs = []
        for index in range(grp * fsdp):
            plane, rest = divmod(index, fsdp)
            chip, core = divmod(rest, CORES)
            there = target(plane, chip, core)
            pairs.append((index, (there[0] * chips + there[1]) * CORES + there[2]))
        return lax.ppermute(value, both, pairs)

    def swap(value, bit):
        return moved(value, lambda g, c, k: (g ^ bit, c, k))

    def sibling(value):
        return moved(value, lambda g, c, k: (g, c, k ^ 1))

    part = jnp.concatenate(
        [
            lax.dynamic_slice_in_dim(s, turn * (s.shape[1] // grp), s.shape[1] // grp, axis=1)
            for s in shards
        ],
        axis=1,
    )
    along = [
        moved(part, lambda g, c, k, step=step: (g, (c - step) % chips, k))
        for step in range(1, chips)
    ]
    mine = jnp.concatenate(along, axis=0)
    one, two = swap(mine, 1), swap(mine, 2)
    half = mine.shape[0] // 2
    low, high = swap(one[:half], 2), swap(two[half:], 1)
    sent = [mine, one, two, low, high]
    return sent, [sibling(v) for v in sent], [sibling(s) for s in shards]


def piece_plan(chips, rows, wide, offset):
    plan = []
    half = (chips - 1) * rows // 2
    for turn in range(3):
        for step in range(1, chips):
            for side in range(2):
                plan.append((1 + turn, (step - 1) * rows, rows, offset, side, step, 0, turn))
    for step in range(1, chips):
        for side in range(2):
            first, last = (step - 1) * rows, step * rows
            for buffer, low, high, base in ((4, 0, half, 0), (5, half, 2 * half, half)):
                start, stop = max(first, low), min(last, high)
                if start < stop:
                    plan.append(
                        (buffer, start - base, stop - start, offset, side, step, start - first, 3)
                    )
    return plan


class Weight:
    def __init__(self, shape, wide, pieces, plan, chips, rows):
        self.shape, self.wide, self.pieces = shape, wide, pieces
        self.plan, self.chips, self.rows = plan, chips, rows

    @property
    def count(self):
        return len(self.pieces)

    @property
    def copies(self):
        return 1 if self.plan is None else 2 + len(self.plan)

    def start(self, refs, whole, sems, pos):
        if self.plan is None:
            copy = pltpu.make_async_copy(refs[0], whole, sems.at[0])
            copy.start()
            return [[copy], [], [], []]
        plane, chip, core = pos[0], pos[1], pos[2]
        groups = [[], [], [], []]
        number = 0

        def go(source, target, turn):
            nonlocal number
            copy = pltpu.make_async_copy(source, target, sems.at[number])
            copy.start()
            groups[turn].append(copy)
            number += 1

        for side in range(2):
            row = pl.multiple_of((chip * CORES + (core ^ side)) * self.rows, self.rows)
            go(refs[side * 6], whole.at[pl.ds(row, self.rows), :], 0)
        for buffer, low, count, column, side, step, inner, turn in self.plan:
            there = lax.rem(chip + step, self.chips)
            row = (there * CORES + (core ^ side)) * self.rows + inner
            row = pl.multiple_of(row, math.gcd(self.rows, inner) if inner else self.rows)
            left = pl.multiple_of((plane ^ turn) * self.wide, LANES)
            go(
                refs[side * 6 + buffer].at[pl.ds(low, count), pl.ds(column, self.wide)],
                whole.at[pl.ds(row, count), pl.ds(left, self.wide)],
                turn,
            )
        return groups

    def each_turn(self, refs, whole, sems, pos, body):
        groups = self.start(refs, whole, sems, pos)
        for turn in range(4):
            for copy in groups[turn]:
                copy.wait()
            left = (pos[0] ^ turn) * self.wide if self.plan is not None else turn * self.wide
            body(left)


def gather_chunks(chunks, grp, fsdp, turn):
    found = []
    chips = fsdp // CORES
    for shards in chunks:
        rows = shards[0].shape[0]
        simple = grp == 4 and fsdp % CORES == 0 and rows % LANES == 0 and chips % 2 == 0
        if simple:
            sent, other, other_own = spread_shards(shards, grp, fsdp, turn)
        offset = 0
        for number, shard in enumerate(shards):
            wide = shard.shape[1] // 4
            shape = (rows * fsdp, shard.shape[1])
            if simple:
                pieces = [shard] + sent + [other_own[number]] + other
                plan = piece_plan(chips, rows, wide, offset)
            else:
                pieces, plan = [lax.all_gather(shard, "fsdp", axis=0, tiled=True)], None
            offset += wide
            found.append(Weight(shape, wide, pieces, plan, chips, rows))
    return found


def block_of(wide):
    return 256 if wide % 256 == 0 else LANES


def call_with_weight(weight, body, pos, inputs, out_shapes, scratch, room, flops, name):
    n_in, n_out = len(inputs), len(out_shapes)

    def kernel(*refs):
        pos_ref = refs[0]
        pieces = refs[1 : 1 + weight.count]
        refs = refs[1 + weight.count :]
        ins, outs, rest = refs[:n_in], refs[n_in : n_in + n_out], refs[n_in + n_out :]
        whole, sems = rest[0], rest[1]

        def each_turn(work):
            weight.each_turn(pieces, whole, sems, pos_ref, work)

        body(ins, outs, rest[2:], whole, each_turn)

    return pl.pallas_call(
        kernel,
        out_shape=out_shapes,
        in_specs=[SMEM] + [ANY] * weight.count + [VMEM] * n_in,
        out_specs=[VMEM] * n_out,
        scratch_shapes=[
            pltpu.VMEM(weight.shape, bf16),
            pltpu.SemaphoreType.DMA((weight.copies,)),
        ]
        + list(scratch),
        compiler_params=pltpu.CompilerParams(vmem_limit_bytes=room * MIB),
        cost_estimate=pl.CostEstimate(flops=flops, bytes_accessed=2 * math.prod(weight.shape), transcendentals=0),
        name=name,
    )(pos, *weight.pieces, *inputs)


def dot32(left, right):
    return jnp.dot(left, right, preferred_element_type=f32)


def column_loop(wide, left, work):
    size = block_of(wide)

    @pl.loop(0, wide // size)
    def _(number):
        work(pl.ds(pl.multiple_of(left + number * size, LANES), size))


def project_qkv(weight, pos, normed):
    def body(ins, outs, scratch, whole, each_turn):
        def quarter(left):
            def work(columns):
                outs[0][:, columns] = dot32(ins[0][...], whole[:, columns]).astype(bf16)

            column_loop(weight.wide, left, work)

        each_turn(quarter)

    rows = normed.shape[0]
    return call_with_weight(
        weight, body, pos, [normed],
        [jax.ShapeDtypeStruct((rows, weight.shape[1]), bf16)], [], 24,
        2 * rows * math.prod(weight.shape), "project_qkv",
    )[0]


def attend(qkv, images, padded, seq, width):
    head_dim = width // HEADS
    per = LANES // head_dim
    blocks = width // LANES
    factor = 1.0 / (math.sqrt(head_dim) * math.log(2.0))

    def kernel(query, keys, values, out):
        q, k, v = query[0], keys[0], values[0]
        lane = lax.broadcasted_iota(jnp.int32, (1, LANES), 1)
        column = lax.broadcasted_iota(jnp.int32, (1, padded), 1)
        beside = jnp.concatenate([v, jnp.ones_like(v)], axis=1)
        total = None
        for head in range(per):
            own = (lane // head_dim) == head
            scores = lax.dot_general(
                jnp.where(own, q, jnp.zeros_like(q)), k,
                (((1,), (1,)), ((), ())), preferred_element_type=f32,
            )
            scores = jnp.where(column < seq, scores, -1e30)
            top = jnp.max(scores, axis=-1, keepdims=True)
            probs = jnp.exp2((scores - top) * factor).astype(bf16)
            both = dot32(probs, beside)
            mixed = both[:, :LANES] / both[:, LANES:]
            total = mixed if total is None else jnp.where(own, mixed, total)
        out[0] = total.astype(bf16)

    spec = lambda shift: pl.BlockSpec((1, padded, LANES), lambda i, h: (i, 0, h + shift * blocks))
    shaped = qkv.reshape(images, padded, 3 * width)
    mixed = pl.pallas_call(
        kernel,
        grid=(images, blocks),
        out_shape=jax.ShapeDtypeStruct((images, padded, width), bf16),
        in_specs=[spec(0), spec(1), spec(2)],
        out_specs=spec(0),
        compiler_params=pltpu.CompilerParams(vmem_limit_bytes=16 * MIB),
        cost_estimate=pl.CostEstimate(
            flops=8 * images * padded * padded * width, bytes_accessed=8 * images * padded * width,
            transcendentals=images * HEADS * padded * padded,
        ),
        name="attend",
    )(shaped, shaped, shaped)
    return mixed.reshape(images * padded, width)


def project_out(weight, pos, mixed, tokens, gain):
    rows, width = mixed.shape

    def body(ins, outs, scratch, whole, each_turn):
        mixed_ref, tokens_ref, gain_ref = ins
        resid, normed = outs

        def quarter(left):
            def work(columns):
                product = dot32(mixed_ref[...], whole[:, columns])
                resid[:, columns] = (tokens_ref[:, columns].astype(f32) + product).astype(bf16)

            column_loop(weight.wide, left, work)

        each_turn(quarter)
        step = 32 if rows % 32 == 0 else 16

        @pl.loop(0, rows // step)
        def _(number):
            at = pl.ds(pl.multiple_of(number * step, step), step)
            normed[at, :] = norm_rows(resid[at, :].astype(f32), gain_ref[...]).astype(bf16)

    shape = jax.ShapeDtypeStruct((rows, width), bf16)
    return call_with_weight(
        weight, body, pos, [mixed, tokens, gain.reshape(1, -1)], [shape, shape], [], 16,
        2 * rows * math.prod(weight.shape), "project_out",
    )


def gelu(values):
    return 0.5 * values * (1.0 + lax.erf(values * math.sqrt(0.5)))


def project_up(weight, pos, normed):
    rows = normed.shape[0]

    def body(ins, outs, scratch, whole, each_turn):
        def quarter(left):
            def work(columns):
                outs[0][:, columns] = gelu(dot32(ins[0][...], whole[:, columns])).astype(bf16)

            column_loop(weight.wide, left, work)

        each_turn(quarter)

    return call_with_weight(
        weight, body, pos, [normed],
        [jax.ShapeDtypeStruct((rows, weight.shape[1]), bf16)], [], 28,
        4 * rows * math.prod(weight.shape), "project_up",
    )[0]


def project_down(weight, pos, active, resid, gain, images, seq, devices):
    rows, width = resid.shape
    padded = rows // images

    def body(ins, outs, scratch, whole, each_turn):
        active_ref, resid_ref, gain_ref = ins
        (final,) = scratch
        (pooled,) = outs

        def quarter(left):
            def work(columns):
                product = dot32(active_ref[...], whole[:, columns])
                final[:, columns] = resid_ref[:, columns].astype(f32) + product

            column_loop(weight.wide, left, work)

        each_turn(quarter)
        step = 16
        for image in range(images):

            def add(number, total):
                at = pl.ds(pl.multiple_of(image * padded + number * step, step), step)
                posted = norm_rows(final[at, :], gain_ref[...])
                row = lax.broadcasted_iota(jnp.int32, (step, 1), 0) + number * step
                return total + jnp.where(row < seq, posted, 0.0)

            total = lax.fori_loop(0, padded // step, add, jnp.zeros((step, width), f32))
            mean = (jnp.sum(total, axis=0, keepdims=True) / seq).astype(bf16)
            for device in range(devices):
                pooled[device, image : image + 1, :] = mean

    return call_with_weight(
        weight, body, pos, [active, resid, gain.reshape(1, -1)],
        [jax.ShapeDtypeStruct((devices, images, width), bf16)],
        [pltpu.VMEM((rows, width), f32)], 32,
        2 * rows * math.prod(weight.shape), "project_down",
    )[0]


def thirds(values):
    first = values.astype(bf16)
    left = values - first.astype(f32)
    second = left.astype(bf16)
    return first, second, (left - second.astype(f32)).astype(bf16)


def update(pos, every, proj, sums, named, table, accum, images, share):
    rows, width = table.shape
    every_image, depth = every.shape
    blocks = rows // LANES
    per = 4 if blocks % 4 == 0 else 1
    side = max(share, LANES)
    over = (((0,), (0,)), ((), ()))

    def kernel(pos_ref, every_ref, proj_ref, sums_ref, named_ref, table_ref, accum_ref,
               table_out, accum_out, content_out, proj_out, units, grads, square):
        @pl.when(pl.program_id(0) == 0)
        def _():
            content = dot32(every_ref[...], proj_ref[...])
            scale = lax.rsqrt(jnp.mean(content * content, axis=-1, keepdims=True) + epsilon)
            unit = content * scale
            for number, part in enumerate(thirds(unit)):
                units[number * every_image : (number + 1) * every_image, :] = part
            grad_unit = LOOK_IMG * unit - sums_ref[...]
            inner = jnp.mean(grad_unit * unit, axis=-1, keepdims=True)
            grad = scale * (grad_unit - unit * inner)
            grads[...] = grad
            me = pos_ref[3]
            for image in range(images):
                content_out[image : image + 1, :] = grads[pl.ds(me * images + image, 1), :]
            column = me * share
            block = pl.multiple_of((column // side) * side, side)
            mine = every_ref[:, pl.ds(block, side)]
            total = None
            for part in thirds(grad):
                product = lax.dot_general(mine, part, over, preferred_element_type=f32)
                total = product if total is None else total + product
            square[...] = total
            unit_rows = math.gcd(share, side)
            proj_out[...] = square[pl.ds(pl.multiple_of(column - block, unit_rows), share), :]

        ones = jnp.ones((every_image, width), bf16)
        for number in range(per):
            at = slice(number * LANES, (number + 1) * LANES)
            count = named_ref[number]
            times = lax.dot_general(count, ones, over, preferred_element_type=f32)
            taken = None
            for part in range(3):
                product = lax.dot_general(
                    count, units[part * every_image : (part + 1) * every_image, :], over,
                    preferred_element_type=f32,
                )
                taken = product if taken is None else taken + product
            old = table_ref[at, :]
            grad_rows = times * old - taken
            grown = accum_ref[at, :] + grad_rows * grad_rows
            accum_out[at, :] = grown
            table_out[at, :] = old - learn_rate * grad_rows / jnp.sqrt(grown)

    whole = lambda shape: pl.BlockSpec(shape, lambda i: (0,) * len(shape))
    strip = pl.BlockSpec((per * LANES, width), lambda i: (i, 0))
    return pl.pallas_call(
        kernel,
        grid=(blocks // per,),
        out_shape=[
            jax.ShapeDtypeStruct(table.shape, f32),
            jax.ShapeDtypeStruct(table.shape, f32),
            jax.ShapeDtypeStruct((images, width), f32),
            jax.ShapeDtypeStruct((share, width), f32),
        ],
        in_specs=[
            SMEM, whole(every.shape), whole(proj.shape), whole(sums.shape),
            pl.BlockSpec((per, every_image, LANES), lambda i: (i, 0, 0)), strip, strip,
        ],
        out_specs=[strip, strip, whole((images, width)), whole((share, width))],
        scratch_shapes=[
            pltpu.VMEM((3 * every_image, width), bf16),
            pltpu.VMEM((every_image, width), f32),
            pltpu.VMEM((side, width), f32),
        ],
        compiler_params=pltpu.CompilerParams(vmem_limit_bytes=24 * MIB),
        name="update",
    )(pos, every, proj, sums, named, table, accum)


def broadcast_all(value, devices):
    return lax.all_to_all(
        jnp.broadcast_to(value[None], (devices,) + value.shape), BOTH, 0, 0, tiled=True
    )


def on_device(
    hidden, ln1_gain, w_qkv, w_out, ln2_gain, w_up, w_down, post_gain, w_proj,
    table, accum, place, lookup_table, lookup_row,
):
    images, seq, width = hidden.shape
    grp, fsdp = lax.axis_size("grp"), lax.axis_size("fsdp")
    devices = grp * fsdp
    plane, spot = lax.axis_index("grp"), lax.axis_index("fsdp")
    me = plane * fsdp + spot
    pos = jnp.stack([plane, spot // CORES, spot % CORES, me]).astype(jnp.int32)

    qkv_w, out_w, up_w, down_w = gather_chunks(
        [[w_qkv], [w_out, w_up], [w_down]], grp, fsdp, plane
    )

    rows_dev, proj_width = table.shape[1:]
    every_image = images * devices
    my_table = jnp.sum(jnp.where(place == me, jnp.arange(place.shape[0], dtype=jnp.int32), 0))
    both = jnp.stack([lookup_table[:, 0], lookup_row])
    named = broadcast_all(both, devices)
    tables = named[:, 0].reshape(every_image, LOOK_IMG)
    rows = named[:, 1].reshape(every_image, LOOK_IMG)
    high = jnp.where(tables == my_table, rows // LANES, -1)
    left = (high[:, :, None] == jnp.arange(rows_dev // LANES)[None, None, :]).astype(bf16)
    right = ((rows % LANES)[:, :, None] == jnp.arange(LANES)[None, None, :]).astype(bf16)
    counts = jnp.einsum("ilh,ilr->ihr", left, right, preferred_element_type=f32)
    partial = jnp.dot(
        counts.reshape(every_image, rows_dev), table[0],
        precision=lax.Precision.HIGHEST, preferred_element_type=f32,
    )
    shares = lax.all_to_all(
        partial.reshape(devices, images, proj_width), BOTH, 0, 0, tiled=True
    )
    sums = broadcast_all(jnp.sum(shares, axis=0), devices).reshape(every_image, proj_width)
    counts = jnp.transpose(counts, (1, 0, 2)).astype(bf16)

    padded = -(-seq // 16) * 16
    tokens = jnp.pad(hidden, ((0, 0), (0, padded - seq), (0, 0))).reshape(images * padded, width)
    normed = norm_rows(tokens.astype(f32), ln1_gain).astype(bf16)
    qkv = project_qkv(qkv_w, pos, normed)
    mixed = attend(qkv, images, padded, seq, width)
    resid, normed_two = project_out(out_w, pos, mixed, tokens, ln2_gain)
    active = project_up(up_w, pos, normed_two)
    pooled = project_down(down_w, pos, active, resid, post_gain, images, seq, devices)
    every = lax.all_to_all(pooled, BOTH, 0, 0, tiled=True).reshape(every_image, width)
    table_new, accum_new, content_grad, proj_grad = update(
        pos, every, w_proj, sums, counts, table[0], accum[0], images, width // devices
    )
    return table_new[None], accum_new[None], content_grad, proj_grad


def solution(mesh):
    rows = P(("grp", "fsdp"), None)
    deep = P(("grp", "fsdp"), None, None)
    split = P("fsdp", None)
    placed = (
        deep, P(), split, split, P(), split, split, P(), P(), deep, deep, P(), rows, P(("grp", "fsdp")),
    )
    return jax.shard_map(
        on_device, mesh=mesh, in_specs=placed, out_specs=(deep, deep, rows, rows), check_vma=False
    )
```

profile of v0, /device:TPU:1, one launch (start us, length us, event | category | flops | bytes accessed | tf_op | source)
XLA Modules:
  0.0 268.5 jit_solution(1804904122614172688)
XLA Ops:
  0.6 0.9 constant_dynamic-slice_fusion
  1.6 4.2 %collective-permute-start.27 = (bf16[128,768]{1,0:T(8,128)(2,1)S(1)}, bf16[128,768]{1,0:T(8,128)(2,1)S(1)}, u32[]{:S(2)}, u32[]{:S(2)}) collective-permute-start(bf16[128,768]{1,0:T(8,128)(2,1)S(1)} %constant_dynamic-slice_fusion), channel_id=1, source_target_pairs={{0,6},{1,7},{2,0},{3,1},{4,2},{5,3},{6,4},{7,5},{8,14},{9,15},{10,... | collective-permute-start | bytes 589832 | tf_op jit(solution)/shard_map/ppermute | solution.py:46
  6.3 1.5 collective-permute-start.34
  7.8 1.0 constant_dynamic-slice_fusion.3
  8.7 2.6 collective-permute-start
  11.3 0.8 constant_dynamic-slice_fusion.2
  12.2 1.0 constant_dynamic-slice_fusion.1
  13.2 0.9 collective-permute-start.1
  14.8 7.4 %collective-permute-done.28 = bf16[128,768]{1,0:T(8,128)(2,1)S(1)} collective-permute-done((bf16[128,768]{1,0:T(8,128)(2,1)S(1)}, bf16[128,768]{1,0:T(8,128)(2,1)S(1)}, u32[]{:S(2)}, u32[]{:S(2)}) %collective-permute-start.28) | collective-permute-done | bytes 196640 | tf_op jit(solution)/shard_map/ppermute | solution.py:46
  22.9 3.3 %collective-permute-start.13 = (bf16[128,1280]{1,0:T(8,128)(2,1)S(1)}, bf16[128,1280]{1,0:T(8,128)(2,1)S(1)}, u32[]{:S(2)}, u32[]{:S(2)}) collective-permute-start(bf16[128,1280]{1,0:T(8,128)(2,1)S(1)} %pad_maximum_fusion), channel_id=1, source_target_pairs={{0,6},{1,7},{2,0},{3,1},{4,2},{5,3},{6,4},{7,5},{8,14},{9,15},{10,... | collective-permute-start | bytes 983048 | tf_op jit(solution)/shard_map/ppermute | solution.py:46
  26.8 11.5 %collective-permute-start.14 = (bf16[128,1280]{1,0:T(8,128)(2,1)S(1)}, bf16[128,1280]{1,0:T(8,128)(2,1)S(1)}, u32[]{:S(2)}, u32[]{:S(2)}) collective-permute-start(bf16[128,1280]{1,0:T(8,128)(2,1)S(1)} %pad_maximum_fusion), channel_id=1, source_target_pairs={{0,4},{1,5},{2,6},{3,7},{4,0},{5,1},{6,2},{7,3},{8,12},{9,13},{10,... | collective-permute-start | bytes 983048 | tf_op jit(solution)/shard_map/ppermute | solution.py:46
  39.0 7.6 %collective-permute-done.1 = bf16[512,256]{1,0:T(8,128)(2,1)S(1)} collective-permute-done((bf16[512,256]{1,0:T(8,128)(2,1)S(1)}, bf16[512,256]{1,0:T(8,128)(2,1)S(1)}, u32[]{:S(2)}, u32[]{:S(2)}) %collective-permute-start.1) | collective-permute-done | bytes 262176 | tf_op jit(solution)/shard_map/ppermute | solution.py:46
  46.6 7.1 %collective-permute-start.15 = (bf16[128,1280]{1,0:T(8,128)(2,1)S(1)}, bf16[128,1280]{1,0:T(8,128)(2,1)S(1)}, u32[]{:S(2)}, u32[]{:S(2)}) collective-permute-start(bf16[128,1280]{1,0:T(8,128)(2,1)S(1)} %pad_maximum_fusion), channel_id=1, source_target_pairs={{0,2},{1,3},{2,4},{3,5},{4,6},{5,7},{6,0},{7,1},{8,10},{9,11},{10,... | collective-permute-start | bytes 983048 | tf_op jit(solution)/shard_map/ppermute | solution.py:46
  54.4 2.4 collective-permute-start.26
  57.6 1.2 collective-permute-start.30
  59.6 1.2 collective-permute-start.31
  60.8 11.9 %collective-permute-done.14 = bf16[128,1280]{1,0:T(8,128)(2,1)S(1)} collective-permute-done((bf16[128,1280]{1,0:T(8,128)(2,1)S(1)}, bf16[128,1280]{1,0:T(8,128)(2,1)S(1)}, u32[]{:S(2)}, u32[]{:S(2)}) %collective-permute-start.14) | collective-permute-done | bytes 327712 | tf_op jit(solution)/shard_map/ppermute | solution.py:46
  72.8 1.3 collective-permute-start.35
  74.1 1.2 collective-permute-start.3
  77.8 10.5 %all-to-all-start.1 = ((s32[32,2,128]{2,1,0:T(2,128)}), s32[32,2,128]{2,1,0:T(2,128)}, u32[]{:S(2)}, u32[]{:S(2)}) async-start(s32[32,2,128]{2,1,0:T(2,128)} %broadcast_in_dim.14), calls=%async_computation.1 | async-start | bytes 65536 | tf_op jit(solution)/shard_map/all_to_all | solution.py:454
  88.4 1.5 collective-permute-start.17
  90.5 2.4 convert_reduce_fusion
  93.8 1.2 collective-permute-start.4
  95.8 22.7 %collective-permute-done.32.refs_5_ = bf16[192,768]{1,0:T(8,128)(2,1)} collective-permute-done((bf16[192,768]{1,0:T(8,128)(2,1)S(1)}, bf16[192,768]{1,0:T(8,128)(2,1)}, u32[]{:S(2)}, u32[]{:S(2)}) %collective-permute-start.32) | collective-permute-done | bytes 294944 | tf_op jit(solution)/shard_map/ppermute | solution.py:46
  118.5 1.4 collective-permute-start.33
  119.8 2.2 fusion.1
  122.0 2.2 collective-permute-start.38
  125.7 2.5 collective-permute-start.39
  128.2 7.0 %collective-permute-done.4.refs_4_ = bf16[1536,256]{1,0:T(8,128)(2,1)S(1)} collective-permute-done((bf16[1536,256]{1,0:T(8,128)(2,1)}, bf16[1536,256]{1,0:T(8,128)(2,1)S(1)}, u32[]{:S(2)}, u32[]{:S(2)}) %collective-permute-start.4) | collective-permute-done | bytes 786464 | tf_op jit(solution)/shard_map/ppermute | solution.py:46
  135.2 1.3 collective-permute-start.18
  137.2 2.5 copy.51
  140.1 1.3 pad.4.clone
  141.5 1.5 collective-permute-start.36
  143.9 1.8 slice.35
  145.7 1.2 collective-permute-start.19
  146.9 1.4 compare_reduce_fusion
  149.3 1.6 fusion.4
  151.0 2.1 dot_general.9
  153.7 4.7 %collective-permute-done.19.refs_6_ = bf16[192,1280]{1,0:T(8,128)(2,1)} collective-permute-done((bf16[192,1280]{1,0:T(8,128)(2,1)}, bf16[192,1280]{1,0:T(8,128)(2,1)}, u32[]{:S(2)}, u32[]{:S(2)}) %collective-permute-start.19) | collective-permute-done | bytes 491552 | tf_op jit(solution)/shard_map/ppermute | solution.py:46
  158.4 1.3 collective-permute-start.25
  159.7 2.4 fusion.2
  162.7 4.3 %all-to-all-start.2 = ((f32[32,2,256]{2,1,0:T(2,128)}), f32[32,2,256]{2,1,0:T(2,128)S(1)}, u32[]{:S(2)}, u32[]{:S(2)}) async-start(f32[32,2,256]{2,1,0:T(2,128)} %copy.42), calls=%async_computation.2 | async-start | bytes 131072 | tf_op jit(solution)/shard_map/all_to_all | solution.py:489
  167.4 1.4 multiply_convert_fusion.refs_13_
  168.9 5.4 %all-to-all-done.2 = f32[32,2,256]{2,1,0:T(2,128)S(1)} async-done(((f32[32,2,256]{2,1,0:T(2,128)}), f32[32,2,256]{2,1,0:T(2,128)S(1)}, u32[]{:S(2)}, u32[]{:S(2)}) %all-to-all-start.2) | async-done | bytes 65568 | tf_op jit(solution)/shard_map/all_to_all | solution.py:489
  175.0 2.6 all-to-all-start.3
  177.6 1.1 slice.32
  178.7 1.0 slice.33
  179.7 1.5 collective-permute-start.5
  181.2 1.2 collective-permute-start.6
  182.4 1.2 copy-done.4
  183.6 1.1 copy-done.14
  184.7 1.1 copy-done.16
  185.8 1.1 copy-done.19
  186.9 8.0 %project_qkv.1 = bf16[544,3072]{1,0:T(8,128)(2,1)S(1)} custom-call(s32[4]{0:T(128)S(1)} %pad_add_fusion.1.refs_0_.pos_ref, bf16[128,3072]{1,0:T(8,128)(2,1)S(1)} %copy-done.19, bf16[384,768]{1,0:T(8,128)(2,1)} %constant_dynamic-update-slice_fusion.6.refs_2_, bf16[384,768]{1,0:T(8,128)(2,1)S(1)} %copy-done.14, bf16[384,768]{1,0:T(8,128)(2,1)S(1)} %copy-done.16, ...), custom_call_target="tpu_custom_call" | custom-call | flops 3422552064 | bytes 6291456 | tf_op jit(solution)/shard_map/project_qkv/pallas_call | solution.py:186
  195.0 1.0 collective-permute-start.7
  195.9 15.0 %attend.1 = bf16[2,272,1024]{2,1,0:T(8,128)(2,1)S(1)} custom-call(bf16[2,272,3072]{2,1,0:T(8,128)(2,1)S(1)} %bitcast.22, bf16[2,272,3072]{2,1,0:T(8,128)(2,1)S(1)} %bitcast.23, bf16[2,272,3072]{2,1,0:T(8,128)(2,1)S(1)} %bitcast.24), custom_call_target="tpu_custom_call" | custom-call | flops 1212153856 | bytes 4456448 | tf_op jit(solution)/shard_map/attend/pallas_call | solution.py:260
  211.0 8.3 %project_out.1 = (bf16[544,1024]{1,0:T(8,128)(2,1)S(1)}, bf16[544,1024]{1,0:T(8,128)(2,1)S(1)}) custom-call(s32[4]{0:T(128)S(1)} %pad_add_fusion.1.refs_0_.pos_ref, bf16[128,1024]{1,0:T(8,128)(2,1)S(1)} %copy-done.6, bf16[384,1280]{1,0:T(8,128)(2,1)} %constant_dynamic-update-slice_fusion.3.refs_2_, bf16[384,1280]{1,0:T(8,128)(2,1)S(1)} %copy-done.2, ...), custom_call_target="tpu_custom_call" | custom-call | flops 1140850688 | bytes 2097152 | tf_op jit(solution)/shard_map/project_out/pallas_call | solution.py:186
  220.5 10.3 %project_up.1.refs_13_ = bf16[544,4096]{1,0:T(8,128)(2,1)S(1)} custom-call(s32[4]{0:T(128)S(1)} %pad_add_fusion.1.refs_0_.pos_ref, bf16[128,4096]{1,0:T(8,128)(2,1)S(1)} %copy-done.17, bf16[384,1280]{1,0:T(8,128)(2,1)} %constant_dynamic-update-slice_fusion.3.refs_2_, bf16[384,1280]{1,0:T(8,128)(2,1)S(1)} %copy-done.2, ...), custom_call_target="tpu_custom_call" | custom-call | flops 9126805504 | bytes 8388608 | tf_op jit(solution)/shard_map/project_up/pallas_call | solution.py:186
  230.8 19.2 %project_down.1 = bf16[32,2,1024]{2,1,0:T(2,128)(2,1)} custom-call(s32[4]{0:T(128)S(1)} %pad_add_fusion.1.refs_0_.pos_ref, bf16[512,1024]{1,0:T(8,128)(2,1)S(1)} %copy-done.18, bf16[1536,256]{1,0:T(8,128)(2,1)} %constant_dynamic-update-slice_fusion.refs_2_, bf16[1536,256]{1,0:T(8,128)(2,1)S(1)} %copy-done.10, bf16[1536,256]{1,0:T(8,128)(2,1)S(1)} %copy-done.12, ...), custom_call_target="tpu_custom_call" | custom-call | flops 4563402752 | bytes 8388608 | tf_op jit(solution)/shard_map/project_down/pallas_call | solution.py:186
  250.0 3.7 %all-to-all-start = ((bf16[32,2,1024]{2,1,0:T(2,128)(2,1)}), bf16[32,2,1024]{2,1,0:T(2,128)(2,1)S(1)}, u32[]{:S(2)}, u32[]{:S(2)}) async-start(bf16[32,2,1024]{2,1,0:T(2,128)(2,1)} %project_down.1), calls=%async_computation | async-start | bytes 262144 | tf_op jit(solution)/shard_map/all_to_all | solution.py:503
  253.7 1.2 copy.52
  255.0 7.0 %all-to-all-done = bf16[32,2,1024]{2,1,0:T(2,128)(2,1)S(1)} async-done(((bf16[32,2,1024]{2,1,0:T(2,128)(2,1)}), bf16[32,2,1024]{2,1,0:T(2,128)(2,1)S(1)}, u32[]{:S(2)}, u32[]{:S(2)}) %all-to-all-start) | async-done | bytes 131104 | tf_op jit(solution)/shard_map/all_to_all | solution.py:503
  262.0 1.6 copy-done.3
  263.6 4.9 %update.1 = (f32[2048,256]{1,0:T(8,128)}, f32[2048,256]{1,0:T(8,128)}, f32[2,256]{1,0:T(2,128)}, f32[32,256]{1,0:T(8,128)}) custom-call(s32[4]{0:T(128)S(1)} %pad_add_fusion.1.refs_0_.pos_ref, bf16[64,1024]{1,0:T(8,128)(2,1)S(1)} %reshape.130.every_ref, bf16[1024,256]{1,0:T(8,128)(2,1)S(1)} %copy-done.5, f32[64,256]{1,0:T(8,128)S(1)} %reshape.131.sums_ref, ...), custom_call_target="tpu_custom_call" | custom-call | tf_op jit(solution)/shard_map/update/pallas_call | solution.py:429
  (135 shorter events, 18.3 us)
Async XLA Ops:
  1.6 52.9 %copy-start.6 = (bf16[128,1024]{1,0:T(8,128)(2,1)S(1)}, bf16[128,1024]{1,0:T(8,128)(2,1)}, u32[]{:S(2)}) copy-start(bf16[128,1024]{1,0:T(8,128)(2,1)} %refs_1_.5) | copy-start | bytes 786436
  1.6 11.6 %collective-permute-start.27 = (bf16[128,768]{1,0:T(8,128)(2,1)S(1)}, bf16[128,768]{1,0:T(8,128)(2,1)S(1)}, u32[]{:S(2)}, u32[]{:S(2)}) collective-permute-start(bf16[128,768]{1,0:T(8,128)(2,1)S(1)} %constant_dynamic-slice_fusion), channel_id=1, source_target_pairs={{0,6},{1,7},{2,0},{3,1},{4,2},{5,3},{6,4},{7,5},{8,14},{9,15},{10,... | collective-permute-start | bytes 589832 | tf_op jit(solution)/shard_map/ppermute | solution.py:46
  5.8 16.4 %collective-permute-start.28 = (bf16[128,768]{1,0:T(8,128)(2,1)S(1)}, bf16[128,768]{1,0:T(8,128)(2,1)S(1)}, u32[]{:S(2)}, u32[]{:S(2)}) collective-permute-start(bf16[128,768]{1,0:T(8,128)(2,1)S(1)} %constant_dynamic-slice_fusion), channel_id=1, source_target_pairs={{0,4},{1,5},{2,6},{3,7},{4,0},{5,1},{6,2},{7,3},{8,12},{9,13},{10,... | collective-permute-start | bytes 589832 | tf_op jit(solution)/shard_map/ppermute | solution.py:46
  5.8 17.0 %collective-permute-start.29 = (bf16[128,768]{1,0:T(8,128)(2,1)S(1)}, bf16[128,768]{1,0:T(8,128)(2,1)S(1)}, u32[]{:S(2)}, u32[]{:S(2)}) collective-permute-start(bf16[128,768]{1,0:T(8,128)(2,1)S(1)} %constant_dynamic-slice_fusion), channel_id=1, source_target_pairs={{0,2},{1,3},{2,4},{3,5},{4,6},{5,7},{6,0},{7,1},{8,10},{9,11},{10,... | collective-permute-start | bytes 589832 | tf_op jit(solution)/shard_map/ppermute | solution.py:46
  6.3 84.2 %collective-permute-start.34 = (bf16[128,3072]{1,0:T(8,128)(2,1)}, bf16[128,3072]{1,0:T(8,128)(2,1)}, u32[]{:S(2)}, u32[]{:S(2)}) collective-permute-start(bf16[128,3072]{1,0:T(8,128)(2,1)} %refs_1_.4), channel_id=1, source_target_pairs={{0,1},{1,0},{2,3},{3,2},{4,5},{5,4},{6,7},{7,6},{8,9},{9,8},{10,11... | collective-permute-start | bytes 2359304 | tf_op jit(solution)/shard_map/ppermute | solution.py:46
  8.7 18.1 %collective-permute-start = (bf16[512,256]{1,0:T(8,128)(2,1)S(1)}, bf16[512,256]{1,0:T(8,128)(2,1)S(1)}, u32[]{:S(2)}, u32[]{:S(2)}) collective-permute-start(bf16[512,256]{1,0:T(8,128)(2,1)S(1)} %constant_dynamic-slice_fusion.3), channel_id=1, source_target_pairs={{0,6},{1,7},{2,0},{3,1},{4,2},{5,3},{6,4},{7,5},{8,14},{9,15},{10,... | collective-permute-start | bytes 786440 | tf_op jit(solution)/shard_map/ppermute | solution.py:46
  13.2 33.5 %collective-permute-start.1 = (bf16[512,256]{1,0:T(8,128)(2,1)S(1)}, bf16[512,256]{1,0:T(8,128)(2,1)S(1)}, u32[]{:S(2)}, u32[]{:S(2)}) collective-permute-start(bf16[512,256]{1,0:T(8,128)(2,1)S(1)} %constant_dynamic-slice_fusion.3), channel_id=1, source_target_pairs={{0,4},{1,5},{2,6},{3,7},{4,0},{5,1},{6,2},{7,3},{8,12},{9,13},{10,... | collective-permute-start | bytes 786440 | tf_op jit(solution)/shard_map/ppermute | solution.py:46
  14.8 62.4 %copy-start.25 = (s32[128]{0:T(128)S(1)}, s32[128]{0:T(128)}, u32[]{:S(2)}) copy-start(s32[128]{0:T(128)} %param.27) | copy-start | bytes 1540
  14.8 62.4 %copy-start.26 = (s32[128,1]{0,1:T(1,128)S(1)}, s32[128,1]{0,1:T(1,128)}, u32[]{:S(2)}) copy-start(s32[128,1]{0,1:T(1,128)} %param.26) | copy-start | bytes 1540
  22.2 32.3 %collective-permute-start.2 = (bf16[512,256]{1,0:T(8,128)(2,1)S(1)}, bf16[512,256]{1,0:T(8,128)(2,1)S(1)}, u32[]{:S(2)}, u32[]{:S(2)}) collective-permute-start(bf16[512,256]{1,0:T(8,128)(2,1)S(1)} %constant_dynamic-slice_fusion.3), channel_id=1, source_target_pairs={{0,2},{1,3},{2,4},{3,5},{4,6},{5,7},{6,0},{7,1},{8,10},{9,11},{10,... | collective-permute-start | bytes 786440 | tf_op jit(solution)/shard_map/ppermute | solution.py:46
  22.9 34.8 %collective-permute-start.13 = (bf16[128,1280]{1,0:T(8,128)(2,1)S(1)}, bf16[128,1280]{1,0:T(8,128)(2,1)S(1)}, u32[]{:S(2)}, u32[]{:S(2)}) collective-permute-start(bf16[128,1280]{1,0:T(8,128)(2,1)S(1)} %pad_maximum_fusion), channel_id=1, source_target_pairs={{0,6},{1,7},{2,0},{3,1},{4,2},{5,3},{6,4},{7,5},{8,14},{9,15},{10,... | collective-permute-start | bytes 983048 | tf_op jit(solution)/shard_map/ppermute | solution.py:46
  26.8 46.0 %collective-permute-start.14 = (bf16[128,1280]{1,0:T(8,128)(2,1)S(1)}, bf16[128,1280]{1,0:T(8,128)(2,1)S(1)}, u32[]{:S(2)}, u32[]{:S(2)}) collective-permute-start(bf16[128,1280]{1,0:T(8,128)(2,1)S(1)} %pad_maximum_fusion), channel_id=1, source_target_pairs={{0,4},{1,5},{2,6},{3,7},{4,0},{5,1},{6,2},{7,3},{8,12},{9,13},{10,... | collective-permute-start | bytes 983048 | tf_op jit(solution)/shard_map/ppermute | solution.py:46
  46.6 27.5 %collective-permute-start.15 = (bf16[128,1280]{1,0:T(8,128)(2,1)S(1)}, bf16[128,1280]{1,0:T(8,128)(2,1)S(1)}, u32[]{:S(2)}, u32[]{:S(2)}) collective-permute-start(bf16[128,1280]{1,0:T(8,128)(2,1)S(1)} %pad_maximum_fusion), channel_id=1, source_target_pairs={{0,2},{1,3},{2,4},{3,5},{4,6},{5,7},{6,0},{7,1},{8,10},{9,11},{10,... | collective-permute-start | bytes 983048 | tf_op jit(solution)/shard_map/ppermute | solution.py:46
  54.4 5.1 %collective-permute-start.26 = (bf16[128,1024]{1,0:T(8,128)(2,1)S(1)}, bf16[128,1024]{1,0:T(8,128)(2,1)S(1)}, u32[]{:S(2)}, u32[]{:S(2)}) collective-permute-start(bf16[128,1024]{1,0:T(8,128)(2,1)S(1)} %copy-done.6), channel_id=1, source_target_pairs={{0,1},{1,0},{2,3},{3,2},{4,5},{5,4},{6,7},{7,6},{8,9},{9,8},{10,11... | collective-permute-start | bytes 786440 | tf_op jit(solution)/shard_map/ppermute | solution.py:46
  57.6 19.2 %collective-permute-start.30 = (bf16[384,768]{1,0:T(8,128)(2,1)}, bf16[384,768]{1,0:T(8,128)(2,1)S(1)}, u32[]{:S(2)}, u32[]{:S(2)}) collective-permute-start(bf16[384,768]{1,0:T(8,128)(2,1)} %constant_dynamic-update-slice_fusion.6.refs_2_), channel_id=1, source_target_pairs={{0,8},{1,9},{2,10},{3,11},{4,12},{5,13},{6,14},{7,15},{8,0},{9,1},... | collective-permute-start | bytes 1769480 | tf_op jit(solution)/shard_map/ppermute | solution.py:46
  59.6 17.2 %copy-start.7 = (bf16[128,1024]{1,0:T(8,128)(2,1)}, bf16[128,1024]{1,0:T(8,128)(2,1)S(1)}, u32[]{:S(2)}) copy-start(bf16[128,1024]{1,0:T(8,128)(2,1)S(1)} %collective-permute-done.26.refs_7_) | copy-start | bytes 786436
  59.6 28.8 %collective-permute-start.31 = (bf16[384,768]{1,0:T(8,128)(2,1)}, bf16[384,768]{1,0:T(8,128)(2,1)S(1)}, u32[]{:S(2)}, u32[]{:S(2)}) collective-permute-start(bf16[384,768]{1,0:T(8,128)(2,1)} %constant_dynamic-update-slice_fusion.6.refs_2_), channel_id=1, source_target_pairs={{0,16},{1,17},{2,18},{3,19},{4,20},{5,21},{6,22},{7,23},{8,24},{9,... | collective-permute-start | bytes 1769480 | tf_op jit(solution)/shard_map/ppermute | solution.py:46
  72.8 17.1 %collective-permute-start.35 = (bf16[384,768]{1,0:T(8,128)(2,1)}, bf16[384,768]{1,0:T(8,128)(2,1)}, u32[]{:S(2)}, u32[]{:S(2)}) collective-permute-start(bf16[384,768]{1,0:T(8,128)(2,1)} %constant_dynamic-update-slice_fusion.6.refs_2_), channel_id=1, source_target_pairs={{0,1},{1,0},{2,3},{3,2},{4,5},{5,4},{6,7},{7,6},{8,9},{9,8},{10,11... | collective-permute-start | bytes 1769480 | tf_op jit(solution)/shard_map/ppermute | solution.py:46
  74.1 19.7 %collective-permute-start.3 = (bf16[1536,256]{1,0:T(8,128)(2,1)}, bf16[1536,256]{1,0:T(8,128)(2,1)S(1)}, u32[]{:S(2)}, u32[]{:S(2)}) collective-permute-start(bf16[1536,256]{1,0:T(8,128)(2,1)} %constant_dynamic-update-slice_fusion.refs_2_), channel_id=1, source_target_pairs={{0,8},{1,9},{2,10},{3,11},{4,12},{5,13},{6,14},{7,15},{8,0},{9,1},... | collective-permute-start | bytes 2359304 | tf_op jit(solution)/shard_map/ppermute | solution.py:46
  76.8 16.1 %copy-start.13 = (bf16[384,768]{1,0:T(8,128)(2,1)}, bf16[384,768]{1,0:T(8,128)(2,1)S(1)}, u32[]{:S(2)}) copy-start(bf16[384,768]{1,0:T(8,128)(2,1)S(1)} %collective-permute-done.30.refs_3_) | copy-start | bytes 1769476
  76.8 45.2 %collective-permute-start.16 = (bf16[384,1280]{1,0:T(8,128)(2,1)}, bf16[384,1280]{1,0:T(8,128)(2,1)S(1)}, u32[]{:S(2)}, u32[]{:S(2)}) collective-permute-start(bf16[384,1280]{1,0:T(8,128)(2,1)} %constant_dynamic-update-slice_fusion.3.refs_2_), channel_id=1, source_target_pairs={{0,8},{1,9},{2,10},{3,11},{4,12},{5,13},{6,14},{7,15},{8,0},{9,1},... | collective-permute-start | bytes 2949128 | tf_op jit(solution)/shard_map/ppermute | solution.py:46
  77.8 65.3 %all-to-all-start.1 = ((s32[32,2,128]{2,1,0:T(2,128)}), s32[32,2,128]{2,1,0:T(2,128)}, u32[]{:S(2)}, u32[]{:S(2)}) async-start(s32[32,2,128]{2,1,0:T(2,128)} %broadcast_in_dim.14), calls=%async_computation.1 | async-start | bytes 65536 | tf_op jit(solution)/shard_map/all_to_all | solution.py:454
  88.3 31.5 %copy-start.22 = (bf16[2,257,1024]{2,0,1:T(2,128)(2,1)S(1)}, bf16[2,257,1024]{2,0,1:T(2,128)(2,1)}, u32[]{:S(2)}) copy-start(bf16[2,257,1024]{2,0,1:T(2,128)(2,1)} %param.14) | copy-start | bytes 3158020
  88.4 48.2 %copy-start.27 = (s32[32]{0:T(128)S(1)}, s32[32]{0:T(128)}, u32[]{:S(2)}) copy-start(s32[32]{0:T(128)} %param.25) | copy-start | bytes 388
  88.4 37.3 %copy-start.15 = (bf16[384,768]{1,0:T(8,128)(2,1)}, bf16[384,768]{1,0:T(8,128)(2,1)S(1)}, u32[]{:S(2)}) copy-start(bf16[384,768]{1,0:T(8,128)(2,1)S(1)} %collective-permute-done.31.refs_4_) | copy-start | bytes 1769476
  88.4 53.1 %collective-permute-start.17 = (bf16[384,1280]{1,0:T(8,128)(2,1)}, bf16[384,1280]{1,0:T(8,128)(2,1)}, u32[]{:S(2)}, u32[]{:S(2)}) collective-permute-start(bf16[384,1280]{1,0:T(8,128)(2,1)} %constant_dynamic-update-slice_fusion.3.refs_2_), channel_id=1, source_target_pairs={{0,16},{1,17},{2,18},{3,19},{4,20},{5,21},{6,22},{7,23},{8,24},{9,... | collective-permute-start | bytes 2949128 | tf_op jit(solution)/shard_map/ppermute | solution.py:46
  89.8 53.1 %collective-permute-start.21 = (bf16[384,1280]{1,0:T(8,128)(2,1)}, bf16[384,1280]{1,0:T(8,128)(2,1)}, u32[]{:S(2)}, u32[]{:S(2)}) collective-permute-start(bf16[384,1280]{1,0:T(8,128)(2,1)} %constant_dynamic-update-slice_fusion.3.refs_2_), channel_id=1, source_target_pairs={{0,1},{1,0},{2,3},{3,2},{4,5},{5,4},{6,7},{7,6},{8,9},{9,8},{10,11... | collective-permute-start | bytes 2949128 | tf_op jit(solution)/shard_map/ppermute | solution.py:46
  90.5 28.0 %collective-permute-start.32 = (bf16[192,768]{1,0:T(8,128)(2,1)S(1)}, bf16[192,768]{1,0:T(8,128)(2,1)}, u32[]{:S(2)}, u32[]{:S(2)}) collective-permute-start(bf16[192,768]{1,0:T(8,128)(2,1)S(1)} %slice.36), channel_id=1, source_target_pairs={{0,16},{1,17},{2,18},{3,19},{4,20},{5,21},{6,22},{7,23},{8,24},{9,... | collective-permute-start | bytes 884744 | tf_op jit(solution)/shard_map/ppermute | solution.py:46
  93.8 46.0 %copy-start.9 = (bf16[1536,256]{1,0:T(8,128)(2,1)}, bf16[1536,256]{1,0:T(8,128)(2,1)S(1)}, u32[]{:S(2)}) copy-start(bf16[1536,256]{1,0:T(8,128)(2,1)S(1)} %collective-permute-done.3.refs_3_) | copy-start | bytes 2359300
  93.8 41.5 %collective-permute-start.4 = (bf16[1536,256]{1,0:T(8,128)(2,1)}, bf16[1536,256]{1,0:T(8,128)(2,1)S(1)}, u32[]{:S(2)}, u32[]{:S(2)}) collective-permute-start(bf16[1536,256]{1,0:T(8,128)(2,1)} %constant_dynamic-update-slice_fusion.refs_2_), channel_id=1, source_target_pairs={{0,16},{1,17},{2,18},{3,19},{4,20},{5,21},{6,22},{7,23},{8,24},{9,... | collective-permute-start | bytes 2359304 | tf_op jit(solution)/shard_map/ppermute | solution.py:46
  118.5 7.2 %collective-permute-start.33 = (bf16[192,768]{1,0:T(8,128)(2,1)}, bf16[192,768]{1,0:T(8,128)(2,1)}, u32[]{:S(2)}, u32[]{:S(2)}) collective-permute-start(bf16[192,768]{1,0:T(8,128)(2,1)} %slice.37), channel_id=1, source_target_pairs={{0,8},{1,9},{2,10},{3,11},{4,12},{5,13},{6,14},{7,15},{8,0},{9,1},... | collective-permute-start | bytes 884744 | tf_op jit(solution)/shard_map/ppermute | solution.py:46
  122.0 18.1 %copy-start.1 = (bf16[384,1280]{1,0:T(8,128)(2,1)}, bf16[384,1280]{1,0:T(8,128)(2,1)S(1)}, u32[]{:S(2)}) copy-start(bf16[384,1280]{1,0:T(8,128)(2,1)S(1)} %collective-permute-done.16.refs_3_) | copy-start | bytes 2949124
  122.0 23.7 %collective-permute-start.38 = (bf16[192,768]{1,0:T(8,128)(2,1)}, bf16[192,768]{1,0:T(8,128)(2,1)}, u32[]{:S(2)}, u32[]{:S(2)}) collective-permute-start(bf16[192,768]{1,0:T(8,128)(2,1)} %collective-permute-done.32.refs_5_), channel_id=1, source_target_pairs={{0,1},{1,0},{2,3},{3,2},{4,5},{5,4},{6,7},{7,6},{8,9},{9,8},{10,11... | collective-permute-start | bytes 884744 | tf_op jit(solution)/shard_map/ppermute | solution.py:46
  125.7 14.1 %copy-start.23 = (f32[2,272]{0,1:T(8,128)S(1)}, f32[2,272]{0,1:T(8,128)}, u32[]{:S(2)}) copy-start(f32[2,272]{0,1:T(8,128)} %add_rsqrt_fusion) | copy-start | bytes 6532
  125.7 22.7 %collective-permute-start.39 = (bf16[192,768]{1,0:T(8,128)(2,1)}, bf16[192,768]{1,0:T(8,128)(2,1)}, u32[]{:S(2)}, u32[]{:S(2)}) collective-permute-start(bf16[192,768]{1,0:T(8,128)(2,1)} %collective-permute-done.33.refs_6_), channel_id=1, source_target_pairs={{0,1},{1,0},{2,3},{3,2},{4,5},{5,4},{6,7},{7,6},{8,9},{9,8},{10,11... | collective-permute-start | bytes 884744 | tf_op jit(solution)/shard_map/ppermute | solution.py:46
  135.2 14.0 %collective-permute-start.18 = (bf16[192,1280]{1,0:T(8,128)(2,1)}, bf16[192,1280]{1,0:T(8,128)(2,1)}, u32[]{:S(2)}, u32[]{:S(2)}) collective-permute-start(bf16[192,1280]{1,0:T(8,128)(2,1)} %slice.34), channel_id=1, source_target_pairs={{0,16},{1,17},{2,18},{3,19},{4,20},{5,21},{6,22},{7,23},{8,24},{9,... | collective-permute-start | bytes 1474568 | tf_op jit(solution)/shard_map/ppermute | solution.py:46
  141.5 18.2 %copy-start = (f32[1,2048,256]{2,1,0:T(8,128)S(1)}, f32[1,2048,256]{2,1,0:T(8,128)}, u32[]{:S(2)}) copy-start(f32[1,2048,256]{2,1,0:T(8,128)} %param.23) | copy-start | bytes 6291460
  141.5 11.6 %collective-permute-start.36 = (bf16[384,768]{1,0:T(8,128)(2,1)}, bf16[384,768]{1,0:T(8,128)(2,1)}, u32[]{:S(2)}, u32[]{:S(2)}) collective-permute-start(bf16[384,768]{1,0:T(8,128)(2,1)} %copy-done.13), channel_id=1, source_target_pairs={{0,1},{1,0},{2,3},{3,2},{4,5},{5,4},{6,7},{7,6},{8,9},{9,8},{10,11... | collective-permute-start | bytes 1769480 | tf_op jit(solution)/shard_map/ppermute | solution.py:46
  143.0 10.6 %collective-permute-start.37 = (bf16[384,768]{1,0:T(8,128)(2,1)}, bf16[384,768]{1,0:T(8,128)(2,1)}, u32[]{:S(2)}, u32[]{:S(2)}) collective-permute-start(bf16[384,768]{1,0:T(8,128)(2,1)} %copy-done.15), channel_id=1, source_target_pairs={{0,1},{1,0},{2,3},{3,2},{4,5},{5,4},{6,7},{7,6},{8,9},{9,8},{10,11... | collective-permute-start | bytes 1769480 | tf_op jit(solution)/shard_map/ppermute | solution.py:46
  145.7 12.7 %collective-permute-start.19 = (bf16[192,1280]{1,0:T(8,128)(2,1)}, bf16[192,1280]{1,0:T(8,128)(2,1)}, u32[]{:S(2)}, u32[]{:S(2)}) collective-permute-start(bf16[192,1280]{1,0:T(8,128)(2,1)} %slice.35), channel_id=1, source_target_pairs={{0,8},{1,9},{2,10},{3,11},{4,12},{5,13},{6,14},{7,15},{8,0},{9,1},... | collective-permute-start | bytes 1474568 | tf_op jit(solution)/shard_map/ppermute | solution.py:46
  148.5 32.7 %collective-permute-start.22 = (bf16[384,1280]{1,0:T(8,128)(2,1)}, bf16[384,1280]{1,0:T(8,128)(2,1)}, u32[]{:S(2)}, u32[]{:S(2)}) collective-permute-start(bf16[384,1280]{1,0:T(8,128)(2,1)} %copy-done.1), channel_id=1, source_target_pairs={{0,1},{1,0},{2,3},{3,2},{4,5},{5,4},{6,7},{7,6},{8,9},{9,8},{10,11... | collective-permute-start | bytes 2949128 | tf_op jit(solution)/shard_map/ppermute | solution.py:46
  149.3 17.8 %collective-permute-start.24 = (bf16[192,1280]{1,0:T(8,128)(2,1)}, bf16[192,1280]{1,0:T(8,128)(2,1)}, u32[]{:S(2)}, u32[]{:S(2)}) collective-permute-start(bf16[192,1280]{1,0:T(8,128)(2,1)} %collective-permute-done.18.refs_5_), channel_id=1, source_target_pairs={{0,1},{1,0},{2,3},{3,2},{4,5},{5,4},{6,7},{7,6},{8,9},{9,8},{10,11... | collective-permute-start | bytes 1474568 | tf_op jit(solution)/shard_map/ppermute | solution.py:46
  151.0 16.4 %copy-start.24 = (f32[1024]{0:T(1024)S(1)}, f32[1024]{0:T(1024)}, u32[]{:S(2)}) copy-start(f32[1024]{0:T(1024)} %param.15) | copy-start | bytes 12292
  153.1 66.2 %collective-permute-start.20 = (bf16[128,4096]{1,0:T(8,128)(2,1)}, bf16[128,4096]{1,0:T(8,128)(2,1)}, u32[]{:S(2)}, u32[]{:S(2)}) collective-permute-start(bf16[128,4096]{1,0:T(8,128)(2,1)} %refs_1_.6), channel_id=1, source_target_pairs={{0,1},{1,0},{2,3},{3,2},{4,5},{5,4},{6,7},{7,6},{8,9},{9,8},{10,11... | collective-permute-start | bytes 3145736 | tf_op jit(solution)/shard_map/ppermute | solution.py:46
  153.6 41.4 %collective-permute-start.23 = (bf16[384,1280]{1,0:T(8,128)(2,1)}, bf16[384,1280]{1,0:T(8,128)(2,1)}, u32[]{:S(2)}, u32[]{:S(2)}) collective-permute-start(bf16[384,1280]{1,0:T(8,128)(2,1)} %collective-permute-done.17.refs_4_), channel_id=1, source_target_pairs={{0,1},{1,0},{2,3},{3,2},{4,5},{5,4},{6,7},{7,6},{8,9},{9,8},{10,11... | collective-permute-start | bytes 2949128 | tf_op jit(solution)/shard_map/ppermute | solution.py:46
  158.4 21.3 %collective-permute-start.25 = (bf16[192,1280]{1,0:T(8,128)(2,1)}, bf16[192,1280]{1,0:T(8,128)(2,1)}, u32[]{:S(2)}, u32[]{:S(2)}) collective-permute-start(bf16[192,1280]{1,0:T(8,128)(2,1)} %collective-permute-done.19.refs_6_), channel_id=1, source_target_pairs={{0,1},{1,0},{2,3},{3,2},{4,5},{5,4},{6,7},{7,6},{8,9},{9,8},{10,11... | collective-permute-start | bytes 1474568 | tf_op jit(solution)/shard_map/ppermute | solution.py:46
  162.7 11.6 %all-to-all-start.2 = ((f32[32,2,256]{2,1,0:T(2,128)}), f32[32,2,256]{2,1,0:T(2,128)S(1)}, u32[]{:S(2)}, u32[]{:S(2)}) async-start(f32[32,2,256]{2,1,0:T(2,128)} %copy.42), calls=%async_computation.2 | async-start | bytes 131072 | tf_op jit(solution)/shard_map/all_to_all | solution.py:489
  167.1 52.4 %collective-permute-start.8 = (bf16[1536,256]{1,0:T(8,128)(2,1)}, bf16[1536,256]{1,0:T(8,128)(2,1)}, u32[]{:S(2)}, u32[]{:S(2)}) collective-permute-start(bf16[1536,256]{1,0:T(8,128)(2,1)} %constant_dynamic-update-slice_fusion.refs_2_), channel_id=1, source_target_pairs={{0,1},{1,0},{2,3},{3,2},{4,5},{5,4},{6,7},{7,6},{8,9},{9,8},{10,11... | collective-permute-start | bytes 2359304 | tf_op jit(solution)/shard_map/ppermute | solution.py:46
  175.0 75.0 %all-to-all-start.3 = ((f32[32,2,256]{2,1,0:T(2,128)}), f32[32,2,256]{2,1,0:T(2,128)S(1)}, u32[]{:S(2)}, u32[]{:S(2)}) async-start(f32[32,2,256]{2,1,0:T(2,128)} %broadcast_in_dim.16), calls=%async_computation.3 | async-start | bytes 131072 | tf_op jit(solution)/shard_map/all_to_all | solution.py:454
  177.5 17.4 %copy-start.18 = (bf16[512,1024]{1,0:T(8,128)(2,1)S(1)}, bf16[512,1024]{1,0:T(8,128)(2,1)}, u32[]{:S(2)}) copy-start(bf16[512,1024]{1,0:T(8,128)(2,1)} %refs_1_.7) | copy-start | bytes 3145732
  179.7 40.2 %collective-permute-start.5 = (bf16[768,256]{1,0:T(8,128)(2,1)S(1)}, bf16[768,256]{1,0:T(8,128)(2,1)S(1)}, u32[]{:S(2)}, u32[]{:S(2)}) collective-permute-start(bf16[768,256]{1,0:T(8,128)(2,1)S(1)} %slice.32), channel_id=1, source_target_pairs={{0,16},{1,17},{2,18},{3,19},{4,20},{5,21},{6,22},{7,23},{8,24},{9,... | collective-permute-start | bytes 1179656 | tf_op jit(solution)/shard_map/ppermute | solution.py:46
  181.2 38.8 %collective-permute-start.6 = (bf16[768,256]{1,0:T(8,128)(2,1)S(1)}, bf16[768,256]{1,0:T(8,128)(2,1)S(1)}, u32[]{:S(2)}, u32[]{:S(2)}) collective-permute-start(bf16[768,256]{1,0:T(8,128)(2,1)S(1)} %slice.33), channel_id=1, source_target_pairs={{0,8},{1,9},{2,10},{3,11},{4,12},{5,13},{6,14},{7,15},{8,0},{9,1},... | collective-permute-start | bytes 1179656 | tf_op jit(solution)/shard_map/ppermute | solution.py:46
  195.0 35.8 %collective-permute-start.7 = (bf16[512,1024]{1,0:T(8,128)(2,1)S(1)}, bf16[512,1024]{1,0:T(8,128)(2,1)S(1)}, u32[]{:S(2)}, u32[]{:S(2)}) collective-permute-start(bf16[512,1024]{1,0:T(8,128)(2,1)S(1)} %copy-done.18), channel_id=1, source_target_pairs={{0,1},{1,0},{2,3},{3,2},{4,5},{5,4},{6,7},{7,6},{8,9},{9,8},{10,11... | collective-permute-start | bytes 3145736 | tf_op jit(solution)/shard_map/ppermute | solution.py:46
  195.9 15.0 %copy-start.2 = (bf16[384,1280]{1,0:T(8,128)(2,1)S(1)}, bf16[384,1280]{1,0:T(8,128)(2,1)}, u32[]{:S(2)}) copy-start(bf16[384,1280]{1,0:T(8,128)(2,1)} %copy-done.1) | copy-start | bytes 2949124
  195.9 15.0 %copy-start.8 = (bf16[128,1024]{1,0:T(8,128)(2,1)S(1)}, bf16[128,1024]{1,0:T(8,128)(2,1)}, u32[]{:S(2)}) copy-start(bf16[128,1024]{1,0:T(8,128)(2,1)} %copy-done.7) | copy-start | bytes 786436
  195.9 15.0 %copy-start.20 = (f32[1024]{0:T(1024)S(1)}, f32[1024]{0:T(1024)}, u32[]{:S(2)}) copy-start(f32[1024]{0:T(1024)} %param.18) | copy-start | bytes 12292
  211.0 9.5 %copy-start.17 = (bf16[128,4096]{1,0:T(8,128)(2,1)S(1)}, bf16[128,4096]{1,0:T(8,128)(2,1)}, u32[]{:S(2)}) copy-start(bf16[128,4096]{1,0:T(8,128)(2,1)} %refs_1_.6) | copy-start | bytes 3145732
  219.3 11.4 %collective-permute-start.10 = (bf16[1536,256]{1,0:T(8,128)(2,1)S(1)}, bf16[1536,256]{1,0:T(8,128)(2,1)S(1)}, u32[]{:S(2)}, u32[]{:S(2)}) collective-permute-start(bf16[1536,256]{1,0:T(8,128)(2,1)S(1)} %copy-done.12), channel_id=1, source_target_pairs={{0,1},{1,0},{2,3},{3,2},{4,5},{5,4},{6,7},{7,6},{8,9},{9,8},{10,11... | collective-permute-start | bytes 2359304 | tf_op jit(solution)/shard_map/ppermute | solution.py:46
  219.5 11.3 %collective-permute-start.9 = (bf16[1536,256]{1,0:T(8,128)(2,1)S(1)}, bf16[1536,256]{1,0:T(8,128)(2,1)S(1)}, u32[]{:S(2)}, u32[]{:S(2)}) collective-permute-start(bf16[1536,256]{1,0:T(8,128)(2,1)S(1)} %copy-done.10), channel_id=1, source_target_pairs={{0,1},{1,0},{2,3},{3,2},{4,5},{5,4},{6,7},{7,6},{8,9},{9,8},{10,11... | collective-permute-start | bytes 2359304 | tf_op jit(solution)/shard_map/ppermute | solution.py:46
  219.9 10.8 %collective-permute-start.11 = (bf16[768,256]{1,0:T(8,128)(2,1)S(1)}, bf16[768,256]{1,0:T(8,128)(2,1)S(1)}, u32[]{:S(2)}, u32[]{:S(2)}) collective-permute-start(bf16[768,256]{1,0:T(8,128)(2,1)S(1)} %collective-permute-done.5.refs_5_), channel_id=1, source_target_pairs={{0,1},{1,0},{2,3},{3,2},{4,5},{5,4},{6,7},{7,6},{8,9},{9,8},{10,11... | collective-permute-start | bytes 1179656 | tf_op jit(solution)/shard_map/ppermute | solution.py:46
  220.0 10.7 %collective-permute-start.12 = (bf16[768,256]{1,0:T(8,128)(2,1)S(1)}, bf16[768,256]{1,0:T(8,128)(2,1)S(1)}, u32[]{:S(2)}, u32[]{:S(2)}) collective-permute-start(bf16[768,256]{1,0:T(8,128)(2,1)S(1)} %collective-permute-done.6.refs_6_), channel_id=1, source_target_pairs={{0,1},{1,0},{2,3},{3,2},{4,5},{5,4},{6,7},{7,6},{8,9},{9,8},{10,11... | collective-permute-start | bytes 1179656 | tf_op jit(solution)/shard_map/ppermute | solution.py:46
  220.4 10.3 %copy-start.21 = (f32[1024]{0:T(1024)S(1)}, f32[1024]{0:T(1024)}, u32[]{:S(2)}) copy-start(f32[1024]{0:T(1024)} %param.21) | copy-start | bytes 12292
  230.8 31.2 %copy-start.5 = (bf16[1024,256]{1,0:T(8,128)(2,1)S(1)}, bf16[1024,256]{1,0:T(8,128)(2,1)}, u32[]{:S(2)}) copy-start(bf16[1024,256]{1,0:T(8,128)(2,1)} %proj_ref.1) | copy-start | bytes 1572868
  250.0 11.9 %all-to-all-start = ((bf16[32,2,1024]{2,1,0:T(2,128)(2,1)}), bf16[32,2,1024]{2,1,0:T(2,128)(2,1)S(1)}, u32[]{:S(2)}, u32[]{:S(2)}) async-start(bf16[32,2,1024]{2,1,0:T(2,128)(2,1)} %project_down.1), calls=%async_computation | async-start | bytes 262144 | tf_op jit(solution)/shard_map/all_to_all | solution.py:503
  (8 other events, 27.8 us)
where the time goes:
time: 270 us; the launch traced here: 268 us
  starting transfers between devices  81.6 us (30%)
  waiting for transfers between devices  74.7 us (28%)
  Pallas kernels  65.7 us (24%)
  local copies, waits for them, and re-layouts  32.4 us (12%)
  other arithmetic  8.94 us (3%)
  matrix products  4.04 us (1%)
    ppermute x40, waiting for transfers between devices, moved(): return lax.ppermute(value, both, pairs)  62.3 us
    ppermute x40, starting transfers between devices, moved(): return lax.ppermute(value, both, pairs)  60.5 us
    pallas_call x4, Pallas kernels, call_with_weight(): pl.pallas_call(kernel, out_shape=out_shapes, in_specs=[SMEM] + [ANY] * we...  45.8 us
    pallas_call x1, Pallas kernels, attend(): pl.pallas_call(kernel, grid=(images, blocks), out_shape=jax.ShapeDtypeStr...  15 us
    unnamed x65, local copies, waits for them, and re-layouts  13.2 us
    all_to_all x2, starting transfers between devices, broadcast_all(): lax.all_to_all(jnp.broadcast_to(value[None], (devices,) + value.shape), B...  13.1 us
    all_to_all x1, waiting for transfers between devices, on_device(): lax.all_to_all(pooled, BOTH, 0, 0, tiled=True).reshape(every_image, width)  6.97 us
    slice x6, local copies, waits for them, and re-layouts, spread_shards(): low, high = (swap(one[:half], 2), swap(two[half:], 1))  5.55 us
  transfers between devices with their start and end apart: 44, of which 9 were waited for; matrix products, arithmetic and copies ran while one was open for 14% of the time, Pallas kernels for 23%

commit v1 on v0

v1 whole, which is shorter than its diff:
```python
import functools
import math

import jax
import jax.numpy as jnp
from jax import lax
from jax.experimental import pallas as pl
from jax.experimental.pallas import tpu as pltpu
from jax.sharding import PartitionSpec as P

HEADS = 16
LOOK_IMG = 64
CORES = 2
LANES = 128
MIB = 1 << 20
ROOM = 58

epsilon = 1e-06
learn_rate = 0.5
bf16 = jnp.bfloat16
f32 = jnp.float32
BOTH = ("grp", "fsdp")

VMEM = pl.BlockSpec(memory_space=pltpu.VMEM)
SMEM = pl.BlockSpec(memory_space=pltpu.SMEM)
ANY = pl.BlockSpec(memory_space=pl.ANY)
SHORT = pl.CostEstimate(flops=1, bytes_accessed=1, transcendentals=0)


def norm_rows(values, gain):
    center = jnp.mean(values, axis=-1, keepdims=True)
    shifted = values - center
    spread = jnp.mean(shifted * shifted, axis=-1, keepdims=True)
    return shifted * lax.rsqrt(spread + epsilon) * gain


def after(values, *others):
    return lax.optimization_barrier((tuple(values), tuple(others)))[0]


class Routes:
    def __init__(self, grp, fsdp):
        self.grp, self.fsdp, self.chips = grp, fsdp, fsdp // CORES

    def moved(self, value, target):
        pairs = []
        for index in range(self.grp * self.fsdp):
            plane, rest = divmod(index, self.fsdp)
            chip, core = divmod(rest, CORES)
            there = target(plane, chip, core)
            pairs.append((index, (there[0] * self.chips + there[1]) * CORES + there[2]))
        return lax.ppermute(value, BOTH, pairs)

    def along(self, value, *steps):
        return [
            self.moved(value, lambda g, c, k, step=step: (g, (c - step) % self.chips, k))
            for step in steps
        ]

    def swap(self, value, bit):
        return self.moved(value, lambda g, c, k: (g ^ bit, c, k))

    def sibling(self, value):
        return self.moved(value, lambda g, c, k: (g, c, k ^ 1))


def quarter_of(shards, plane):
    return jnp.concatenate(
        [
            lax.dynamic_slice_in_dim(s, plane * (s.shape[1] // 4), s.shape[1] // 4, axis=1)
            for s in shards
        ],
        axis=1,
    )


def piece_plan(chips, rows, wide, offset, halved):
    plan = []
    half = (chips - 1) * rows // 2
    for turn in range(3):
        for step in range(1, chips):
            for side in range(2):
                plan.append((1 + turn, (step - 1) * rows, rows, offset, side, step, 0, turn))
    for step in range(1, chips):
        for side in range(2):
            if not halved:
                plan.append((3 + step, 0, rows, offset, side, step, 0, 3))
                continue
            first, last = (step - 1) * rows, step * rows
            for buffer, low, high, base in ((4, 0, half, 0), (5, half, 2 * half, half)):
                start, stop = max(first, low), min(last, high)
                if start < stop:
                    plan.append(
                        (buffer, start - base, stop - start, offset, side, step, start - first, 3)
                    )
    return plan


class Weight:
    def __init__(self, shape, wide, pieces, plan, chips, rows):
        self.shape, self.wide, self.pieces = shape, wide, pieces
        self.plan, self.chips, self.rows = plan, chips, rows

    @property
    def count(self):
        return len(self.pieces)

    @property
    def copies(self):
        return 1 if self.plan is None else 2 + len(self.plan)

    def start(self, refs, whole, sems, pos):
        if self.plan is None:
            copy = pltpu.make_async_copy(refs[0], whole, sems.at[0])
            copy.start()
            return [[copy], [], [], []]
        plane, chip, core = pos[0], pos[1], pos[2]
        groups = [[], [], [], []]
        number, half = 0, self.count // 2

        def go(source, target, turn):
            nonlocal number
            copy = pltpu.make_async_copy(source, target, sems.at[number])
            copy.start()
            groups[turn].append(copy)
            number += 1

        for side in range(2):
            row = pl.multiple_of((chip * CORES + (core ^ side)) * self.rows, self.rows)
            go(refs[side * half], whole.at[pl.ds(row, self.rows), :], 0)
        for buffer, low, count, column, side, step, inner, turn in self.plan:
            there = lax.rem(chip + step, self.chips)
            row = (there * CORES + (core ^ side)) * self.rows + inner
            row = pl.multiple_of(row, math.gcd(self.rows, inner) if inner else self.rows)
            left = pl.multiple_of((plane ^ turn) * self.wide, LANES)
            go(
                refs[side * half + buffer].at[pl.ds(low, count), pl.ds(column, self.wide)],
                whole.at[pl.ds(row, count), pl.ds(left, self.wide)],
                turn,
            )
        return groups

    def each_turn(self, refs, whole, sems, pos, body):
        groups = self.start(refs, whole, sems, pos)
        for turn in range(4):
            for copy in groups[turn]:
                copy.wait()
            left = (pos[0] ^ turn) * self.wide if self.plan is not None else turn * self.wide
            body(left)


def weights_of(shards, pieces, chips, rows, halved):
    found, offset = [], 0
    sent, other, other_own = pieces
    for number, shard in enumerate(shards):
        wide = shard.shape[1] // 4
        found.append(
            Weight(
                (rows * chips * CORES, shard.shape[1]), wide,
                [shard] + sent + [other_own[number]] + other,
                piece_plan(chips, rows, wide, offset, halved), chips, rows,
            )
        )
        offset += wide
    return found


def whole_weight(shard, fsdp):
    full = lax.all_gather(shard, "fsdp", axis=0, tiled=True)
    return Weight(full.shape, shard.shape[1] // 4, [full], None, fsdp // CORES, shard.shape[0])


def block_of(wide):
    return next(size for size in (1024, 768, 512, 256, LANES) if wide % size == 0)


def call_with_weight(weight, body, pos, inputs, out_shapes, scratch, room, name):
    n_in, n_out = len(inputs), len(out_shapes)

    def kernel(*refs):
        pos_ref = refs[0]
        pieces = refs[1 : 1 + weight.count]
        refs = refs[1 + weight.count :]
        ins, outs, rest = refs[:n_in], refs[n_in : n_in + n_out], refs[n_in + n_out :]
        whole, sems = rest[0], rest[1]

        def each_turn(work):
            weight.each_turn(pieces, whole, sems, pos_ref, work)

        body(ins, outs, rest[2:], whole, each_turn)

    return pl.pallas_call(
        kernel,
        out_shape=out_shapes,
        in_specs=[SMEM] + [ANY] * weight.count + [VMEM] * n_in,
        out_specs=[VMEM] * n_out,
        scratch_shapes=[
            pltpu.VMEM(weight.shape, bf16),
            pltpu.SemaphoreType.DMA((weight.copies,)),
        ]
        + list(scratch),
        compiler_params=pltpu.CompilerParams(vmem_limit_bytes=room * MIB),
        cost_estimate=SHORT,
        name=name,
    )(pos, *weight.pieces, *inputs)


def dot32(left, right):
    return jnp.dot(left, right, preferred_element_type=f32)


def column_loop(wide, left, work):
    size = block_of(wide)

    @pl.loop(0, wide // size)
    def _(number):
        work(pl.ds(pl.multiple_of(left + number * size, LANES), size))


def prepare(hidden, gain, padded):
    images, seq, width = hidden.shape
    full = seq // 16

    def kernel(hidden_ref, gain_ref, tokens, normed):
        for image in range(images):
            for number in range(padded // 16):
                at = slice(image * padded + number * 16, image * padded + (number + 1) * 16)
                if number < full:
                    part = hidden_ref[image, number * 16 : (number + 1) * 16, :]
                    tokens[at, :] = part
                    rows = part.astype(f32)
                else:
                    index = lax.broadcasted_iota(jnp.int32, (16, 1), 0)
                    rows = jnp.zeros((16, width), f32)
                    for extra in range(seq - number * 16):
                        row = hidden_ref[image, pl.ds(number * 16 + extra, 1), :].astype(f32)
                        rows = jnp.where(index == extra, row, rows)
                    tokens[at, :] = rows.astype(bf16)
                normed[at, :] = norm_rows(rows, gain_ref[...]).astype(bf16)

    shape = jax.ShapeDtypeStruct((images * padded, width), bf16)
    return pl.pallas_call(
        kernel, out_shape=[shape, shape], in_specs=[VMEM, VMEM], out_specs=[VMEM, VMEM],
        compiler_params=pltpu.CompilerParams(vmem_limit_bytes=16 * MIB),
        cost_estimate=SHORT, name="prepare",
    )(hidden, gain.reshape(1, -1))


def project_qkv(weight, pos, normed):
    def body(ins, outs, scratch, whole, each_turn):
        def quarter(left):
            def work(columns):
                outs[0][:, columns] = dot32(ins[0][...], whole[:, columns]).astype(bf16)

            column_loop(weight.wide, left, work)

        each_turn(quarter)

    rows = normed.shape[0]
    return call_with_weight(
        weight, body, pos, [normed],
        [jax.ShapeDtypeStruct((rows, weight.shape[1]), bf16)], [], ROOM, "project_qkv",
    )[0]


def attend(qkv, seq, width):
    images, padded = qkv.shape[:2]
    head_dim = width // HEADS
    per = LANES // head_dim
    wide = math.gcd(width, 4 * LANES)
    blocks = width // wide
    factor = 1.0 / (math.sqrt(head_dim) * math.log(2.0))

    def kernel(query, keys, values, out):
        lane = lax.broadcasted_iota(jnp.int32, (1, LANES), 1)
        column = lax.broadcasted_iota(jnp.int32, (1, padded), 1)
        for pair in range(wide // LANES):
            at = slice(pair * LANES, (pair + 1) * LANES)
            q, k, v = query[0, :, at], keys[0, :, at], values[0, :, at]
            beside = jnp.concatenate([v, jnp.ones_like(v)], axis=1)
            total = None
            for head in range(per):
                own = (lane // head_dim) == head
                scores = lax.dot_general(
                    jnp.where(own, q, jnp.zeros_like(q)), k,
                    (((1,), (1,)), ((), ())), preferred_element_type=f32,
                )
                scores = jnp.where(column < seq, scores, -1e30)
                top = jnp.max(scores, axis=-1, keepdims=True)
                probs = jnp.exp2((scores - top) * factor).astype(bf16)
                both = dot32(probs, beside)
                mixed = both[:, :LANES] / both[:, LANES:]
                total = mixed if total is None else jnp.where(own, mixed, total)
            out[0, :, at] = total.astype(bf16)

    spec = lambda shift: pl.BlockSpec((1, padded, wide), lambda i, h: (i, 0, h + shift * blocks))
    return pl.pallas_call(
        kernel,
        grid=(images, blocks),
        out_shape=jax.ShapeDtypeStruct((images, padded, width), bf16),
        in_specs=[spec(0), spec(1), spec(2)],
        out_specs=spec(0),
        compiler_params=pltpu.CompilerParams(vmem_limit_bytes=ROOM * MIB),
        cost_estimate=SHORT,
        name="attend",
    )(qkv, qkv, qkv)


def project_out(weight, pos, mixed, tokens, gain):
    rows, width = mixed.shape

    def body(ins, outs, scratch, whole, each_turn):
        mixed_ref, tokens_ref, gain_ref = ins
        resid, normed = outs

        def quarter(left):
            def work(columns):
                product = dot32(mixed_ref[...], whole[:, columns])
                resid[:, columns] = (tokens_ref[:, columns].astype(f32) + product).astype(bf16)

            column_loop(weight.wide, left, work)

        each_turn(quarter)
        for number in range(rows // 16):
            at = slice(number * 16, (number + 1) * 16)
            normed[at, :] = norm_rows(resid[at, :].astype(f32), gain_ref[...]).astype(bf16)

    shape = jax.ShapeDtypeStruct((rows, width), bf16)
    return call_with_weight(
        weight, body, pos, [mixed, tokens, gain.reshape(1, -1)], [shape, shape], [], ROOM, "project_out",
    )


def gelu(values):
    return 0.5 * values * (1.0 + lax.erf(values * math.sqrt(0.5)))


def project_up(weight, pos, normed):
    rows = normed.shape[0]

    def body(ins, outs, scratch, whole, each_turn):
        def quarter(left):
            def work(columns):
                outs[0][:, columns] = gelu(dot32(ins[0][...], whole[:, columns])).astype(bf16)

            column_loop(weight.wide, left, work)

        each_turn(quarter)

    return call_with_weight(
        weight, body, pos, [normed],
        [jax.ShapeDtypeStruct((rows, weight.shape[1]), bf16)], [], ROOM, "project_up",
    )[0]


def thirds(values):
    first = values.astype(bf16)
    left = values - first.astype(f32)
    second = left.astype(bf16)
    return first, second, (left - second.astype(f32)).astype(bf16)


def project_down(weight, pos, active, resid, gain, sums, images, seq, devices):
    rows, width = resid.shape
    padded = rows // images

    def body(ins, outs, scratch, whole, each_turn):
        active_ref, resid_ref, gain_ref, sums_ref = ins
        (final,) = scratch
        (pooled,) = outs
        split = [part.astype(f32) for part in thirds(sums_ref[...])]

        def quarter(left):
            def work(columns):
                product = dot32(active_ref[...], whole[:, columns])
                final[:, columns] = resid_ref[:, columns].astype(f32) + product

            column_loop(weight.wide, left, work)

        each_turn(quarter)
        step = 16
        for image in range(images):
            total = jnp.zeros((step, width), f32)
            for number in range(padded // step):
                at = slice(image * padded + number * step, image * padded + (number + 1) * step)
                posted = norm_rows(final[at, :], gain_ref[...])
                if (number + 1) * step > seq:
                    row = lax.broadcasted_iota(jnp.int32, (step, 1), 0) + number * step
                    posted = jnp.where(row < seq, posted, 0.0)
                total = total + posted
            mean = jnp.sum(total, axis=0, keepdims=True) / seq
            at = slice(image, image + 1)
            row = jnp.concatenate([mean] + [part[at, :] for part in split], axis=1).astype(bf16)
            for device in range(devices):
                pooled[device, at, :] = row

    return call_with_weight(
        weight, body, pos, [active, resid, gain.reshape(1, -1), sums],
        [jax.ShapeDtypeStruct((devices, images, width + 3 * sums.shape[1]), bf16)],
        [pltpu.VMEM((rows, width), f32)], ROOM, "project_down",
    )[0]


def update(pos, every, proj, named, table, accum, images, share):
    rows, width = table.shape
    every_image, depth = every.shape[0], proj.shape[0]
    blocks = rows // LANES
    per = 4 if blocks % 4 == 0 else 1
    side = max(share, LANES)
    over = (((0,), (0,)), ((), ()))

    def kernel(pos_ref, every_ref, proj_ref, named_ref, table_ref, accum_ref,
               table_out, accum_out, content_out, proj_out, units, grads, square):
        @pl.when(pl.program_id(0) == 0)
        def _():
            content = dot32(every_ref[:, :depth], proj_ref[...])
            scale = lax.rsqrt(jnp.mean(content * content, axis=-1, keepdims=True) + epsilon)
            unit = content * scale
            for number, part in enumerate(thirds(unit)):
                units[:, number * width : (number + 1) * width] = part
            units[:, 3 * width :] = jnp.ones((every_image, width), bf16)
            sums = sum(
                every_ref[:, depth + part * width : depth + (part + 1) * width].astype(f32)
                for part in range(3)
            )
            grad_unit = LOOK_IMG * unit - sums
            inner = jnp.mean(grad_unit * unit, axis=-1, keepdims=True)
            grad = scale * (grad_unit - unit * inner)
            grads[...] = grad
            me = pos_ref[3]
            for image in range(images):
                content_out[image : image + 1, :] = grads[pl.ds(me * images + image, 1), :]
            column = me * share
            block = pl.multiple_of((column // side) * side, side)
            mine = every_ref[:, pl.ds(block, side)]
            total = None
            for part in thirds(grad):
                product = lax.dot_general(mine, part, over, preferred_element_type=f32)
                total = product if total is None else total + product
            square[...] = total
            unit_rows = math.gcd(share, side)
            proj_out[...] = square[pl.ds(pl.multiple_of(column - block, unit_rows), share), :]

        for number in range(per):
            at = slice(number * LANES, (number + 1) * LANES)
            found = dot32(named_ref[at, :], units[...])
            taken = found[:, :width] + found[:, width : 2 * width] + found[:, 2 * width : 3 * width]
            old = table_ref[at, :]
            grad_rows = found[:, 3 * width :] * old - taken
            grown = accum_ref[at, :] + grad_rows * grad_rows
            accum_out[at, :] = grown
            table_out[at, :] = old - learn_rate * grad_rows / jnp.sqrt(grown)

    whole = lambda shape: pl.BlockSpec(shape, lambda i: (0,) * len(shape))
    strip = pl.BlockSpec((per * LANES, width), lambda i: (i, 0))
    return pl.pallas_call(
        kernel,
        grid=(blocks // per,),
        out_shape=[
            jax.ShapeDtypeStruct(table.shape, f32),
            jax.ShapeDtypeStruct(table.shape, f32),
            jax.ShapeDtypeStruct((images, width), f32),
            jax.ShapeDtypeStruct((share, width), f32),
        ],
        in_specs=[
            SMEM, whole(every.shape), whole(proj.shape),
            pl.BlockSpec((per * LANES, every_image), lambda i: (i, 0)), strip, strip,
        ],
        out_specs=[strip, strip, whole((images, width)), whole((share, width))],
        scratch_shapes=[
            pltpu.VMEM((every_image, 4 * width), bf16),
            pltpu.VMEM((every_image, width), f32),
            pltpu.VMEM((side, width), f32),
        ],
        compiler_params=pltpu.CompilerParams(vmem_limit_bytes=ROOM * MIB),
        name="update",
    )(pos, every, proj, named, table, accum)


def broadcast_all(value, devices):
    return lax.all_to_all(
        jnp.broadcast_to(value[None], (devices,) + value.shape), BOTH, 0, 0, tiled=True
    )


def count_rows(named, table, mine, images):
    rows_dev = table.shape[0]
    tables = named[:, 0].reshape(images, LOOK_IMG)
    spots = named[:, 1].reshape(images, LOOK_IMG)
    high = jnp.where(tables == mine, spots // LANES, -1)
    left = (high[:, :, None] == jnp.arange(rows_dev // LANES)[None, None, :]).astype(bf16)
    right = ((spots % LANES)[:, :, None] == jnp.arange(LANES)[None, None, :]).astype(bf16)
    counts = jnp.einsum("ilh,ilr->ihr", left, right, preferred_element_type=f32)
    partial = jnp.dot(
        counts.reshape(images, rows_dev), table,
        precision=lax.Precision.HIGHEST, preferred_element_type=f32,
    )
    return jnp.transpose(counts, (1, 2, 0)).reshape(rows_dev, images).astype(bf16), partial


def on_device(
    hidden, ln1_gain, w_qkv, w_out, ln2_gain, w_up, w_down, post_gain, w_proj,
    table, accum, place, lookup_table, lookup_row,
):
    images, seq, width = hidden.shape
    grp, fsdp = lax.axis_size("grp"), lax.axis_size("fsdp")
    devices = grp * fsdp
    plane, spot = lax.axis_index("grp"), lax.axis_index("fsdp")
    me = plane * fsdp + spot
    pos = jnp.stack([plane, spot // CORES, spot % CORES, me]).astype(jnp.int32)

    rows = w_qkv.shape[0]
    routes = Routes(grp, fsdp)
    chips = routes.chips
    simple = grp == 4 and fsdp % CORES == 0 and chips % 2 == 0 and rows % LANES == 0
    joined = lambda parts: jnp.concatenate(parts, axis=0)
    half = (chips - 1) * rows // 2
    middle = chips // 2
    near = [step for step in range(1, chips) if step != middle]
    padded = -(-seq // 16) * 16
    tokens, normed = prepare(hidden, ln1_gain, padded)
    if simple:
        first = quarter_of([w_qkv, w_out], plane)
        a_one = joined(routes.along(first, *range(1, chips)))
        own = [routes.sibling(w) for w in after([w_qkv, w_out], first)]
        own += [routes.sibling(w) for w in after([w_up, w_down], own, normed)]
        second, third, fourth = (
            quarter_of([w_up], plane), quarter_of([w_down], plane), quarter_of([w_down], plane ^ 3),
        )

    rows_dev, proj_width = table.shape[1:]
    every_image = images * devices
    my_table = jnp.sum(jnp.where(place == me, jnp.arange(place.shape[0], dtype=jnp.int32), 0))
    named = broadcast_all(jnp.stack([lookup_table[:, 0], lookup_row]), devices)
    per_device = lambda v: v.reshape(devices, images, proj_width)
    counting = functools.partial(count_rows, table=table[0], mine=my_table, images=every_image)

    if simple:
        a_one, second, third, fourth, named = after([a_one, second, third, fourth, named], own, normed)
        x_one, y_one = routes.swap(a_one, 1), routes.swap(a_one, 2)
        ends = routes.along(second, *near)
        a_one_other = routes.sibling(a_one)
        counts, partial = counting(named)
        x_one, y_one, second, counts, partial = after(
            [x_one, y_one, second, counts, partial], ends, a_one_other
        )
        low_one, high_one = routes.swap(x_one[:half], 2), routes.swap(y_one[half:], 1)
        mid = routes.along(second, middle)
        a_two = joined(ends[: middle - 1] + mid + ends[middle - 1 :])
        other = [a_one_other] + [routes.sibling(v) for v in (x_one, y_one)]
        low_one, high_one, a_two, third = after(
            [low_one, high_one, a_two, third], other
        )
        other = other + [routes.sibling(v) for v in (low_one, high_one)]
        pieces = [a_one, x_one, y_one, low_one, high_one], other, own[:2]
        qkv_w, out_w = weights_of([w_qkv, w_out], pieces, chips, rows, True)
        x_two, y_two = routes.swap(a_two, 1), routes.swap(a_two, 2)
        ends = routes.along(third, *near)
        (a_two_sent,) = after([a_two], other)
        a_two_other = routes.sibling(a_two_sent)
        qkv = project_qkv(qkv_w, pos, normed)
        mixed = attend(qkv.reshape(images, padded, 3 * width), seq, width)
        x_two, y_two, ends, mixed, third, a_two_other = after(
            [x_two, y_two, ends, mixed, third, a_two_other]
        )
        mixed = mixed.reshape(images * padded, width)
        low_two, high_two = routes.swap(x_two[:half], 2), routes.swap(y_two[half:], 1)
        mid = routes.along(third, middle)
        other = [a_two_other] + [routes.sibling(v) for v in (x_two, y_two)]
        resid, normed_two = project_out(out_w, pos, mixed, tokens, ln2_gain)
        low_two, high_two, mid, other, normed_two = after([low_two, high_two, mid, other, normed_two])
        other = other + [routes.sibling(v) for v in (low_two, high_two)]
        pieces = [a_two, x_two, y_two, low_two, high_two], other, own[2:3]
        (up_w,) = weights_of([w_up], pieces, chips, rows, True)
        a_three = joined(ends[: middle - 1] + mid + ends[middle - 1 :])
        x_three, y_three = routes.swap(a_three, 1), routes.swap(a_three, 2)
        ends = routes.along(fourth, *near)
        (normed_two,) = after([normed_two], other)
        active = project_up(up_w, pos, normed_two)
        active, partial, a_three_sent, x_three, y_three, ends, fourth = after(
            [active, partial, a_three, x_three, y_three, ends, fourth]
        )
        mid = routes.along(fourth, middle)
        other = [routes.sibling(v) for v in (a_three_sent, x_three, y_three)]
        sums = jnp.sum(lax.all_to_all(per_device(partial), BOTH, 0, 0, tiled=True), axis=0)
        ends, mid, other = after([ends, mid, other], sums)
        diagonal = ends[: middle - 1] + mid + ends[middle - 1 :]
        other = other + [routes.sibling(v) for v in diagonal]
        pieces = [a_three, x_three, y_three] + diagonal, other, own[3:]
        (down_w,) = weights_of([w_down], pieces, chips, w_down.shape[0], False)
    else:
        counts, partial = counting(named)
        sums = jnp.sum(lax.all_to_all(per_device(partial), BOTH, 0, 0, tiled=True), axis=0)
        qkv_w, out_w, up_w, down_w = [whole_weight(w, fsdp) for w in (w_qkv, w_out, w_up, w_down)]
        qkv = project_qkv(qkv_w, pos, normed).reshape(images, padded, 3 * width)
        mixed = attend(qkv, seq, width).reshape(images * padded, width)
        resid, normed_two = project_out(out_w, pos, mixed, tokens, ln2_gain)
        active = project_up(up_w, pos, normed_two)
    pooled = project_down(down_w, pos, active, resid, post_gain, sums, images, seq, devices)
    every = lax.all_to_all(pooled, BOTH, 0, 0, tiled=True).reshape(every_image, -1)
    table_new, accum_new, content_grad, proj_grad = update(
        pos, every, w_proj, counts, table[0], accum[0], images, width // devices
    )
    return table_new[None], accum_new[None], content_grad, proj_grad


def solution(mesh):
    rows = P(("grp", "fsdp"), None)
    deep = P(("grp", "fsdp"), None, None)
    split = P("fsdp", None)
    placed = (
        deep, P(), split, split, P(), split, split, P(), P(), deep, deep, P(), rows, P(("grp", "fsdp")),
    )
    return jax.shard_map(
        on_device, mesh=mesh, in_specs=placed, out_specs=(deep, deep, rows, rows), check_vma=False
    )
```

time: 270 us -> 199 us (0.74)
  starting transfers between devices: 81.6 us -> 41.2 us
  waiting for transfers between devices: 74.7 us -> 37.7 us
  blocking collectives: 0 us -> 29.5 us
  local copies, waits for them, and re-layouts: 32.4 us -> 19.1 us
  other arithmetic: 8.94 us -> 4.48 us
  Pallas kernels: 65.7 us -> 61.8 us
    all_to_all x0 -> x2, blocking collectives: none -> 29.5 us  [the longest x1 16.4 us: on_device(): lax.all_to_all(per_device(partial), BOTH, 0, 0, tiled=True)]
    ppermute x40 -> x42, waiting for transfers between devices: 62.3 us -> 34.8 us  [moved(): return lax.ppermute(value, BOTH, pairs)]
    ppermute x40 -> x42, starting transfers between devices: 60.5 us -> 35.2 us  [moved(): return lax.ppermute(value, BOTH, pairs)]
    all_to_all x2 -> x0, waiting for transfers between devices: 12.4 us -> none  [the longest x1 6.97 us: on_device(): lax.all_to_all(pooled, BOTH, 0, 0, tiled=True).reshape(every_image, width)]
    all_to_all x2 -> x0, starting transfers between devices: 8.01 us -> none  [the longest x1 4.31 us: on_device(): lax.all_to_all(partial.reshape(devices, images, proj_width), BOTH, 0, 0,...]
    unnamed x65 -> x69, local copies, waits for them, and re-layouts: 13.2 us -> 5.77 us
    all_to_all x2 -> x1, starting transfers between devices: 13.1 us -> 6.07 us  [broadcast_all(): lax.all_to_all(jnp.broadcast_to(value[None], (devices,) + value.shape), B...]
    pallas_call x1, Pallas kernels: 15 us -> 8.92 us  [attend(): pl.pallas_call(kernel, grid=(images, blocks), out_shape=jax.ShapeDtypeStr...]
  transfers between devices with their start and end apart: 44 -> 43, of which waited for: 9 -> 13; matrix products, arithmetic and copies ran while one was open for 14% -> 9% of each run, Pallas kernels for 23% -> 20%
where the time goes in v1:
time: 199 us; the launch traced here: 198 us
  Pallas kernels  61.8 us (31%)
  starting transfers between devices  41.2 us (21%)
  waiting for transfers between devices  37.7 us (19%)
  blocking collectives  29.5 us (15%)
  local copies, waits for them, and re-layouts  19.1 us (10%)
  other arithmetic  4.48 us (2%)
  matrix products  3.15 us (2%)
    pallas_call x4, Pallas kernels, call_with_weight(): pl.pallas_call(kernel, out_shape=out_shapes, in_specs=[SMEM] + [ANY] * we...  45.3 us
    ppermute x42, starting transfers between devices, moved(): return lax.ppermute(value, BOTH, pairs)  35.2 us
    ppermute x42, waiting for transfers between devices, moved(): return lax.ppermute(value, BOTH, pairs)  34.8 us
    all_to_all x1, blocking collectives, on_device(): lax.all_to_all(per_device(partial), BOTH, 0, 0, tiled=True)  16.4 us
    all_to_all x1, blocking collectives, on_device(): lax.all_to_all(pooled, BOTH, 0, 0, tiled=True).reshape(every_image, -1)  13.1 us
    pallas_call x1, Pallas kernels, attend(): pl.pallas_call(kernel, grid=(images, blocks), out_shape=jax.ShapeDtypeStr...  8.92 us
    pallas_call x1, Pallas kernels, update(): pl.pallas_call(kernel, grid=(blocks // per,), out_shape=[jax.ShapeDtypeSt...  6.87 us
    all_to_all x1, starting transfers between devices, broadcast_all(): lax.all_to_all(jnp.broadcast_to(value[None], (devices,) + value.shape), B...  6.07 us
  transfers between devices with their start and end apart: 43, of which 13 were waited for; matrix products, arithmetic and copies ran while one was open for 9% of the time, Pallas kernels for 20%

profile of v1, /device:TPU:1, one launch (start us, length us, event | category | flops | bytes accessed | tf_op | source)
XLA Modules:
  0.0 198.1 jit_solution(10751341722208601587)
XLA Ops:
  0.7 0.9 constant_dynamic-slice_fusion.3
  1.6 0.9 constant_dynamic-slice_fusion.4
  2.7 0.5 collective-permute-start.4
  3.5 0.8 prepare.1
  4.2 1.0 copy-done
  5.2 1.0 copy-done.1
  6.7 4.4 %collective-permute-start = (bf16[128,1024]{1,0:T(8,128)(2,1)S(1)}, bf16[128,1024]{1,0:T(8,128)(2,1)S(1)}, u32[]{:S(2)}, u32[]{:S(2)}) collective-permute-start(bf16[128,1024]{1,0:T(8,128)(2,1)S(1)} %pad_maximum_fusion.2), channel_id=1, source_target_pairs={{0,6},{1,7},{2,0},{3,1},{4,2},{5,3},{6,4},{7,5},{8,14},{9,15},{10,... | collective-permute-start | bytes 786440 | tf_op jit(solution)/shard_map/ppermute | solution.py:52
  11.1 0.5 collective-permute-start.2
  11.6 0.6 broadcast_in_dim.12
  12.2 6.1 %all-to-all-start = ((s32[32,2,128]{2,1,0:T(2,128)}), s32[32,2,128]{2,1,0:T(2,128)S(1)}, u32[]{:S(2)}, u32[]{:S(2)}) async-start(s32[32,2,128]{2,1,0:T(2,128)} %broadcast_in_dim.12), calls=%async_computation | async-start | bytes 65536 | tf_op jit(solution)/shard_map/all_to_all | solution.py:481
  18.3 0.6 fusion.9
  19.0 1.7 constant_dynamic-slice_fusion.2
  20.6 1.8 constant_dynamic-slice_fusion
  22.5 11.0 %collective-permute-done.1 = bf16[128,1024]{1,0:T(8,128)(2,1)S(1)} collective-permute-done((bf16[128,1024]{1,0:T(8,128)(2,1)S(1)}, bf16[128,1024]{1,0:T(8,128)(2,1)S(1)}, u32[]{:S(2)}, u32[]{:S(2)}) %collective-permute-start.1) | collective-permute-done | bytes 262176 | tf_op jit(solution)/shard_map/ppermute | solution.py:52
  33.6 2.9 %all-to-all-done = s32[32,2,128]{2,1,0:T(2,128)S(1)} async-done(((s32[32,2,128]{2,1,0:T(2,128)}), s32[32,2,128]{2,1,0:T(2,128)S(1)}, u32[]{:S(2)}, u32[]{:S(2)}) %all-to-all-start) | async-done | bytes 32800 | tf_op jit(solution)/shard_map/all_to_all | solution.py:481
  37.6 0.7 collective-permute-start.10
  38.2 2.7 %collective-permute-start.9 = (bf16[128,1024]{1,0:T(8,128)(2,1)}, bf16[128,1024]{1,0:T(8,128)(2,1)}, u32[]{:S(2)}, u32[]{:S(2)}) collective-permute-start(bf16[128,1024]{1,0:T(8,128)(2,1)} %constant_dynamic-slice_fusion.2), channel_id=1, source_target_pairs={{0,6},{1,7},{2,0},{3,1},{4,2},{5,3},{6,4},{7,5},{8,14},{9,15},{10,... | collective-permute-start | bytes 786440 | tf_op jit(solution)/shard_map/ppermute | solution.py:52
  41.0 0.7 compare_reduce_fusion
  41.8 1.3 fusion
  43.1 0.7 convert_bitcast_fusion
  43.9 2.0 %copy.23 = bf16[16,128,64]{2,1,0:T(8,128)(2,1)} copy(bf16[16,128,64]{1,0,2:T(8,128)(2,1)} %convert_bitcast_fusion) | data formatting | bytes 524288 | tf_op jit(solution)/shard_map/convert_element_type | solution.py:498
  45.9 1.9 fusion.2
  47.7 4.9 %collective-permute-done.9 = bf16[128,1024]{1,0:T(8,128)(2,1)} collective-permute-done((bf16[128,1024]{1,0:T(8,128)(2,1)}, bf16[128,1024]{1,0:T(8,128)(2,1)}, u32[]{:S(2)}, u32[]{:S(2)}) %collective-permute-start.9) | collective-permute-done | bytes 262176 | tf_op jit(solution)/shard_map/ppermute | solution.py:52
  52.7 3.3 %collective-permute-done.7.refs_3_ = bf16[384,1024]{1,0:T(8,128)(2,1)} collective-permute-done((bf16[384,1024]{1,0:T(8,128)(2,1)S(1)}, bf16[384,1024]{1,0:T(8,128)(2,1)}, u32[]{:S(2)}, u32[]{:S(2)}) %collective-permute-start.7) | collective-permute-done | bytes 786464 | tf_op jit(solution)/shard_map/ppermute | solution.py:52
  56.1 1.2 collective-permute-start.15
  57.3 2.6 %collective-permute-start.14 = (bf16[128,1024]{1,0:T(8,128)(2,1)}, bf16[128,1024]{1,0:T(8,128)(2,1)S(1)}, u32[]{:S(2)}, u32[]{:S(2)}) collective-permute-start(bf16[128,1024]{1,0:T(8,128)(2,1)} %constant_dynamic-slice_fusion.2), channel_id=1, source_target_pairs={{0,4},{1,5},{2,6},{3,7},{4,0},{5,1},{6,2},{7,3},{8,12},{9,13},{10,... | collective-permute-start | bytes 786440 | tf_op jit(solution)/shard_map/ppermute | solution.py:52
  59.9 1.0 slice.20
  60.9 1.0 slice.21
  62.3 1.2 collective-permute-start.13
  63.5 8.4 %collective-permute-done.14 = bf16[128,1024]{1,0:T(8,128)(2,1)S(1)} collective-permute-done((bf16[128,1024]{1,0:T(8,128)(2,1)}, bf16[128,1024]{1,0:T(8,128)(2,1)S(1)}, u32[]{:S(2)}, u32[]{:S(2)}) %collective-permute-start.14) | collective-permute-done | bytes 262176 | tf_op jit(solution)/shard_map/ppermute | solution.py:52
  71.8 1.1 pad_maximum_fusion.1.refs_2_
  73.0 1.2 collective-permute-start.21
  74.3 1.2 collective-permute-start.17
  75.4 0.9 collective-permute-start.18
  76.3 0.8 copy-done.11
  77.1 1.0 collective-permute-start.23
  78.1 2.7 %collective-permute-start.19 = (bf16[512,256]{1,0:T(8,128)(2,1)}, bf16[512,256]{1,0:T(8,128)(2,1)}, u32[]{:S(2)}, u32[]{:S(2)}) collective-permute-start(bf16[512,256]{1,0:T(8,128)(2,1)} %get-tuple-element.80), channel_id=1, source_target_pairs={{0,6},{1,7},{2,0},{3,1},{4,2},{5,3},{6,4},{7,5},{8,14},{9,15},{10,... | collective-permute-start | bytes 786440 | tf_op jit(solution)/shard_map/ppermute | solution.py:52
  80.7 0.6 pad_add_fusion.1.refs_0_.pos_ref
  81.3 10.2 %project_qkv.1 = bf16[544,3072]{1,0:T(8,128)(2,1)} custom-call(s32[4]{0:T(128)} %pad_add_fusion.1.refs_0_.pos_ref, bf16[128,3072]{1,0:T(8,128)(2,1)} %refs_1_.4, bf16[384,1024]{1,0:T(8,128)(2,1)} %copy-done.4, bf16[384,1024]{1,0:T(8,128)(2,1)} %collective-permute-done.7.refs_3_, bf16[384,1024]{1,0:T(8,128)(2,1)} %collective-permute-done.8.refs_4_, ...), custom_call_target="tpu_custom_call" | custom-call | flops 1 | bytes 1 | tf_op jit(solution)/shard_map/project_qkv/pallas_call | solution.py:192
  91.6 8.9 %attend.1 = bf16[2,272,1024]{2,1,0:T(8,128)(2,1)} custom-call(bf16[2,272,3072]{2,1,0:T(8,128)(2,1)} %bitcast.25, bf16[2,272,3072]{2,1,0:T(8,128)(2,1)} %bitcast.26, bf16[2,272,3072]{2,1,0:T(8,128)(2,1)} %bitcast.27), custom_call_target="tpu_custom_call" | custom-call | flops 1 | bytes 1 | tf_op jit(solution)/shard_map/attend/pallas_call | solution.py:297
  100.5 1.1 collective-permute-start.27
  101.7 1.0 slice.23
  102.8 1.2 collective-permute-start.24
  104.6 7.7 %project_out.1 = (bf16[544,1024]{1,0:T(8,128)(2,1)}, bf16[544,1024]{1,0:T(8,128)(2,1)}) custom-call(s32[4]{0:T(128)} %pad_add_fusion.1.refs_0_.pos_ref, bf16[128,1024]{1,0:T(8,128)(2,1)} %refs_1_.5, bf16[384,1024]{1,0:T(8,128)(2,1)} %copy-done.4, bf16[384,1024]{1,0:T(8,128)(2,1)} %collective-permute-done.7.refs_3_, ...), custom_call_target="tpu_custom_call" | custom-call | flops 1 | bytes 1 | tf_op jit(solution)/shard_map/project_out/pallas_call | solution.py:192
  112.3 1.0 constant_dynamic-update-slice_fusion.2
  113.3 4.8 %collective-permute-done.26 = bf16[512,256]{1,0:T(8,128)(2,1)S(1)} collective-permute-done((bf16[512,256]{1,0:T(8,128)(2,1)}, bf16[512,256]{1,0:T(8,128)(2,1)S(1)}, u32[]{:S(2)}, u32[]{:S(2)}) %collective-permute-start.26) | collective-permute-done | bytes 262176 | tf_op jit(solution)/shard_map/ppermute | solution.py:52
  118.1 1.2 constant_dynamic-update-slice_fusion.refs_2_
  119.3 1.2 collective-permute-start.31
  120.8 2.3 %collective-permute-start.29 = (bf16[192,1024]{1,0:T(8,128)(2,1)S(1)}, bf16[192,1024]{1,0:T(8,128)(2,1)S(1)}, u32[]{:S(2)}, u32[]{:S(2)}) collective-permute-start(bf16[192,1024]{1,0:T(8,128)(2,1)S(1)} %collective-permute-done.24.refs_5_), channel_id=1, source_target_pairs={{0,1},{1,0},{2,3},{3,2},{4,5},{5,4},{6,7},{7,6},{8,9},{9,8},{10,11... | collective-permute-start | bytes 1179656 | tf_op jit(solution)/shard_map/ppermute | solution.py:52
  123.1 1.2 collective-permute-start.33
  124.6 0.4 collective-permute-done.30.refs_12_
  125.3 0.8 copy-done.23
  126.0 11.4 %project_up.1.refs_15_ = bf16[544,4096]{1,0:T(8,128)(2,1)} custom-call(s32[4]{0:T(128)} %pad_add_fusion.1.refs_0_.pos_ref, bf16[128,4096]{1,0:T(8,128)(2,1)} %refs_1_.6, bf16[384,1024]{1,0:T(8,128)(2,1)} %copy-done.7, bf16[384,1024]{1,0:T(8,128)(2,1)} %copy-done.8, bf16[384,1024]{1,0:T(8,128)(2,1)} %collective-permute-done.18.refs_4_, ...), custom_call_target="tpu_custom_call" | custom-call | flops 1 | bytes 1 | tf_op jit(solution)/shard_map/project_up/pallas_call | solution.py:192
  137.5 2.9 %collective-permute-start.36 = (bf16[1536,256]{1,0:T(8,128)(2,1)S(1)}, bf16[1536,256]{1,0:T(8,128)(2,1)S(1)}, u32[]{:S(2)}, u32[]{:S(2)}) collective-permute-start(bf16[1536,256]{1,0:T(8,128)(2,1)S(1)} %constant_dynamic-update-slice_fusion.refs_2_), channel_id=1, source_target_pairs={{0,1},{1,0},{2,3},{3,2},{4,5},{5,4},{6,7},{7,6},{8,9},{9,8},{10,11... | collective-permute-start | bytes 2359304 | tf_op jit(solution)/shard_map/ppermute | solution.py:52
  140.6 0.4 collective-permute-start.38
  141.0 16.4 %all_to_all.15 = f32[32,2,256]{2,1,0:T(2,128)S(1)} all-to-all(f32[32,2,256]{2,1,0:T(2,128)S(1)} %reshape.97), channel_id=1, replica_groups=mesh['grp'=4,'fsdp'=8] {'grp','fsdp'}, dimensions={0} | all-to-all | bytes 131072 | tf_op jit(solution)/shard_map/all_to_all | solution.py:585
  157.4 0.6 reduce_sum.19.refs_18_
  158.0 0.5 collective-permute-start.39
  159.0 0.7 collective-permute-done.39.refs_12_
  159.7 0.6 collective-permute-done.40.refs_13_
  161.3 16.0 %project_down.1 = bf16[32,2,1792]{2,1,0:T(2,128)(2,1)} custom-call(s32[4]{0:T(128)} %pad_add_fusion.1.refs_0_.pos_ref, bf16[512,1024]{1,0:T(8,128)(2,1)} %refs_1_.7, bf16[1536,256]{1,0:T(8,128)(2,1)} %copy-done.13, bf16[1536,256]{1,0:T(8,128)(2,1)} %copy-done.15, bf16[1536,256]{1,0:T(8,128)(2,1)} %copy-done.16, bf16[512,256]{1,0:T(8,128)(2,1)} %copy-done.24, ...), custom_call_target="tpu_custom_call" | custom-call | flops 1 | bytes 1 | tf_op jit(solution)/shard_map/project_down/pallas_call | solution.py:192
  177.4 13.1 %all_to_all.16 = bf16[32,2,1792]{2,1,0:T(2,128)(2,1)S(1)} all-to-all(bf16[32,2,1792]{2,1,0:T(2,128)(2,1)} %project_down.1), channel_id=1, replica_groups=mesh['grp'=4,'fsdp'=8] {'grp','fsdp'}, dimensions={0} | all-to-all | bytes 458752 | tf_op jit(solution)/shard_map/all_to_all | solution.py:600
  190.5 0.8 reshape.99.every_ref
  191.2 6.9 %update.1 = (f32[2048,256]{1,0:T(8,128)}, f32[2048,256]{1,0:T(8,128)}, f32[2,256]{1,0:T(2,128)}, f32[32,256]{1,0:T(8,128)}) custom-call(s32[4]{0:T(128)} %pad_add_fusion.1.refs_0_.pos_ref, bf16[64,1792]{1,0:T(8,128)(2,1)} %reshape.99.every_ref, bf16[1024,256]{1,0:T(8,128)(2,1)} %proj_ref.1, bf16[2048,64]{1,0:T(8,128)(2,1)} %bitcast.32, ...), custom_call_target="tpu_custom_call" | custom-call | tf_op jit(solution)/shard_map/update/pallas_call | solution.py:456
  (128 shorter events, 6.4 us)
Async XLA Ops:
  2.6 9.0 %copy-start.30 = (s32[128]{0:T(128)S(1)}, s32[128]{0:T(128)}, u32[]{:S(2)}) copy-start(s32[128]{0:T(128)} %param.27) | copy-start | bytes 1540
  2.6 9.0 %copy-start.31 = (s32[128,1]{0,1:T(1,128)S(1)}, s32[128,1]{0,1:T(1,128)}, u32[]{:S(2)}) copy-start(s32[128,1]{0,1:T(1,128)} %param.26) | copy-start | bytes 1540
  2.6 15.7 %copy-start.32 = (s32[32]{0:T(128)S(1)}, s32[32]{0:T(128)}, u32[]{:S(2)}) copy-start(s32[32]{0:T(128)} %param.25) | copy-start | bytes 388
  2.6 3.6 %collective-permute-start.3 = (bf16[128,3072]{1,0:T(8,128)(2,1)}, bf16[128,3072]{1,0:T(8,128)(2,1)}, u32[]{:S(2)}, u32[]{:S(2)}) collective-permute-start(bf16[128,3072]{1,0:T(8,128)(2,1)} %refs_1_.4), channel_id=1, source_target_pairs={{0,1},{1,0},{2,3},{3,2},{4,5},{5,4},{6,7},{7,6},{8,9},{9,8},{10,11... | collective-permute-start | bytes 2359304 | tf_op jit(solution)/shard_map/ppermute | solution.py:52
  2.7 3.5 %collective-permute-start.4 = (bf16[128,1024]{1,0:T(8,128)(2,1)}, bf16[128,1024]{1,0:T(8,128)(2,1)}, u32[]{:S(2)}, u32[]{:S(2)}) collective-permute-start(bf16[128,1024]{1,0:T(8,128)(2,1)} %refs_1_.5), channel_id=1, source_target_pairs={{0,1},{1,0},{2,3},{3,2},{4,5},{5,4},{6,7},{7,6},{8,9},{9,8},{10,11... | collective-permute-start | bytes 786440 | tf_op jit(solution)/shard_map/ppermute | solution.py:52
  6.2 30.2 %collective-permute-start.5 = (bf16[128,4096]{1,0:T(8,128)(2,1)}, bf16[128,4096]{1,0:T(8,128)(2,1)}, u32[]{:S(2)}, u32[]{:S(2)}) collective-permute-start(bf16[128,4096]{1,0:T(8,128)(2,1)} %refs_1_.6), channel_id=1, source_target_pairs={{0,1},{1,0},{2,3},{3,2},{4,5},{5,4},{6,7},{7,6},{8,9},{9,8},{10,11... | collective-permute-start | bytes 3145736 | tf_op jit(solution)/shard_map/ppermute | solution.py:52
  6.3 30.2 %collective-permute-start.6 = (bf16[512,1024]{1,0:T(8,128)(2,1)}, bf16[512,1024]{1,0:T(8,128)(2,1)}, u32[]{:S(2)}, u32[]{:S(2)}) collective-permute-start(bf16[512,1024]{1,0:T(8,128)(2,1)} %refs_1_.7), channel_id=1, source_target_pairs={{0,1},{1,0},{2,3},{3,2},{4,5},{5,4},{6,7},{7,6},{8,9},{9,8},{10,11... | collective-permute-start | bytes 3145736 | tf_op jit(solution)/shard_map/ppermute | solution.py:52
  6.7 15.7 %collective-permute-start = (bf16[128,1024]{1,0:T(8,128)(2,1)S(1)}, bf16[128,1024]{1,0:T(8,128)(2,1)S(1)}, u32[]{:S(2)}, u32[]{:S(2)}) collective-permute-start(bf16[128,1024]{1,0:T(8,128)(2,1)S(1)} %pad_maximum_fusion.2), channel_id=1, source_target_pairs={{0,6},{1,7},{2,0},{3,1},{4,2},{5,3},{6,4},{7,5},{8,14},{9,15},{10,... | collective-permute-start | bytes 786440 | tf_op jit(solution)/shard_map/ppermute | solution.py:52
  11.1 22.3 %collective-permute-start.1 = (bf16[128,1024]{1,0:T(8,128)(2,1)S(1)}, bf16[128,1024]{1,0:T(8,128)(2,1)S(1)}, u32[]{:S(2)}, u32[]{:S(2)}) collective-permute-start(bf16[128,1024]{1,0:T(8,128)(2,1)S(1)} %pad_maximum_fusion.2), channel_id=1, source_target_pairs={{0,4},{1,5},{2,6},{3,7},{4,0},{5,1},{6,2},{7,3},{8,12},{9,13},{10,... | collective-permute-start | bytes 786440 | tf_op jit(solution)/shard_map/ppermute | solution.py:52
  11.1 22.3 %collective-permute-start.2 = (bf16[128,1024]{1,0:T(8,128)(2,1)S(1)}, bf16[128,1024]{1,0:T(8,128)(2,1)S(1)}, u32[]{:S(2)}, u32[]{:S(2)}) collective-permute-start(bf16[128,1024]{1,0:T(8,128)(2,1)S(1)} %pad_maximum_fusion.2), channel_id=1, source_target_pairs={{0,2},{1,3},{2,4},{3,5},{4,6},{5,7},{6,0},{7,1},{8,10},{9,11},{10,... | collective-permute-start | bytes 786440 | tf_op jit(solution)/shard_map/ppermute | solution.py:52
  12.2 24.2 %all-to-all-start = ((s32[32,2,128]{2,1,0:T(2,128)}), s32[32,2,128]{2,1,0:T(2,128)S(1)}, u32[]{:S(2)}, u32[]{:S(2)}) async-start(s32[32,2,128]{2,1,0:T(2,128)} %broadcast_in_dim.12), calls=%async_computation | async-start | bytes 65536 | tf_op jit(solution)/shard_map/all_to_all | solution.py:481
  33.5 14.2 %copy-start.4 = (bf16[384,1024]{1,0:T(8,128)(2,1)}, bf16[384,1024]{1,0:T(8,128)(2,1)S(1)}, u32[]{:S(2)}) copy-start(bf16[384,1024]{1,0:T(8,128)(2,1)S(1)} %pad_maximum_fusion.refs_2_) | copy-start | bytes 2359300
  33.5 12.3 %copy-start.3 = (f32[1,2048,256]{2,1,0:T(8,128)S(1)}, f32[1,2048,256]{2,1,0:T(8,128)}, u32[]{:S(2)}) copy-start(f32[1,2048,256]{2,1,0:T(8,128)} %param.23) | copy-start | bytes 6291460
  36.5 16.2 %collective-permute-start.11 = (bf16[384,1024]{1,0:T(8,128)(2,1)S(1)}, bf16[384,1024]{1,0:T(8,128)(2,1)}, u32[]{:S(2)}, u32[]{:S(2)}) collective-permute-start(bf16[384,1024]{1,0:T(8,128)(2,1)S(1)} %pad_maximum_fusion.refs_2_), channel_id=1, source_target_pairs={{0,1},{1,0},{2,3},{3,2},{4,5},{5,4},{6,7},{7,6},{8,9},{9,8},{10,11... | collective-permute-start | bytes 2359304 | tf_op jit(solution)/shard_map/ppermute | solution.py:52
  36.9 19.1 %collective-permute-start.7 = (bf16[384,1024]{1,0:T(8,128)(2,1)S(1)}, bf16[384,1024]{1,0:T(8,128)(2,1)}, u32[]{:S(2)}, u32[]{:S(2)}) collective-permute-start(bf16[384,1024]{1,0:T(8,128)(2,1)S(1)} %pad_maximum_fusion.refs_2_), channel_id=1, source_target_pairs={{0,8},{1,9},{2,10},{3,11},{4,12},{5,13},{6,14},{7,15},{8,0},{9,1},... | collective-permute-start | bytes 2359304 | tf_op jit(solution)/shard_map/ppermute | solution.py:52
  37.2 18.9 %collective-permute-start.8 = (bf16[384,1024]{1,0:T(8,128)(2,1)S(1)}, bf16[384,1024]{1,0:T(8,128)(2,1)}, u32[]{:S(2)}, u32[]{:S(2)}) collective-permute-start(bf16[384,1024]{1,0:T(8,128)(2,1)S(1)} %pad_maximum_fusion.refs_2_), channel_id=1, source_target_pairs={{0,16},{1,17},{2,18},{3,19},{4,20},{5,21},{6,22},{7,23},{8,24},{9,... | collective-permute-start | bytes 2359304 | tf_op jit(solution)/shard_map/ppermute | solution.py:52
  37.6 10.2 %collective-permute-start.10 = (bf16[128,1024]{1,0:T(8,128)(2,1)}, bf16[128,1024]{1,0:T(8,128)(2,1)}, u32[]{:S(2)}, u32[]{:S(2)}) collective-permute-start(bf16[128,1024]{1,0:T(8,128)(2,1)} %constant_dynamic-slice_fusion.2), channel_id=1, source_target_pairs={{0,2},{1,3},{2,4},{3,5},{4,6},{5,7},{6,0},{7,1},{8,10},{9,11},{10,... | collective-permute-start | bytes 786440 | tf_op jit(solution)/shard_map/ppermute | solution.py:52
  38.2 14.5 %collective-permute-start.9 = (bf16[128,1024]{1,0:T(8,128)(2,1)}, bf16[128,1024]{1,0:T(8,128)(2,1)}, u32[]{:S(2)}, u32[]{:S(2)}) collective-permute-start(bf16[128,1024]{1,0:T(8,128)(2,1)} %constant_dynamic-slice_fusion.2), channel_id=1, source_target_pairs={{0,6},{1,7},{2,0},{3,1},{4,2},{5,3},{6,4},{7,5},{8,14},{9,15},{10,... | collective-permute-start | bytes 786440 | tf_op jit(solution)/shard_map/ppermute | solution.py:52
  56.1 16.9 %collective-permute-start.15 = (bf16[384,1024]{1,0:T(8,128)(2,1)}, bf16[384,1024]{1,0:T(8,128)(2,1)S(1)}, u32[]{:S(2)}, u32[]{:S(2)}) collective-permute-start(bf16[384,1024]{1,0:T(8,128)(2,1)} %collective-permute-done.7.refs_3_), channel_id=1, source_target_pairs={{0,1},{1,0},{2,3},{3,2},{4,5},{5,4},{6,7},{7,6},{8,9},{9,8},{10,11... | collective-permute-start | bytes 2359304 | tf_op jit(solution)/shard_map/ppermute | solution.py:52
  57.3 15.7 %collective-permute-start.16 = (bf16[384,1024]{1,0:T(8,128)(2,1)}, bf16[384,1024]{1,0:T(8,128)(2,1)S(1)}, u32[]{:S(2)}, u32[]{:S(2)}) collective-permute-start(bf16[384,1024]{1,0:T(8,128)(2,1)} %collective-permute-done.8.refs_4_), channel_id=1, source_target_pairs={{0,1},{1,0},{2,3},{3,2},{4,5},{5,4},{6,7},{7,6},{8,9},{9,8},{10,11... | collective-permute-start | bytes 2359304 | tf_op jit(solution)/shard_map/ppermute | solution.py:52
  57.3 14.6 %collective-permute-start.14 = (bf16[128,1024]{1,0:T(8,128)(2,1)}, bf16[128,1024]{1,0:T(8,128)(2,1)S(1)}, u32[]{:S(2)}, u32[]{:S(2)}) collective-permute-start(bf16[128,1024]{1,0:T(8,128)(2,1)} %constant_dynamic-slice_fusion.2), channel_id=1, source_target_pairs={{0,4},{1,5},{2,6},{3,7},{4,0},{5,1},{6,2},{7,3},{8,12},{9,13},{10,... | collective-permute-start | bytes 786440 | tf_op jit(solution)/shard_map/ppermute | solution.py:52
  61.9 11.0 %collective-permute-start.12 = (bf16[192,1024]{1,0:T(8,128)(2,1)S(1)}, bf16[192,1024]{1,0:T(8,128)(2,1)S(1)}, u32[]{:S(2)}, u32[]{:S(2)}) collective-permute-start(bf16[192,1024]{1,0:T(8,128)(2,1)S(1)} %slice.20), channel_id=1, source_target_pairs={{0,16},{1,17},{2,18},{3,19},{4,20},{5,21},{6,22},{7,23},{8,24},{9,... | collective-permute-start | bytes 1179656 | tf_op jit(solution)/shard_map/ppermute | solution.py:52
  62.3 10.7 %collective-permute-start.13 = (bf16[192,1024]{1,0:T(8,128)(2,1)S(1)}, bf16[192,1024]{1,0:T(8,128)(2,1)S(1)}, u32[]{:S(2)}, u32[]{:S(2)}) collective-permute-start(bf16[192,1024]{1,0:T(8,128)(2,1)S(1)} %slice.21), channel_id=1, source_target_pairs={{0,8},{1,9},{2,10},{3,11},{4,12},{5,13},{6,14},{7,15},{8,0},{9,1},... | collective-permute-start | bytes 1179656 | tf_op jit(solution)/shard_map/ppermute | solution.py:52
  72.9 18.6 %copy-start.7 = (bf16[384,1024]{1,0:T(8,128)(2,1)}, bf16[384,1024]{1,0:T(8,128)(2,1)S(1)}, u32[]{:S(2)}) copy-start(bf16[384,1024]{1,0:T(8,128)(2,1)S(1)} %pad_maximum_fusion.1.refs_2_) | copy-start | bytes 2359300
  73.0 8.4 %copy-start.9 = (bf16[192,1024]{1,0:T(8,128)(2,1)}, bf16[192,1024]{1,0:T(8,128)(2,1)S(1)}, u32[]{:S(2)}) copy-start(bf16[192,1024]{1,0:T(8,128)(2,1)S(1)} %collective-permute-done.12.refs_5_) | copy-start | bytes 1179652
  73.0 3.3 %copy-start.10 = (bf16[192,1024]{1,0:T(8,128)(2,1)}, bf16[192,1024]{1,0:T(8,128)(2,1)S(1)}, u32[]{:S(2)}) copy-start(bf16[192,1024]{1,0:T(8,128)(2,1)S(1)} %collective-permute-done.13.refs_6_) | copy-start | bytes 1179652
  73.0 8.3 %copy-start.5 = (bf16[384,1024]{1,0:T(8,128)(2,1)}, bf16[384,1024]{1,0:T(8,128)(2,1)S(1)}, u32[]{:S(2)}) copy-start(bf16[384,1024]{1,0:T(8,128)(2,1)S(1)} %collective-permute-done.15.refs_9_) | copy-start | bytes 2359300
  73.0 8.3 %copy-start.6 = (bf16[384,1024]{1,0:T(8,128)(2,1)}, bf16[384,1024]{1,0:T(8,128)(2,1)S(1)}, u32[]{:S(2)}) copy-start(bf16[384,1024]{1,0:T(8,128)(2,1)S(1)} %collective-permute-done.16.refs_10_) | copy-start | bytes 2359300
  73.0 3.3 %collective-permute-start.21 = (bf16[192,1024]{1,0:T(8,128)(2,1)S(1)}, bf16[192,1024]{1,0:T(8,128)(2,1)S(1)}, u32[]{:S(2)}, u32[]{:S(2)}) collective-permute-start(bf16[192,1024]{1,0:T(8,128)(2,1)S(1)} %collective-permute-done.12.refs_5_), channel_id=1, source_target_pairs={{0,1},{1,0},{2,3},{3,2},{4,5},{5,4},{6,7},{7,6},{8,9},{9,8},{10,11... | collective-permute-start | bytes 1179656 | tf_op jit(solution)/shard_map/ppermute | solution.py:52
  74.2 2.1 %collective-permute-start.22 = (bf16[192,1024]{1,0:T(8,128)(2,1)S(1)}, bf16[192,1024]{1,0:T(8,128)(2,1)S(1)}, u32[]{:S(2)}, u32[]{:S(2)}) collective-permute-start(bf16[192,1024]{1,0:T(8,128)(2,1)S(1)} %collective-permute-done.13.refs_6_), channel_id=1, source_target_pairs={{0,1},{1,0},{2,3},{3,2},{4,5},{5,4},{6,7},{7,6},{8,9},{9,8},{10,11... | collective-permute-start | bytes 1179656 | tf_op jit(solution)/shard_map/ppermute | solution.py:52
  74.3 26.2 %collective-permute-start.17 = (bf16[384,1024]{1,0:T(8,128)(2,1)S(1)}, bf16[384,1024]{1,0:T(8,128)(2,1)S(1)}, u32[]{:S(2)}, u32[]{:S(2)}) collective-permute-start(bf16[384,1024]{1,0:T(8,128)(2,1)S(1)} %pad_maximum_fusion.1.refs_2_), channel_id=1, source_target_pairs={{0,8},{1,9},{2,10},{3,11},{4,12},{5,13},{6,14},{7,15},{8,0},{9,1},... | collective-permute-start | bytes 2359304 | tf_op jit(solution)/shard_map/ppermute | solution.py:52
  75.4 25.1 %collective-permute-start.18 = (bf16[384,1024]{1,0:T(8,128)(2,1)S(1)}, bf16[384,1024]{1,0:T(8,128)(2,1)}, u32[]{:S(2)}, u32[]{:S(2)}) collective-permute-start(bf16[384,1024]{1,0:T(8,128)(2,1)S(1)} %pad_maximum_fusion.1.refs_2_), channel_id=1, source_target_pairs={{0,16},{1,17},{2,18},{3,19},{4,20},{5,21},{6,22},{7,23},{8,24},{9,... | collective-permute-start | bytes 2359304 | tf_op jit(solution)/shard_map/ppermute | solution.py:52
  77.1 23.4 %collective-permute-start.23 = (bf16[384,1024]{1,0:T(8,128)(2,1)S(1)}, bf16[384,1024]{1,0:T(8,128)(2,1)}, u32[]{:S(2)}, u32[]{:S(2)}) collective-permute-start(bf16[384,1024]{1,0:T(8,128)(2,1)S(1)} %pad_maximum_fusion.1.refs_2_), channel_id=1, source_target_pairs={{0,1},{1,0},{2,3},{3,2},{4,5},{5,4},{6,7},{7,6},{8,9},{9,8},{10,11... | collective-permute-start | bytes 2359304 | tf_op jit(solution)/shard_map/ppermute | solution.py:52
  78.1 22.4 %collective-permute-start.19 = (bf16[512,256]{1,0:T(8,128)(2,1)}, bf16[512,256]{1,0:T(8,128)(2,1)}, u32[]{:S(2)}, u32[]{:S(2)}) collective-permute-start(bf16[512,256]{1,0:T(8,128)(2,1)} %get-tuple-element.80), channel_id=1, source_target_pairs={{0,6},{1,7},{2,0},{3,1},{4,2},{5,3},{6,4},{7,5},{8,14},{9,15},{10,... | collective-permute-start | bytes 786440 | tf_op jit(solution)/shard_map/ppermute | solution.py:52
  80.7 19.7 %collective-permute-start.20 = (bf16[512,256]{1,0:T(8,128)(2,1)}, bf16[512,256]{1,0:T(8,128)(2,1)}, u32[]{:S(2)}, u32[]{:S(2)}) collective-permute-start(bf16[512,256]{1,0:T(8,128)(2,1)} %get-tuple-element.80), channel_id=1, source_target_pairs={{0,2},{1,3},{2,4},{3,5},{4,6},{5,7},{6,0},{7,1},{8,10},{9,11},{10,... | collective-permute-start | bytes 786440 | tf_op jit(solution)/shard_map/ppermute | solution.py:52
  100.5 11.8 %copy-start.8 = (bf16[384,1024]{1,0:T(8,128)(2,1)}, bf16[384,1024]{1,0:T(8,128)(2,1)S(1)}, u32[]{:S(2)}) copy-start(bf16[384,1024]{1,0:T(8,128)(2,1)S(1)} %collective-permute-done.17.refs_3_) | copy-start | bytes 2359300
  100.5 17.5 %collective-permute-start.27 = (bf16[384,1024]{1,0:T(8,128)(2,1)S(1)}, bf16[384,1024]{1,0:T(8,128)(2,1)S(1)}, u32[]{:S(2)}, u32[]{:S(2)}) collective-permute-start(bf16[384,1024]{1,0:T(8,128)(2,1)S(1)} %collective-permute-done.17.refs_3_), channel_id=1, source_target_pairs={{0,1},{1,0},{2,3},{3,2},{4,5},{5,4},{6,7},{7,6},{8,9},{9,8},{10,11... | collective-permute-start | bytes 2359304 | tf_op jit(solution)/shard_map/ppermute | solution.py:52
  101.6 16.4 %collective-permute-start.28 = (bf16[384,1024]{1,0:T(8,128)(2,1)}, bf16[384,1024]{1,0:T(8,128)(2,1)S(1)}, u32[]{:S(2)}, u32[]{:S(2)}) collective-permute-start(bf16[384,1024]{1,0:T(8,128)(2,1)} %collective-permute-done.18.refs_4_), channel_id=1, source_target_pairs={{0,1},{1,0},{2,3},{3,2},{4,5},{5,4},{6,7},{7,6},{8,9},{9,8},{10,11... | collective-permute-start | bytes 2359304 | tf_op jit(solution)/shard_map/ppermute | solution.py:52
  102.8 15.3 %collective-permute-start.24 = (bf16[192,1024]{1,0:T(8,128)(2,1)S(1)}, bf16[192,1024]{1,0:T(8,128)(2,1)S(1)}, u32[]{:S(2)}, u32[]{:S(2)}) collective-permute-start(bf16[192,1024]{1,0:T(8,128)(2,1)S(1)} %slice.22), channel_id=1, source_target_pairs={{0,16},{1,17},{2,18},{3,19},{4,20},{5,21},{6,22},{7,23},{8,24},{9,... | collective-permute-start | bytes 1179656 | tf_op jit(solution)/shard_map/ppermute | solution.py:52
  104.0 14.1 %collective-permute-start.25 = (bf16[192,1024]{1,0:T(8,128)(2,1)S(1)}, bf16[192,1024]{1,0:T(8,128)(2,1)S(1)}, u32[]{:S(2)}, u32[]{:S(2)}) collective-permute-start(bf16[192,1024]{1,0:T(8,128)(2,1)S(1)} %slice.23), channel_id=1, source_target_pairs={{0,8},{1,9},{2,10},{3,11},{4,12},{5,13},{6,14},{7,15},{8,0},{9,1},... | collective-permute-start | bytes 1179656 | tf_op jit(solution)/shard_map/ppermute | solution.py:52
  104.3 13.7 %collective-permute-start.26 = (bf16[512,256]{1,0:T(8,128)(2,1)}, bf16[512,256]{1,0:T(8,128)(2,1)S(1)}, u32[]{:S(2)}, u32[]{:S(2)}) collective-permute-start(bf16[512,256]{1,0:T(8,128)(2,1)} %get-tuple-element.80), channel_id=1, source_target_pairs={{0,4},{1,5},{2,6},{3,7},{4,0},{5,1},{6,2},{7,3},{8,12},{9,13},{10,... | collective-permute-start | bytes 786440 | tf_op jit(solution)/shard_map/ppermute | solution.py:52
  118.0 7.0 %copy-start.20 = (bf16[192,1024]{1,0:T(8,128)(2,1)}, bf16[192,1024]{1,0:T(8,128)(2,1)S(1)}, u32[]{:S(2)}) copy-start(bf16[192,1024]{1,0:T(8,128)(2,1)S(1)} %collective-permute-done.24.refs_5_) | copy-start | bytes 1179652
  118.0 7.0 %copy-start.21 = (bf16[192,1024]{1,0:T(8,128)(2,1)}, bf16[192,1024]{1,0:T(8,128)(2,1)S(1)}, u32[]{:S(2)}) copy-start(bf16[192,1024]{1,0:T(8,128)(2,1)S(1)} %collective-permute-done.25.refs_6_) | copy-start | bytes 1179652
  118.1 7.0 %copy-start.18 = (bf16[384,1024]{1,0:T(8,128)(2,1)}, bf16[384,1024]{1,0:T(8,128)(2,1)S(1)}, u32[]{:S(2)}) copy-start(bf16[384,1024]{1,0:T(8,128)(2,1)S(1)} %collective-permute-done.27.refs_9_) | copy-start | bytes 2359300
  118.1 7.0 %copy-start.19 = (bf16[384,1024]{1,0:T(8,128)(2,1)}, bf16[384,1024]{1,0:T(8,128)(2,1)S(1)}, u32[]{:S(2)}) copy-start(bf16[384,1024]{1,0:T(8,128)(2,1)S(1)} %collective-permute-done.28.refs_10_) | copy-start | bytes 2359300
  119.3 18.2 %copy-start.13 = (bf16[1536,256]{1,0:T(8,128)(2,1)}, bf16[1536,256]{1,0:T(8,128)(2,1)S(1)}, u32[]{:S(2)}) copy-start(bf16[1536,256]{1,0:T(8,128)(2,1)S(1)} %constant_dynamic-update-slice_fusion.refs_2_) | copy-start | bytes 2359300
  119.3 21.7 %copy-start.29 = (f32[64,256]{1,0:T(8,128)S(1)}, f32[64,256]{1,0:T(8,128)}, u32[]{:S(2)}) copy-start(f32[64,256]{1,0:T(8,128)} %fusion.2) | copy-start | bytes 196612
  119.3 18.2 %collective-permute-start.31 = (bf16[1536,256]{1,0:T(8,128)(2,1)S(1)}, bf16[1536,256]{1,0:T(8,128)(2,1)S(1)}, u32[]{:S(2)}, u32[]{:S(2)}) collective-permute-start(bf16[1536,256]{1,0:T(8,128)(2,1)S(1)} %constant_dynamic-update-slice_fusion.refs_2_), channel_id=1, source_target_pairs={{0,8},{1,9},{2,10},{3,11},{4,12},{5,13},{6,14},{7,15},{8,0},{9,1},... | collective-permute-start | bytes 2359304 | tf_op jit(solution)/shard_map/ppermute | solution.py:52
  120.5 17.0 %collective-permute-start.32 = (bf16[1536,256]{1,0:T(8,128)(2,1)S(1)}, bf16[1536,256]{1,0:T(8,128)(2,1)S(1)}, u32[]{:S(2)}, u32[]{:S(2)}) collective-permute-start(bf16[1536,256]{1,0:T(8,128)(2,1)S(1)} %constant_dynamic-update-slice_fusion.refs_2_), channel_id=1, source_target_pairs={{0,16},{1,17},{2,18},{3,19},{4,20},{5,21},{6,22},{7,23},{8,24},{9,... | collective-permute-start | bytes 2359304 | tf_op jit(solution)/shard_map/ppermute | solution.py:52
  120.8 3.6 %collective-permute-start.29 = (bf16[192,1024]{1,0:T(8,128)(2,1)S(1)}, bf16[192,1024]{1,0:T(8,128)(2,1)S(1)}, u32[]{:S(2)}, u32[]{:S(2)}) collective-permute-start(bf16[192,1024]{1,0:T(8,128)(2,1)S(1)} %collective-permute-done.24.refs_5_), channel_id=1, source_target_pairs={{0,1},{1,0},{2,3},{3,2},{4,5},{5,4},{6,7},{7,6},{8,9},{9,8},{10,11... | collective-permute-start | bytes 1179656 | tf_op jit(solution)/shard_map/ppermute | solution.py:52
  123.1 1.9 collective-permute-start.30
  123.1 14.3 %collective-permute-start.33 = (bf16[512,256]{1,0:T(8,128)(2,1)}, bf16[512,256]{1,0:T(8,128)(2,1)S(1)}, u32[]{:S(2)}, u32[]{:S(2)}) collective-permute-start(bf16[512,256]{1,0:T(8,128)(2,1)} %get-tuple-element.100), channel_id=1, source_target_pairs={{0,6},{1,7},{2,0},{3,1},{4,2},{5,3},{6,4},{7,5},{8,14},{9,15},{10,... | collective-permute-start | bytes 786440 | tf_op jit(solution)/shard_map/ppermute | solution.py:52
  124.5 13.0 %collective-permute-start.34 = (bf16[512,256]{1,0:T(8,128)(2,1)}, bf16[512,256]{1,0:T(8,128)(2,1)S(1)}, u32[]{:S(2)}, u32[]{:S(2)}) collective-permute-start(bf16[512,256]{1,0:T(8,128)(2,1)} %get-tuple-element.100), channel_id=1, source_target_pairs={{0,2},{1,3},{2,4},{3,5},{4,6},{5,7},{6,0},{7,1},{8,10},{9,11},{10,... | collective-permute-start | bytes 786440 | tf_op jit(solution)/shard_map/ppermute | solution.py:52
  137.4 23.2 %copy-start.24 = (bf16[512,256]{1,0:T(8,128)(2,1)}, bf16[512,256]{1,0:T(8,128)(2,1)S(1)}, u32[]{:S(2)}) copy-start(bf16[512,256]{1,0:T(8,128)(2,1)S(1)} %collective-permute-done.33.refs_5_) | copy-start | bytes 786436
  137.5 3.0 %copy-start.25 = (bf16[512,256]{1,0:T(8,128)(2,1)}, bf16[512,256]{1,0:T(8,128)(2,1)S(1)}, u32[]{:S(2)}) copy-start(bf16[512,256]{1,0:T(8,128)(2,1)S(1)} %collective-permute-done.34.refs_7_) | copy-start | bytes 786436
  137.5 23.2 %copy-start.15 = (bf16[1536,256]{1,0:T(8,128)(2,1)}, bf16[1536,256]{1,0:T(8,128)(2,1)S(1)}, u32[]{:S(2)}) copy-start(bf16[1536,256]{1,0:T(8,128)(2,1)S(1)} %collective-permute-done.31.refs_3_) | copy-start | bytes 2359300
  137.5 23.1 %copy-start.16 = (bf16[1536,256]{1,0:T(8,128)(2,1)}, bf16[1536,256]{1,0:T(8,128)(2,1)S(1)}, u32[]{:S(2)}) copy-start(bf16[1536,256]{1,0:T(8,128)(2,1)S(1)} %collective-permute-done.32.refs_4_) | copy-start | bytes 2359300
  137.5 20.5 %collective-permute-start.36 = (bf16[1536,256]{1,0:T(8,128)(2,1)S(1)}, bf16[1536,256]{1,0:T(8,128)(2,1)S(1)}, u32[]{:S(2)}, u32[]{:S(2)}) collective-permute-start(bf16[1536,256]{1,0:T(8,128)(2,1)S(1)} %constant_dynamic-update-slice_fusion.refs_2_), channel_id=1, source_target_pairs={{0,1},{1,0},{2,3},{3,2},{4,5},{5,4},{6,7},{7,6},{8,9},{9,8},{10,11... | collective-permute-start | bytes 2359304 | tf_op jit(solution)/shard_map/ppermute | solution.py:52
  140.5 17.6 %collective-permute-start.37 = (bf16[1536,256]{1,0:T(8,128)(2,1)S(1)}, bf16[1536,256]{1,0:T(8,128)(2,1)}, u32[]{:S(2)}, u32[]{:S(2)}) collective-permute-start(bf16[1536,256]{1,0:T(8,128)(2,1)S(1)} %collective-permute-done.31.refs_3_), channel_id=1, source_target_pairs={{0,1},{1,0},{2,3},{3,2},{4,5},{5,4},{6,7},{7,6},{8,9},{9,8},{10,11... | collective-permute-start | bytes 2359304 | tf_op jit(solution)/shard_map/ppermute | solution.py:52
  140.6 17.5 %collective-permute-start.38 = (bf16[1536,256]{1,0:T(8,128)(2,1)S(1)}, bf16[1536,256]{1,0:T(8,128)(2,1)}, u32[]{:S(2)}, u32[]{:S(2)}) collective-permute-start(bf16[1536,256]{1,0:T(8,128)(2,1)S(1)} %collective-permute-done.32.refs_4_), channel_id=1, source_target_pairs={{0,1},{1,0},{2,3},{3,2},{4,5},{5,4},{6,7},{7,6},{8,9},{9,8},{10,11... | collective-permute-start | bytes 2359304 | tf_op jit(solution)/shard_map/ppermute | solution.py:52
  141.0 17.0 %collective-permute-start.35 = (bf16[512,256]{1,0:T(8,128)(2,1)}, bf16[512,256]{1,0:T(8,128)(2,1)}, u32[]{:S(2)}, u32[]{:S(2)}) collective-permute-start(bf16[512,256]{1,0:T(8,128)(2,1)} %get-tuple-element.100), channel_id=1, source_target_pairs={{0,4},{1,5},{2,6},{3,7},{4,0},{5,1},{6,2},{7,3},{8,12},{9,13},{10,... | collective-permute-start | bytes 786440 | tf_op jit(solution)/shard_map/ppermute | solution.py:52
  158.0 1.6 collective-permute-start.39
  158.5 1.7 collective-permute-start.40
  158.6 2.0 %collective-permute-start.41 = (bf16[512,256]{1,0:T(8,128)(2,1)}, bf16[512,256]{1,0:T(8,128)(2,1)S(1)}, u32[]{:S(2)}, u32[]{:S(2)}) collective-permute-start(bf16[512,256]{1,0:T(8,128)(2,1)} %copy-done.25), channel_id=1, source_target_pairs={{0,1},{1,0},{2,3},{3,2},{4,5},{5,4},{6,7},{7,6},{8,9},{9,8},{10,11... | collective-permute-start | bytes 786440 | tf_op jit(solution)/shard_map/ppermute | solution.py:52
  (12 other events, 15.7 us)

commit v2 on v1

--- a/solution.py
+++ b/solution.py
@@ -107,46 +107,41 @@
 
     @property
     def copies(self):
-        return 1 if self.plan is None else 2 + len(self.plan)
-
-    def start(self, refs, whole, sems, pos):
-        if self.plan is None:
-            copy = pltpu.make_async_copy(refs[0], whole, sems.at[0])
-            copy.start()
-            return [[copy], [], [], []]
-        plane, chip, core = pos[0], pos[1], pos[2]
+        return 4 if self.plan is None else 8 + len(self.plan)
+
+    def quarter(self, pos, turn):
+        return turn if self.plan is None else pos[0] ^ turn
+
+    def moves(self, refs, whole, sems, pos):
         groups = [[], [], [], []]
         number, half = 0, self.count // 2
 
         def go(source, target, turn):
             nonlocal number
-            copy = pltpu.make_async_copy(source, target, sems.at[number])
-            copy.start()
-            groups[turn].append(copy)
+            groups[turn].append(pltpu.make_async_copy(source, target, sems.at[number]))
             number += 1
 
-        for side in range(2):
-            row = pl.multiple_of((chip * CORES + (core ^ side)) * self.rows, self.rows)
-            go(refs[side * half], whole.at[pl.ds(row, self.rows), :], 0)
-        for buffer, low, count, column, side, step, inner, turn in self.plan:
-            there = lax.rem(chip + step, self.chips)
-            row = (there * CORES + (core ^ side)) * self.rows + inner
-            row = pl.multiple_of(row, math.gcd(self.rows, inner) if inner else self.rows)
-            left = pl.multiple_of((plane ^ turn) * self.wide, LANES)
-            go(
-                refs[side * half + buffer].at[pl.ds(low, count), pl.ds(column, self.wide)],
-                whole.at[pl.ds(row, count), pl.ds(left, self.wide)],
-                turn,
-            )
+        for turn in range(4):
+            columns = pl.ds(pl.multiple_of(self.quarter(pos, turn) * self.wide, LANES), self.wide)
+            if self.plan is None:
+                go(refs[0].at[:, columns], whole.at[turn], turn)
+                continue
+            chip, core = pos[1], pos[2]
+            for side in range(2):
+                row = pl.multiple_of((chip * CORES + (core ^ side)) * self.rows, self.rows)
+                go(refs[side * half].at[:, columns], whole.at[turn, pl.ds(row, self.rows), :], turn)
+            for buffer, low, count, column, side, step, inner, own in self.plan:
+                if own != turn:
+                    continue
+                there = lax.rem(chip + step, self.chips)
+                row = (there * CORES + (core ^ side)) * self.rows + inner
+                row = pl.multiple_of(row, math.gcd(self.rows, inner) if inner else self.rows)
+                go(
+                    refs[side * half + buffer].at[pl.ds(low, count), pl.ds(column, self.wide)],
+                    whole.at[turn, pl.ds(row, count), :],
+                    turn,
+                )
         return groups
-
-    def each_turn(self, refs, whole, sems, pos, body):
-        groups = self.start(refs, whole, sems, pos)
-        for turn in range(4):
-            for copy in groups[turn]:
-                copy.wait()
-            left = (pos[0] ^ turn) * self.wide if self.plan is not None else turn * self.wide
-            body(left)
 
 
 def weights_of(shards, pieces, chips, rows, halved):
@@ -170,34 +165,63 @@
     return Weight(full.shape, shard.shape[1] // 4, [full], None, fsdp // CORES, shard.shape[0])
 
 
-def block_of(wide):
-    return next(size for size in (1024, 768, 512, 256, LANES) if wide % size == 0)
-
-
-def call_with_weight(weight, body, pos, inputs, out_shapes, scratch, room, name):
-    n_in, n_out = len(inputs), len(out_shapes)
+def call_with_weight(weight, body, pos, inputs, outs, scratch, room, name):
+    n_in, n_out = len(inputs), len(outs)
 
     def kernel(*refs):
-        pos_ref = refs[0]
-        pieces = refs[1 : 1 + weight.count]
-        refs = refs[1 + weight.count :]
-        ins, outs, rest = refs[:n_in], refs[n_in : n_in + n_out], refs[n_in + n_out :]
-        whole, sems = rest[0], rest[1]
+        pos_ref, refs = refs[0], refs[1:]
+        pieces, refs = refs[: weight.count], refs[weight.count :]
+        sources, refs = refs[:n_in], refs[n_in:]
+        targets, refs = refs[:n_out], refs[n_out:]
+        whole, sems, in_sems, out_sem = refs[:4]
+        ins, refs = refs[4 : 4 + n_in], refs[4 + n_in :]
+        held, rest = refs[:n_out], refs[n_out:]
+        first = [
+            pltpu.make_async_copy(source, target, in_sems.at[number])
+            for number, (source, target) in enumerate(zip(sources, ins, strict=True))
+        ]
+        for copy in first:
+            copy.start()
+        groups = weight.moves(pieces, whole, sems, pos_ref)
+        for copy in groups[0]:
+            copy.start()
+        sent = []
 
         def each_turn(work):
-            weight.each_turn(pieces, whole, sems, pos_ref, work)
-
-        body(ins, outs, rest[2:], whole, each_turn)
+            for copy in first:
+                copy.wait()
+            for turn in range(4):
+                for copy in groups[turn]:
+                    copy.wait()
+                for copy in groups[turn + 1] if turn < 3 else []:
+                    copy.start()
+                left = pl.multiple_of(weight.quarter(pos_ref, turn) * weight.wide, LANES)
+                work(turn, whole.at[turn], pl.ds(left, weight.wide))
+
+        def flush(number, *at):
+            copy = pltpu.make_async_copy(
+                held[number].at[at], targets[number].at[at], out_sem.at[len(sent)]
+            )
+            copy.start()
+            sent.append(copy)
+
+        body(ins, held, rest, each_turn, flush)
+        for copy in sent:
+            copy.wait()
 
     return pl.pallas_call(
         kernel,
-        out_shape=out_shapes,
-        in_specs=[SMEM] + [ANY] * weight.count + [VMEM] * n_in,
-        out_specs=[VMEM] * n_out,
+        out_shape=outs,
+        in_specs=[SMEM] + [ANY] * (weight.count + n_in),
+        out_specs=[ANY] * n_out,
         scratch_shapes=[
-            pltpu.VMEM(weight.shape, bf16),
+            pltpu.VMEM((4, weight.shape[0], weight.wide), bf16),
             pltpu.SemaphoreType.DMA((weight.copies,)),
+            pltpu.SemaphoreType.DMA((n_in,)),
+            pltpu.SemaphoreType.DMA((8,)),
         ]
+        + [pltpu.VMEM(v.shape, v.dtype) for v in inputs]
+        + [pltpu.VMEM(v.shape, v.dtype) for v in outs]
         + list(scratch),
         compiler_params=pltpu.CompilerParams(vmem_limit_bytes=room * MIB),
         cost_estimate=SHORT,
@@ -207,14 +231,6 @@
 
 def dot32(left, right):
     return jnp.dot(left, right, preferred_element_type=f32)
-
-
-def column_loop(wide, left, work):
-    size = block_of(wide)
-
-    @pl.loop(0, wide // size)
-    def _(number):
-        work(pl.ds(pl.multiple_of(left + number * size, LANES), size))
 
 
 def prepare(hidden, gain, padded):
@@ -247,20 +263,15 @@
 
 
 def project_qkv(weight, pos, normed):
-    def body(ins, outs, scratch, whole, each_turn):
-        def quarter(left):
-            def work(columns):
-                outs[0][:, columns] = dot32(ins[0][...], whole[:, columns]).astype(bf16)
-
-            column_loop(weight.wide, left, work)
+    def body(ins, outs, scratch, each_turn, flush):
+        def quarter(turn, part, columns):
+            outs[0][:, columns] = dot32(ins[0][...], part[...]).astype(bf16)
+            flush(0, slice(None), columns)
 
         each_turn(quarter)
 
-    rows = normed.shape[0]
-    return call_with_weight(
-        weight, body, pos, [normed],
-        [jax.ShapeDtypeStruct((rows, weight.shape[1]), bf16)], [], ROOM, "project_qkv",
-    )[0]
+    out = jax.ShapeDtypeStruct((normed.shape[0], weight.shape[1]), bf16)
+    return call_with_weight(weight, body, pos, [normed], [out], [], ROOM, "project_qkv")[0]
 
 
 def attend(qkv, seq, width):
@@ -300,7 +311,7 @@
         out_shape=jax.ShapeDtypeStruct((images, padded, width), bf16),
         in_specs=[spec(0), spec(1), spec(2)],
         out_specs=spec(0),
-        compiler_params=pltpu.CompilerParams(vmem_limit_bytes=ROOM * MIB),
+        compiler_params=pltpu.CompilerParams(vmem_limit_bytes=16 * MIB),
         cost_estimate=SHORT,
         name="attend",
     )(qkv, qkv, qkv)
@@ -309,25 +320,24 @@
 def project_out(weight, pos, mixed, tokens, gain):
     rows, width = mixed.shape
 
-    def body(ins, outs, scratch, whole, each_turn):
+    def body(ins, outs, scratch, each_turn, flush):
         mixed_ref, tokens_ref, gain_ref = ins
         resid, normed = outs
 
-        def quarter(left):
-            def work(columns):
-                product = dot32(mixed_ref[...], whole[:, columns])
-                resid[:, columns] = (tokens_ref[:, columns].astype(f32) + product).astype(bf16)
-
-            column_loop(weight.wide, left, work)
+        def quarter(turn, part, columns):
+            product = dot32(mixed_ref[...], part[...])
+            resid[:, columns] = (tokens_ref[:, columns].astype(f32) + product).astype(bf16)
 
         each_turn(quarter)
+        flush(0, slice(None), slice(None))
         for number in range(rows // 16):
             at = slice(number * 16, (number + 1) * 16)
             normed[at, :] = norm_rows(resid[at, :].astype(f32), gain_ref[...]).astype(bf16)
+        flush(1, slice(None), slice(None))
 
     shape = jax.ShapeDtypeStruct((rows, width), bf16)
     return call_with_weight(
-        weight, body, pos, [mixed, tokens, gain.reshape(1, -1)], [shape, shape], [], ROOM, "project_out",
+        weight, body, pos, [mixed, tokens, gain.reshape(1, -1)], [shape, shape], [], 12, "project_out"
     )
 
 
@@ -336,21 +346,20 @@
 
 
 def project_up(weight, pos, normed):
-    rows = normed.shape[0]
-
-    def body(ins, outs, scratch, whole, each_turn):
-        def quarter(left):
-            def work(columns):
-                outs[0][:, columns] = gelu(dot32(ins[0][...], whole[:, columns])).astype(bf16)
-
-            column_loop(weight.wide, left, work)
+    size = math.gcd(weight.wide, 512)
+
+    def body(ins, outs, scratch, each_turn, flush):
+        def quarter(turn, part, columns):
+            for number in range(weight.wide // size):
+                left = pl.multiple_of(columns.start + number * size, LANES)
+                upward = dot32(ins[0][...], part[:, number * size : (number + 1) * size])
+                outs[0][:, pl.ds(left, size)] = gelu(upward).astype(bf16)
+            flush(0, slice(None), columns)
 
         each_turn(quarter)
 
-    return call_with_weight(
-        weight, body, pos, [normed],
-        [jax.ShapeDtypeStruct((rows, weight.shape[1]), bf16)], [], ROOM, "project_up",
-    )[0]
+    out = jax.ShapeDtypeStruct((normed.shape[0], weight.shape[1]), bf16)
+    return call_with_weight(weight, body, pos, [normed], [out], [], 20, "project_up")[0]
 
 
 def thirds(values):
@@ -364,20 +373,17 @@
     rows, width = resid.shape
     padded = rows // images
 
-    def body(ins, outs, scratch, whole, each_turn):
+    def body(ins, outs, scratch, each_turn, flush):
         active_ref, resid_ref, gain_ref, sums_ref = ins
         (final,) = scratch
         (pooled,) = outs
+
+        def quarter(turn, part, columns):
+            product = dot32(active_ref[...], part[...])
+            final[:, columns] = resid_ref[:, columns].astype(f32) + product
+
+        each_turn(quarter)
         split = [part.astype(f32) for part in thirds(sums_ref[...])]
-
-        def quarter(left):
-            def work(columns):
-                product = dot32(active_ref[...], whole[:, columns])
-                final[:, columns] = resid_ref[:, columns].astype(f32) + product
-
-            column_loop(weight.wide, left, work)
-
-        each_turn(quarter)
         step = 16
         for image in range(images):
             total = jnp.zeros((step, width), f32)
@@ -393,11 +399,12 @@
             row = jnp.concatenate([mean] + [part[at, :] for part in split], axis=1).astype(bf16)
             for device in range(devices):
                 pooled[device, at, :] = row
+        flush(0, slice(None), slice(None), slice(None))
 
     return call_with_weight(
         weight, body, pos, [active, resid, gain.reshape(1, -1), sums],
         [jax.ShapeDtypeStruct((devices, images, width + 3 * sums.shape[1]), bf16)],
-        [pltpu.VMEM((rows, width), f32)], ROOM, "project_down",
+        [pltpu.VMEM((rows, width), f32)], 26, "project_down",
     )[0]
 
 
@@ -521,9 +528,10 @@
     tokens, normed = prepare(hidden, ln1_gain, padded)
     if simple:
         first = quarter_of([w_qkv, w_out], plane)
-        a_one = joined(routes.along(first, *range(1, chips)))
+        ends = routes.along(first, *near)
+        mid = routes.along(first, middle)
         own = [routes.sibling(w) for w in after([w_qkv, w_out], first)]
-        own += [routes.sibling(w) for w in after([w_up, w_down], own, normed)]
+        a_one = joined(ends[: middle - 1] + mid + ends[middle - 1 :])
         second, third, fourth = (
             quarter_of([w_up], plane), quarter_of([w_down], plane), quarter_of([w_down], plane ^ 3),
         )
@@ -548,9 +556,8 @@
         mid = routes.along(second, middle)
         a_two = joined(ends[: middle - 1] + mid + ends[middle - 1 :])
         other = [a_one_other] + [routes.sibling(v) for v in (x_one, y_one)]
-        low_one, high_one, a_two, third = after(
-            [low_one, high_one, a_two, third], other
-        )
+        sums = jnp.sum(lax.all_to_all(per_device(partial), BOTH, 0, 0, tiled=True), axis=0)
+        low_one, high_one, a_two, third, sums = after([low_one, high_one, a_two, third, sums], other)
         other = other + [routes.sibling(v) for v in (low_one, high_one)]
         pieces = [a_one, x_one, y_one, low_one, high_one], other, own[:2]
         qkv_w, out_w = weights_of([w_qkv, w_out], pieces, chips, rows, True)
@@ -559,33 +566,37 @@
         (a_two_sent,) = after([a_two], other)
         a_two_other = routes.sibling(a_two_sent)
         qkv = project_qkv(qkv_w, pos, normed)
+        qkv, ends, third = after([qkv, ends, third])
+        mid = routes.along(third, middle)
+        own += [routes.sibling(w) for w in after([w_up, w_down], qkv)]
         mixed = attend(qkv.reshape(images, padded, 3 * width), seq, width)
-        x_two, y_two, ends, mixed, third, a_two_other = after(
-            [x_two, y_two, ends, mixed, third, a_two_other]
+        x_two, y_two, ends, mid, mixed, fourth, a_two_other, own = after(
+            [x_two, y_two, ends, mid, mixed, fourth, a_two_other, own]
         )
+        a_three = joined(ends[: middle - 1] + mid + ends[middle - 1 :])
         mixed = mixed.reshape(images * padded, width)
         low_two, high_two = routes.swap(x_two[:half], 2), routes.swap(y_two[half:], 1)
-        mid = routes.along(third, middle)
+        early = routes.along(fourth, *range(1, middle))
         other = [a_two_other] + [routes.sibling(v) for v in (x_two, y_two)]
+        fourth, other = after([fourth, other])
+        last = routes.along(fourth, *range(middle + 1, chips))
         resid, normed_two = project_out(out_w, pos, mixed, tokens, ln2_gain)
-        low_two, high_two, mid, other, normed_two = after([low_two, high_two, mid, other, normed_two])
+        low_two, high_two, early, other, normed_two, a_three, fourth = after(
+            [low_two, high_two, early, other, normed_two, a_three, fourth]
+        )
         other = other + [routes.sibling(v) for v in (low_two, high_two)]
         pieces = [a_two, x_two, y_two, low_two, high_two], other, own[2:3]
         (up_w,) = weights_of([w_up], pieces, chips, rows, True)
-        a_three = joined(ends[: middle - 1] + mid + ends[middle - 1 :])
         x_three, y_three = routes.swap(a_three, 1), routes.swap(a_three, 2)
-        ends = routes.along(fourth, *near)
-        (normed_two,) = after([normed_two], other)
+        mid = routes.along(fourth, middle)
+        a_three_sent, other = after([a_three, other])
+        a_three_other = routes.sibling(a_three_sent)
         active = project_up(up_w, pos, normed_two)
-        active, partial, a_three_sent, x_three, y_three, ends, fourth = after(
-            [active, partial, a_three, x_three, y_three, ends, fourth]
+        active, mid, a_three_other, x_three, y_three, last = after(
+            [active, mid, a_three_other, x_three, y_three, last]
         )
-        mid = routes.along(fourth, middle)
-        other = [routes.sibling(v) for v in (a_three_sent, x_three, y_three)]
-        sums = jnp.sum(lax.all_to_all(per_device(partial), BOTH, 0, 0, tiled=True), axis=0)
-        ends, mid, other = after([ends, mid, other], sums)
-        diagonal = ends[: middle - 1] + mid + ends[middle - 1 :]
-        other = other + [routes.sibling(v) for v in diagonal]
+        diagonal = early + mid + last
+        other = [a_three_other] + [routes.sibling(v) for v in [x_three, y_three] + diagonal]
         pieces = [a_three, x_three, y_three] + diagonal, other, own[3:]
         (down_w,) = weights_of([w_down], pieces, chips, w_down.shape[0], False)
     else:

time: 199 us -> 189 us (0.950)
  Pallas kernels: 61.8 us -> 52.5 us
  blocking collectives: 29.5 us -> 23.5 us
  waiting for transfers between devices: 37.7 us -> 41.6 us
  other arithmetic: 4.48 us -> 7.8 us
  starting transfers between devices: 41.2 us -> 38.9 us
  matrix products: 3.15 us -> 5.26 us
    pallas_call x4, Pallas kernels: 45.3 us -> 37.5 us  [call_with_weight(): pl.pallas_call(kernel, out_shape=outs, in_specs=[SMEM] + [ANY] * (weight....]
    ppermute x42, waiting for transfers between devices: 34.8 us -> 40.4 us  [moved(): return lax.ppermute(value, BOTH, pairs)]
    all_to_all x1, blocking collectives: 16.4 us -> 11.7 us  [on_device(): lax.all_to_all(per_device(partial), BOTH, 0, 0, tiled=True)]
    concatenate x2 -> x3, other arithmetic: 1.13 us -> 3.25 us  [on_device(): joined = lambda parts: jnp.concatenate(parts, axis=0)]
    unnamed x69 -> x71, local copies, waits for them, and re-layouts: 5.77 us -> 7.1 us
  transfers between devices with their start and end apart: 43 -> 43, of which waited for: 13 -> 13; matrix products, arithmetic and copies ran while one was open for 9% -> 11% of each run, Pallas kernels for 20% -> 17%
where the time goes in v2:
time: 189 us; the launch traced here: 188 us
  Pallas kernels  52.5 us (28%)
  waiting for transfers between devices  41.6 us (22%)
  starting transfers between devices  38.9 us (21%)
  blocking collectives  23.5 us (12%)
  local copies, waits for them, and re-layouts  17.4 us (9%)
  other arithmetic  7.8 us (4%)
  matrix products  5.26 us (3%)
    ppermute x42, waiting for transfers between devices, moved(): return lax.ppermute(value, BOTH, pairs)  40.4 us
    pallas_call x4, Pallas kernels, call_with_weight(): pl.pallas_call(kernel, out_shape=outs, in_specs=[SMEM] + [ANY] * (weight....  37.5 us
    ppermute x42, starting transfers between devices, moved(): return lax.ppermute(value, BOTH, pairs)  33.9 us
    all_to_all x1, blocking collectives, on_device(): lax.all_to_all(pooled, BOTH, 0, 0, tiled=True).reshape(every_image, -1)  11.8 us
    all_to_all x1, blocking collectives, on_device(): lax.all_to_all(per_device(partial), BOTH, 0, 0, tiled=True)  11.7 us
    pallas_call x1, Pallas kernels, attend(): pl.pallas_call(kernel, grid=(images, blocks), out_shape=jax.ShapeDtypeStr...  7.36 us
    unnamed x71, local copies, waits for them, and re-layouts  7.1 us
    pallas_call x1, Pallas kernels, update(): pl.pallas_call(kernel, grid=(blocks // per,), out_shape=[jax.ShapeDtypeSt...  6.86 us
  transfers between devices with their start and end apart: 43, of which 13 were waited for; matrix products, arithmetic and copies ran while one was open for 11% of the time, Pallas kernels for 17%

profile of v2, /device:TPU:1, one launch (start us, length us, event | category | flops | bytes accessed | tf_op | source)
XLA Modules:
  0.0 188.1 jit_solution(13196346273914441538)
XLA Ops:
  0.7 0.9 constant_dynamic-slice_fusion.3
  1.6 0.9 constant_dynamic-slice_fusion.4
  2.7 4.8 %collective-permute-start = (bf16[128,1024]{1,0:T(8,128)(2,1)S(1)}, bf16[128,1024]{1,0:T(8,128)(2,1)}, u32[]{:S(2)}, u32[]{:S(2)}) collective-permute-start(bf16[128,1024]{1,0:T(8,128)(2,1)S(1)} %pad_maximum_fusion.3), channel_id=1, source_target_pairs={{0,6},{1,7},{2,0},{3,1},{4,2},{5,3},{6,4},{7,5},{8,14},{9,15},{10,... | collective-permute-start | bytes 786440 | tf_op jit(solution)/shard_map/ppermute | solution.py:52
  7.9 0.9 collective-permute-start.4
  8.8 0.7 pad_add_fusion
  9.5 0.6 broadcast_in_dim.12
  10.1 4.9 %all-to-all-start = ((s32[32,2,128]{2,1,0:T(2,128)}), s32[32,2,128]{2,1,0:T(2,128)S(1)}, u32[]{:S(2)}, u32[]{:S(2)}) async-start(s32[32,2,128]{2,1,0:T(2,128)} %broadcast_in_dim.12), calls=%async_computation | async-start | bytes 65536 | tf_op jit(solution)/shard_map/all_to_all | solution.py:488
  15.1 1.7 constant_dynamic-slice_fusion.2
  16.8 0.6 fusion.9
  17.6 0.8 prepare.1
  18.4 1.0 copy-done.21
  19.4 1.0 copy-done.22
  20.4 0.9 constant_dynamic-slice_fusion
  21.3 9.0 %collective-permute-done.1 = bf16[128,1024]{1,0:T(8,128)(2,1)} collective-permute-done((bf16[128,1024]{1,0:T(8,128)(2,1)S(1)}, bf16[128,1024]{1,0:T(8,128)(2,1)}, u32[]{:S(2)}, u32[]{:S(2)}) %collective-permute-start.1) | collective-permute-done | bytes 262176 | tf_op jit(solution)/shard_map/ppermute | solution.py:52
  30.3 1.2 pad_maximum_fusion.refs_2_
  31.5 1.3 all-to-all-done
  32.8 0.7 copy-done.25
  33.8 0.6 copy-done.32
  34.8 1.6 collective-permute-start.9
  36.3 2.5 %collective-permute-start.7 = (bf16[128,1024]{1,0:T(8,128)(2,1)}, bf16[128,1024]{1,0:T(8,128)(2,1)}, u32[]{:S(2)}, u32[]{:S(2)}) collective-permute-start(bf16[128,1024]{1,0:T(8,128)(2,1)} %constant_dynamic-slice_fusion.2), channel_id=1, source_target_pairs={{0,6},{1,7},{2,0},{3,1},{4,2},{5,3},{6,4},{7,5},{8,14},{9,15},{10,... | collective-permute-start | bytes 786440 | tf_op jit(solution)/shard_map/ppermute | solution.py:52
  39.0 0.6 compare_reduce_fusion
  39.7 1.6 fusion
  41.4 1.1 convert_bitcast_fusion
  42.5 1.1 copy.23
  43.5 3.6 %fusion.2 = f32[64,256]{1,0:T(8,128)} fusion(f32[8,8,16,128]{3,2,1,0:T(8,128)} %bitcast.17, f32[1,2048,256]{2,1,0:T(8,128)} %param.23), kind=kOutput, calls=%fused_computation.6 | convolution fusion | flops 402653184 | bytes 2686976 | tf_op jit(solution)/shard_map/dot_general | solution.py:501
  47.2 5.3 %collective-permute-done.8 = bf16[128,1024]{1,0:T(8,128)(2,1)} collective-permute-done((bf16[128,1024]{1,0:T(8,128)(2,1)}, bf16[128,1024]{1,0:T(8,128)(2,1)}, u32[]{:S(2)}, u32[]{:S(2)}) %collective-permute-start.8) | collective-permute-done | bytes 262176 | tf_op jit(solution)/shard_map/ppermute | solution.py:52
  52.5 0.6 collective-permute-done.6.refs_4_
  53.1 1.3 collective-permute-start.13
  54.5 2.2 %collective-permute-start.12 = (bf16[128,1024]{1,0:T(8,128)(2,1)}, bf16[128,1024]{1,0:T(8,128)(2,1)}, u32[]{:S(2)}, u32[]{:S(2)}) collective-permute-start(bf16[128,1024]{1,0:T(8,128)(2,1)} %constant_dynamic-slice_fusion.2), channel_id=1, source_target_pairs={{0,4},{1,5},{2,6},{3,7},{4,0},{5,1},{6,2},{7,3},{8,12},{9,13},{10,... | collective-permute-start | bytes 786440 | tf_op jit(solution)/shard_map/ppermute | solution.py:52
  56.8 0.8 slice.20
  57.6 0.8 slice.21
  58.3 0.6 collective-permute-start.10
  58.9 0.6 collective-permute-start.11
  59.6 1.5 reshape.94
  61.1 11.7 %all_to_all.15 = f32[32,2,256]{2,1,0:T(2,128)} all-to-all(f32[32,2,256]{2,1,0:T(2,128)} %reshape.94), channel_id=1, replica_groups=mesh['grp'=4,'fsdp'=8] {'grp','fsdp'}, dimensions={0} | all-to-all | bytes 131072 | tf_op jit(solution)/shard_map/all_to_all | solution.py:559
  72.8 0.9 reduce_sum.19.refs_18_
  73.6 2.0 %pad_maximum_fusion.1.refs_2_ = bf16[384,1024]{1,0:T(8,128)(2,1)} fusion(bf16[128,1024]{1,0:T(8,128)(2,1)} %collective-permute-done.8, bf16[128,1024]{1,0:T(8,128)(2,1)} %collective-permute-done.12, bf16[128,1024]{1,0:T(8,128)(2,1)} %collective-permute-done.7), kind=kLoop, calls=%fused_computation.4 | loop fusion | flops 2359296 | bytes 1572864 | tf_op jit(solution)/shard_map/concatenate | solution.py:523
  76.3 1.8 collective-permute-start.19
  78.1 0.7 pad_add_fusion.1.refs_0_.pos_ref
  78.8 0.7 copy-done.17
  79.5 0.8 copy-done.19
  80.3 9.6 %project_qkv.1 = bf16[544,3072]{1,0:T(8,128)(2,1)} custom-call(s32[4]{0:T(128)} %pad_add_fusion.1.refs_0_.pos_ref, bf16[128,3072]{1,0:T(8,128)(2,1)} %refs_1_.4, bf16[384,1024]{1,0:T(8,128)(2,1)} %copy-done.1, bf16[384,1024]{1,0:T(8,128)(2,1)} %copy-done.3, bf16[384,1024]{1,0:T(8,128)(2,1)} %copy-done.5, bf16[192,1024]{1,0:T(8,128)(2,1)} %copy-done.15, ...), custom_call_target="tpu_custom_call" | custom-call | flops 1 | bytes 1 | tf_op jit(solution)/shard_map/project_qkv/pallas_call | solution.py:212
  90.9 1.9 collective-permute-start.23
  93.3 0.8 collective-permute-start.16
  94.1 10.2 %collective-permute-done.21 = bf16[512,256]{1,0:T(8,128)(2,1)S(1)} collective-permute-done((bf16[512,256]{1,0:T(8,128)(2,1)}, bf16[512,256]{1,0:T(8,128)(2,1)S(1)}, u32[]{:S(2)}, u32[]{:S(2)}) %collective-permute-start.21) | collective-permute-done | bytes 262176 | tf_op jit(solution)/shard_map/ppermute | solution.py:52
  104.3 1.5 collective-permute-start.22
  105.8 1.9 %copy-done = bf16[544,3072]{1,0:T(8,128)(2,1)S(1)} copy-done((bf16[544,3072]{1,0:T(8,128)(2,1)S(1)}, bf16[544,3072]{1,0:T(8,128)(2,1)}, u32[]{:S(2)}) %copy-start) | copy-done | bytes 3342360
  107.8 7.4 %attend.1 = bf16[2,272,1024]{2,1,0:T(8,128)(2,1)S(1)} custom-call(bf16[2,272,3072]{2,1,0:T(8,128)(2,1)S(1)} %bitcast.24, bf16[2,272,3072]{2,1,0:T(8,128)(2,1)S(1)} %bitcast.25, bf16[2,272,3072]{2,1,0:T(8,128)(2,1)S(1)} %bitcast.26), custom_call_target="tpu_custom_call" | custom-call | flops 1 | bytes 1 | tf_op jit(solution)/shard_map/attend/pallas_call | solution.py:308
  115.9 0.8 collective-permute-start.25
  116.7 1.2 collective-permute-start.26
  117.8 1.3 collective-permute-start.27
  119.3 5.8 %project_out.1 = (bf16[544,1024]{1,0:T(8,128)(2,1)S(1)}, bf16[544,1024]{1,0:T(8,128)(2,1)S(1)}) custom-call(s32[4]{0:T(128)S(1)} %copy-done.27, bf16[128,1024]{1,0:T(8,128)(2,1)S(1)} %copy-done.24, bf16[384,1024]{1,0:T(8,128)(2,1)S(1)} %copy-done.2, bf16[384,1024]{1,0:T(8,128)(2,1)S(1)} %copy-done.4, bf16[384,1024]{1,0:T(8,128)(2,1)S(1)} %copy-done.6, ...), custom_call_target="tpu_custom_call" | custom-call | flops 1 | bytes 1 | tf_op jit(solution)/shard_map/project_out/pallas_call | solution.py:212
  125.2 1.5 collective-permute-done.25.refs_5_
  127.0 1.2 collective-permute-start.30
  128.2 1.2 collective-permute-start.34
  130.1 0.7 collective-permute-start.33
  130.9 1.6 collective-permute-start.36
  132.4 9.1 %project_up.1.refs_15_ = bf16[544,4096]{1,0:T(8,128)(2,1)S(1)} custom-call(s32[4]{0:T(128)S(1)} %copy-done.27, bf16[128,4096]{1,0:T(8,128)(2,1)S(1)} %copy-done.14, bf16[384,1024]{1,0:T(8,128)(2,1)S(1)} %copy-done.11, bf16[384,1024]{1,0:T(8,128)(2,1)S(1)} %collective-permute-done.15.refs_3_, bf16[384,1024]{1,0:T(8,128)(2,1)S(1)} %collective-permute-done.16.refs_4_, ...), custom_call_target="tpu_custom_call" | custom-call | flops 1 | bytes 1 | tf_op jit(solution)/shard_map/project_up/pallas_call | solution.py:212
  141.5 9.4 %collective-permute-done.32.refs_6_ = bf16[512,256]{1,0:T(8,128)(2,1)S(1)} collective-permute-done((bf16[512,256]{1,0:T(8,128)(2,1)S(1)}, bf16[512,256]{1,0:T(8,128)(2,1)S(1)}, u32[]{:S(2)}, u32[]{:S(2)}) %collective-permute-start.32) | collective-permute-done | bytes 262176 | tf_op jit(solution)/shard_map/ppermute | solution.py:52
  152.5 2.4 %collective-permute-done.39.refs_12_ = bf16[512,256]{1,0:T(8,128)(2,1)S(1)} collective-permute-done((bf16[512,256]{1,0:T(8,128)(2,1)S(1)}, bf16[512,256]{1,0:T(8,128)(2,1)S(1)}, u32[]{:S(2)}, u32[]{:S(2)}) %collective-permute-start.39) | collective-permute-done | bytes 262176 | tf_op jit(solution)/shard_map/ppermute | solution.py:52
  155.7 13.0 %project_down.1 = bf16[32,2,1792]{2,1,0:T(2,128)(2,1)S(1)} custom-call(s32[4]{0:T(128)S(1)} %copy-done.27, bf16[512,1024]{1,0:T(8,128)(2,1)S(1)} %copy-done.13, bf16[1536,256]{1,0:T(8,128)(2,1)S(1)} %pad_maximum_fusion.2.refs_2_, bf16[1536,256]{1,0:T(8,128)(2,1)S(1)} %collective-permute-done.34.refs_3_, ...), custom_call_target="tpu_custom_call" | custom-call | flops 1 | bytes 1 | tf_op jit(solution)/shard_map/project_down/pallas_call | solution.py:212
  168.7 11.8 %all_to_all.16 = bf16[32,2,1792]{2,1,0:T(2,128)(2,1)S(1)} all-to-all(bf16[32,2,1792]{2,1,0:T(2,128)(2,1)S(1)} %project_down.1), channel_id=1, replica_groups=mesh['grp'=4,'fsdp'=8] {'grp','fsdp'}, dimensions={0} | all-to-all | bytes 458752 | tf_op jit(solution)/shard_map/all_to_all | solution.py:611
  180.5 0.8 reshape.99.every_ref
  181.3 6.9 %update.1 = (f32[2048,256]{1,0:T(8,128)}, f32[2048,256]{1,0:T(8,128)}, f32[2,256]{1,0:T(2,128)}, f32[32,256]{1,0:T(8,128)}) custom-call(s32[4]{0:T(128)} %pad_add_fusion.1.refs_0_.pos_ref, bf16[64,1792]{1,0:T(8,128)(2,1)} %reshape.99.every_ref, bf16[1024,256]{1,0:T(8,128)(2,1)} %proj_ref.1, bf16[2048,64]{1,0:T(8,128)(2,1)} %bitcast.33, ...), custom_call_target="tpu_custom_call" | custom-call | tf_op jit(solution)/shard_map/update/pallas_call | solution.py:463
  (130 shorter events, 8.1 us)
Async XLA Ops:
  0.6 16.1 %copy-start.34 = (s32[32]{0:T(128)S(1)}, s32[32]{0:T(128)}, u32[]{:S(2)}) copy-start(s32[32]{0:T(128)} %param.25) | copy-start | bytes 388
  0.6 16.7 %copy-start.31 = (bf16[2,257,1024]{2,0,1:T(2,128)(2,1)S(1)}, bf16[2,257,1024]{2,0,1:T(2,128)(2,1)}, u32[]{:S(2)}) copy-start(bf16[2,257,1024]{2,0,1:T(2,128)(2,1)} %param.14) | copy-start | bytes 3158020
  2.5 15.1 %copy-start.28 = (f32[1024]{0:T(1024)S(1)}, f32[1024]{0:T(1024)}, u32[]{:S(2)}) copy-start(f32[1024]{0:T(1024)} %param.15) | copy-start | bytes 12292
  2.6 31.0 %collective-permute-start.3 = (bf16[128,3072]{1,0:T(8,128)(2,1)}, bf16[128,3072]{1,0:T(8,128)(2,1)S(1)}, u32[]{:S(2)}, u32[]{:S(2)}) collective-permute-start(bf16[128,3072]{1,0:T(8,128)(2,1)} %refs_1_.4), channel_id=1, source_target_pairs={{0,1},{1,0},{2,3},{3,2},{4,5},{5,4},{6,7},{7,6},{8,9},{9,8},{10,11... | collective-permute-start | bytes 2359304 | tf_op jit(solution)/shard_map/ppermute | solution.py:52
  2.7 18.6 %collective-permute-start = (bf16[128,1024]{1,0:T(8,128)(2,1)S(1)}, bf16[128,1024]{1,0:T(8,128)(2,1)}, u32[]{:S(2)}, u32[]{:S(2)}) collective-permute-start(bf16[128,1024]{1,0:T(8,128)(2,1)S(1)} %pad_maximum_fusion.3), channel_id=1, source_target_pairs={{0,6},{1,7},{2,0},{3,1},{4,2},{5,3},{6,4},{7,5},{8,14},{9,15},{10,... | collective-permute-start | bytes 786440 | tf_op jit(solution)/shard_map/ppermute | solution.py:52
  7.5 22.9 %collective-permute-start.1 = (bf16[128,1024]{1,0:T(8,128)(2,1)S(1)}, bf16[128,1024]{1,0:T(8,128)(2,1)}, u32[]{:S(2)}, u32[]{:S(2)}) collective-permute-start(bf16[128,1024]{1,0:T(8,128)(2,1)S(1)} %pad_maximum_fusion.3), channel_id=1, source_target_pairs={{0,4},{1,5},{2,6},{3,7},{4,0},{5,1},{6,2},{7,3},{8,12},{9,13},{10,... | collective-permute-start | bytes 786440 | tf_op jit(solution)/shard_map/ppermute | solution.py:52
  7.5 22.9 %collective-permute-start.2 = (bf16[128,1024]{1,0:T(8,128)(2,1)S(1)}, bf16[128,1024]{1,0:T(8,128)(2,1)}, u32[]{:S(2)}, u32[]{:S(2)}) collective-permute-start(bf16[128,1024]{1,0:T(8,128)(2,1)S(1)} %pad_maximum_fusion.3), channel_id=1, source_target_pairs={{0,2},{1,3},{2,4},{3,5},{4,6},{5,7},{6,0},{7,1},{8,10},{9,11},{10,... | collective-permute-start | bytes 786440 | tf_op jit(solution)/shard_map/ppermute | solution.py:52
  7.9 24.9 %collective-permute-start.4 = (bf16[128,1024]{1,0:T(8,128)(2,1)}, bf16[128,1024]{1,0:T(8,128)(2,1)S(1)}, u32[]{:S(2)}, u32[]{:S(2)}) collective-permute-start(bf16[128,1024]{1,0:T(8,128)(2,1)} %refs_1_.5), channel_id=1, source_target_pairs={{0,1},{1,0},{2,3},{3,2},{4,5},{5,4},{6,7},{7,6},{8,9},{9,8},{10,11... | collective-permute-start | bytes 786440 | tf_op jit(solution)/shard_map/ppermute | solution.py:52
  10.1 22.7 %all-to-all-start = ((s32[32,2,128]{2,1,0:T(2,128)}), s32[32,2,128]{2,1,0:T(2,128)S(1)}, u32[]{:S(2)}, u32[]{:S(2)}) async-start(s32[32,2,128]{2,1,0:T(2,128)} %broadcast_in_dim.12), calls=%async_computation | async-start | bytes 65536 | tf_op jit(solution)/shard_map/all_to_all | solution.py:488
  31.5 15.7 %copy-start.1 = (bf16[384,1024]{1,0:T(8,128)(2,1)}, bf16[384,1024]{1,0:T(8,128)(2,1)S(1)}, u32[]{:S(2)}) copy-start(bf16[384,1024]{1,0:T(8,128)(2,1)S(1)} %pad_maximum_fusion.refs_2_) | copy-start | bytes 2359300
  33.5 19.0 %collective-permute-start.5 = (bf16[384,1024]{1,0:T(8,128)(2,1)S(1)}, bf16[384,1024]{1,0:T(8,128)(2,1)S(1)}, u32[]{:S(2)}, u32[]{:S(2)}) collective-permute-start(bf16[384,1024]{1,0:T(8,128)(2,1)S(1)} %pad_maximum_fusion.refs_2_), channel_id=1, source_target_pairs={{0,8},{1,9},{2,10},{3,11},{4,12},{5,13},{6,14},{7,15},{8,0},{9,1},... | collective-permute-start | bytes 2359304 | tf_op jit(solution)/shard_map/ppermute | solution.py:52
  34.4 18.7 %collective-permute-start.6 = (bf16[384,1024]{1,0:T(8,128)(2,1)S(1)}, bf16[384,1024]{1,0:T(8,128)(2,1)S(1)}, u32[]{:S(2)}, u32[]{:S(2)}) collective-permute-start(bf16[384,1024]{1,0:T(8,128)(2,1)S(1)} %pad_maximum_fusion.refs_2_), channel_id=1, source_target_pairs={{0,16},{1,17},{2,18},{3,19},{4,20},{5,21},{6,22},{7,23},{8,24},{9,... | collective-permute-start | bytes 2359304 | tf_op jit(solution)/shard_map/ppermute | solution.py:52
  34.8 18.4 %collective-permute-start.9 = (bf16[384,1024]{1,0:T(8,128)(2,1)S(1)}, bf16[384,1024]{1,0:T(8,128)(2,1)S(1)}, u32[]{:S(2)}, u32[]{:S(2)}) collective-permute-start(bf16[384,1024]{1,0:T(8,128)(2,1)S(1)} %pad_maximum_fusion.refs_2_), channel_id=1, source_target_pairs={{0,1},{1,0},{2,3},{3,2},{4,5},{5,4},{6,7},{7,6},{8,9},{9,8},{10,11... | collective-permute-start | bytes 2359304 | tf_op jit(solution)/shard_map/ppermute | solution.py:52
  36.3 10.8 %collective-permute-start.7 = (bf16[128,1024]{1,0:T(8,128)(2,1)}, bf16[128,1024]{1,0:T(8,128)(2,1)}, u32[]{:S(2)}, u32[]{:S(2)}) collective-permute-start(bf16[128,1024]{1,0:T(8,128)(2,1)} %constant_dynamic-slice_fusion.2), channel_id=1, source_target_pairs={{0,6},{1,7},{2,0},{3,1},{4,2},{5,3},{6,4},{7,5},{8,14},{9,15},{10,... | collective-permute-start | bytes 786440 | tf_op jit(solution)/shard_map/ppermute | solution.py:52
  38.9 13.6 %collective-permute-start.8 = (bf16[128,1024]{1,0:T(8,128)(2,1)}, bf16[128,1024]{1,0:T(8,128)(2,1)}, u32[]{:S(2)}, u32[]{:S(2)}) collective-permute-start(bf16[128,1024]{1,0:T(8,128)(2,1)} %constant_dynamic-slice_fusion.2), channel_id=1, source_target_pairs={{0,2},{1,3},{2,4},{3,5},{4,6},{5,7},{6,0},{7,1},{8,10},{9,11},{10,... | collective-permute-start | bytes 786440 | tf_op jit(solution)/shard_map/ppermute | solution.py:52
  52.5 23.2 %copy-start.3 = (bf16[384,1024]{1,0:T(8,128)(2,1)}, bf16[384,1024]{1,0:T(8,128)(2,1)S(1)}, u32[]{:S(2)}) copy-start(bf16[384,1024]{1,0:T(8,128)(2,1)S(1)} %collective-permute-done.5.refs_3_) | copy-start | bytes 2359300
  53.1 22.6 %copy-start.5 = (bf16[384,1024]{1,0:T(8,128)(2,1)}, bf16[384,1024]{1,0:T(8,128)(2,1)S(1)}, u32[]{:S(2)}) copy-start(bf16[384,1024]{1,0:T(8,128)(2,1)S(1)} %collective-permute-done.6.refs_4_) | copy-start | bytes 2359300
  53.1 22.6 %copy-start.7 = (bf16[384,1024]{1,0:T(8,128)(2,1)}, bf16[384,1024]{1,0:T(8,128)(2,1)S(1)}, u32[]{:S(2)}) copy-start(bf16[384,1024]{1,0:T(8,128)(2,1)S(1)} %collective-permute-done.9.refs_8_) | copy-start | bytes 2359300
  53.1 22.6 %collective-permute-start.13 = (bf16[384,1024]{1,0:T(8,128)(2,1)S(1)}, bf16[384,1024]{1,0:T(8,128)(2,1)S(1)}, u32[]{:S(2)}, u32[]{:S(2)}) collective-permute-start(bf16[384,1024]{1,0:T(8,128)(2,1)S(1)} %collective-permute-done.5.refs_3_), channel_id=1, source_target_pairs={{0,1},{1,0},{2,3},{3,2},{4,5},{5,4},{6,7},{7,6},{8,9},{9,8},{10,11... | collective-permute-start | bytes 2359304 | tf_op jit(solution)/shard_map/ppermute | solution.py:52
  54.4 21.3 %collective-permute-start.14 = (bf16[384,1024]{1,0:T(8,128)(2,1)S(1)}, bf16[384,1024]{1,0:T(8,128)(2,1)}, u32[]{:S(2)}, u32[]{:S(2)}) collective-permute-start(bf16[384,1024]{1,0:T(8,128)(2,1)S(1)} %collective-permute-done.6.refs_4_), channel_id=1, source_target_pairs={{0,1},{1,0},{2,3},{3,2},{4,5},{5,4},{6,7},{7,6},{8,9},{9,8},{10,11... | collective-permute-start | bytes 2359304 | tf_op jit(solution)/shard_map/ppermute | solution.py:52
  54.5 19.1 %collective-permute-start.12 = (bf16[128,1024]{1,0:T(8,128)(2,1)}, bf16[128,1024]{1,0:T(8,128)(2,1)}, u32[]{:S(2)}, u32[]{:S(2)}) collective-permute-start(bf16[128,1024]{1,0:T(8,128)(2,1)} %constant_dynamic-slice_fusion.2), channel_id=1, source_target_pairs={{0,4},{1,5},{2,6},{3,7},{4,0},{5,1},{6,2},{7,3},{8,12},{9,13},{10,... | collective-permute-start | bytes 786440 | tf_op jit(solution)/shard_map/ppermute | solution.py:52
  58.3 17.4 %collective-permute-start.10 = (bf16[192,1024]{1,0:T(8,128)(2,1)}, bf16[192,1024]{1,0:T(8,128)(2,1)S(1)}, u32[]{:S(2)}, u32[]{:S(2)}) collective-permute-start(bf16[192,1024]{1,0:T(8,128)(2,1)} %slice.20), channel_id=1, source_target_pairs={{0,16},{1,17},{2,18},{3,19},{4,20},{5,21},{6,22},{7,23},{8,24},{9,... | collective-permute-start | bytes 1179656 | tf_op jit(solution)/shard_map/ppermute | solution.py:52
  58.9 16.8 %collective-permute-start.11 = (bf16[192,1024]{1,0:T(8,128)(2,1)}, bf16[192,1024]{1,0:T(8,128)(2,1)}, u32[]{:S(2)}, u32[]{:S(2)}) collective-permute-start(bf16[192,1024]{1,0:T(8,128)(2,1)} %slice.21), channel_id=1, source_target_pairs={{0,8},{1,9},{2,10},{3,11},{4,12},{5,13},{6,14},{7,15},{8,0},{9,1},... | collective-permute-start | bytes 1179656 | tf_op jit(solution)/shard_map/ppermute | solution.py:52
  75.8 3.0 %collective-permute-start.17 = (bf16[192,1024]{1,0:T(8,128)(2,1)S(1)}, bf16[192,1024]{1,0:T(8,128)(2,1)S(1)}, u32[]{:S(2)}, u32[]{:S(2)}) collective-permute-start(bf16[192,1024]{1,0:T(8,128)(2,1)S(1)} %collective-permute-done.10.refs_5_), channel_id=1, source_target_pairs={{0,1},{1,0},{2,3},{3,2},{4,5},{5,4},{6,7},{7,6},{8,9},{9,8},{10,11... | collective-permute-start | bytes 1179656 | tf_op jit(solution)/shard_map/ppermute | solution.py:52
  76.2 2.6 %collective-permute-start.18 = (bf16[192,1024]{1,0:T(8,128)(2,1)}, bf16[192,1024]{1,0:T(8,128)(2,1)S(1)}, u32[]{:S(2)}, u32[]{:S(2)}) collective-permute-start(bf16[192,1024]{1,0:T(8,128)(2,1)} %collective-permute-done.11.refs_6_), channel_id=1, source_target_pairs={{0,1},{1,0},{2,3},{3,2},{4,5},{5,4},{6,7},{7,6},{8,9},{9,8},{10,11... | collective-permute-start | bytes 1179656 | tf_op jit(solution)/shard_map/ppermute | solution.py:52
  76.3 13.6 %collective-permute-start.19 = (bf16[512,256]{1,0:T(8,128)(2,1)}, bf16[512,256]{1,0:T(8,128)(2,1)S(1)}, u32[]{:S(2)}, u32[]{:S(2)}) collective-permute-start(bf16[512,256]{1,0:T(8,128)(2,1)} %get-tuple-element.83), channel_id=1, source_target_pairs={{0,6},{1,7},{2,0},{3,1},{4,2},{5,3},{6,4},{7,5},{8,14},{9,15},{10,... | collective-permute-start | bytes 786440 | tf_op jit(solution)/shard_map/ppermute | solution.py:52
  78.1 12.2 %collective-permute-start.20 = (bf16[512,256]{1,0:T(8,128)(2,1)}, bf16[512,256]{1,0:T(8,128)(2,1)S(1)}, u32[]{:S(2)}, u32[]{:S(2)}) collective-permute-start(bf16[512,256]{1,0:T(8,128)(2,1)} %get-tuple-element.83), channel_id=1, source_target_pairs={{0,2},{1,3},{2,4},{3,5},{4,6},{5,7},{6,0},{7,1},{8,10},{9,11},{10,... | collective-permute-start | bytes 786440 | tf_op jit(solution)/shard_map/ppermute | solution.py:52
  78.8 12.1 %copy-start.14 = (bf16[128,4096]{1,0:T(8,128)(2,1)S(1)}, bf16[128,4096]{1,0:T(8,128)(2,1)}, u32[]{:S(2)}) copy-start(bf16[128,4096]{1,0:T(8,128)(2,1)} %refs_1_.6) | copy-start | bytes 3145732
  78.8 13.9 %copy-start.13 = (bf16[512,1024]{1,0:T(8,128)(2,1)S(1)}, bf16[512,1024]{1,0:T(8,128)(2,1)}, u32[]{:S(2)}) copy-start(bf16[512,1024]{1,0:T(8,128)(2,1)} %refs_1_.7) | copy-start | bytes 3145732
  78.8 14.0 %copy-start.11 = (bf16[384,1024]{1,0:T(8,128)(2,1)S(1)}, bf16[384,1024]{1,0:T(8,128)(2,1)}, u32[]{:S(2)}) copy-start(bf16[384,1024]{1,0:T(8,128)(2,1)} %pad_maximum_fusion.1.refs_2_) | copy-start | bytes 2359300
  90.3 14.0 %collective-permute-start.21 = (bf16[512,256]{1,0:T(8,128)(2,1)}, bf16[512,256]{1,0:T(8,128)(2,1)S(1)}, u32[]{:S(2)}, u32[]{:S(2)}) collective-permute-start(bf16[512,256]{1,0:T(8,128)(2,1)} %get-tuple-element.83), channel_id=1, source_target_pairs={{0,4},{1,5},{2,6},{3,7},{4,0},{5,1},{6,2},{7,3},{8,12},{9,13},{10,... | collective-permute-start | bytes 786440 | tf_op jit(solution)/shard_map/ppermute | solution.py:52
  90.9 24.4 %collective-permute-start.23 = (bf16[128,4096]{1,0:T(8,128)(2,1)S(1)}, bf16[128,4096]{1,0:T(8,128)(2,1)S(1)}, u32[]{:S(2)}, u32[]{:S(2)}) collective-permute-start(bf16[128,4096]{1,0:T(8,128)(2,1)S(1)} %copy-done.14), channel_id=1, source_target_pairs={{0,1},{1,0},{2,3},{3,2},{4,5},{5,4},{6,7},{7,6},{8,9},{9,8},{10,11... | collective-permute-start | bytes 3145736 | tf_op jit(solution)/shard_map/ppermute | solution.py:52
  92.7 22.5 %collective-permute-start.24 = (bf16[512,1024]{1,0:T(8,128)(2,1)S(1)}, bf16[512,1024]{1,0:T(8,128)(2,1)S(1)}, u32[]{:S(2)}, u32[]{:S(2)}) collective-permute-start(bf16[512,1024]{1,0:T(8,128)(2,1)S(1)} %copy-done.13), channel_id=1, source_target_pairs={{0,1},{1,0},{2,3},{3,2},{4,5},{5,4},{6,7},{7,6},{8,9},{9,8},{10,11... | collective-permute-start | bytes 3145736 | tf_op jit(solution)/shard_map/ppermute | solution.py:52
  92.8 22.4 %collective-permute-start.15 = (bf16[384,1024]{1,0:T(8,128)(2,1)S(1)}, bf16[384,1024]{1,0:T(8,128)(2,1)S(1)}, u32[]{:S(2)}, u32[]{:S(2)}) collective-permute-start(bf16[384,1024]{1,0:T(8,128)(2,1)S(1)} %copy-done.11), channel_id=1, source_target_pairs={{0,8},{1,9},{2,10},{3,11},{4,12},{5,13},{6,14},{7,15},{8,0},{9,1},... | collective-permute-start | bytes 2359304 | tf_op jit(solution)/shard_map/ppermute | solution.py:52
  93.3 21.9 %collective-permute-start.16 = (bf16[384,1024]{1,0:T(8,128)(2,1)S(1)}, bf16[384,1024]{1,0:T(8,128)(2,1)S(1)}, u32[]{:S(2)}, u32[]{:S(2)}) collective-permute-start(bf16[384,1024]{1,0:T(8,128)(2,1)S(1)} %copy-done.11), channel_id=1, source_target_pairs={{0,16},{1,17},{2,18},{3,19},{4,20},{5,21},{6,22},{7,23},{8,24},{9,... | collective-permute-start | bytes 2359304 | tf_op jit(solution)/shard_map/ppermute | solution.py:52
  104.3 10.9 %collective-permute-start.22 = (bf16[384,1024]{1,0:T(8,128)(2,1)S(1)}, bf16[384,1024]{1,0:T(8,128)(2,1)S(1)}, u32[]{:S(2)}, u32[]{:S(2)}) collective-permute-start(bf16[384,1024]{1,0:T(8,128)(2,1)S(1)} %copy-done.11), channel_id=1, source_target_pairs={{0,1},{1,0},{2,3},{3,2},{4,5},{5,4},{6,7},{7,6},{8,9},{9,8},{10,11... | collective-permute-start | bytes 2359304 | tf_op jit(solution)/shard_map/ppermute | solution.py:52
  107.7 10.1 %copy-start.33 = (bf16[512,256]{1,0:T(8,128)(2,1)S(1)}, bf16[512,256]{1,0:T(8,128)(2,1)}, u32[]{:S(2)}) copy-start(bf16[512,256]{1,0:T(8,128)(2,1)} %get-tuple-element.111) | copy-start | bytes 786436
  107.7 11.5 %copy-start.6 = (bf16[384,1024]{1,0:T(8,128)(2,1)S(1)}, bf16[384,1024]{1,0:T(8,128)(2,1)}, u32[]{:S(2)}) copy-start(bf16[384,1024]{1,0:T(8,128)(2,1)} %copy-done.5) | copy-start | bytes 2359300
  107.7 11.5 %copy-start.8 = (bf16[384,1024]{1,0:T(8,128)(2,1)S(1)}, bf16[384,1024]{1,0:T(8,128)(2,1)}, u32[]{:S(2)}) copy-start(bf16[384,1024]{1,0:T(8,128)(2,1)} %copy-done.7) | copy-start | bytes 2359300
  107.7 11.5 %copy-start.10 = (bf16[384,1024]{1,0:T(8,128)(2,1)S(1)}, bf16[384,1024]{1,0:T(8,128)(2,1)}, u32[]{:S(2)}) copy-start(bf16[384,1024]{1,0:T(8,128)(2,1)} %copy-done.9) | copy-start | bytes 2359300
  107.7 11.5 %copy-start.16 = (bf16[192,1024]{1,0:T(8,128)(2,1)S(1)}, bf16[192,1024]{1,0:T(8,128)(2,1)}, u32[]{:S(2)}) copy-start(bf16[192,1024]{1,0:T(8,128)(2,1)} %copy-done.15) | copy-start | bytes 1179652
  107.7 11.4 %copy-start.18 = (bf16[192,1024]{1,0:T(8,128)(2,1)S(1)}, bf16[192,1024]{1,0:T(8,128)(2,1)}, u32[]{:S(2)}) copy-start(bf16[192,1024]{1,0:T(8,128)(2,1)} %copy-done.17) | copy-start | bytes 1179652
  107.7 11.4 %copy-start.20 = (bf16[192,1024]{1,0:T(8,128)(2,1)S(1)}, bf16[192,1024]{1,0:T(8,128)(2,1)}, u32[]{:S(2)}) copy-start(bf16[192,1024]{1,0:T(8,128)(2,1)} %copy-done.19) | copy-start | bytes 1179652
  107.7 11.4 %copy-start.23 = (bf16[544,1024]{1,0:T(8,128)(2,1)S(1)}, bf16[544,1024]{1,0:T(8,128)(2,1)}, u32[]{:S(2)}) copy-start(bf16[544,1024]{1,0:T(8,128)(2,1)} %copy-done.22) | copy-start | bytes 3342340
  107.8 11.4 %copy-start.24 = (bf16[128,1024]{1,0:T(8,128)(2,1)S(1)}, bf16[128,1024]{1,0:T(8,128)(2,1)}, u32[]{:S(2)}) copy-start(bf16[128,1024]{1,0:T(8,128)(2,1)} %refs_1_.5) | copy-start | bytes 786436
  107.8 11.4 %copy-start.26 = (bf16[128,1024]{1,0:T(8,128)(2,1)S(1)}, bf16[128,1024]{1,0:T(8,128)(2,1)}, u32[]{:S(2)}) copy-start(bf16[128,1024]{1,0:T(8,128)(2,1)} %copy-done.25) | copy-start | bytes 786436
  115.2 9.9 %collective-permute-start.28 = (bf16[384,1024]{1,0:T(8,128)(2,1)S(1)}, bf16[384,1024]{1,0:T(8,128)(2,1)S(1)}, u32[]{:S(2)}, u32[]{:S(2)}) collective-permute-start(bf16[384,1024]{1,0:T(8,128)(2,1)S(1)} %collective-permute-done.15.refs_3_), channel_id=1, source_target_pairs={{0,1},{1,0},{2,3},{3,2},{4,5},{5,4},{6,7},{7,6},{8,9},{9,8},{10,11... | collective-permute-start | bytes 2359304 | tf_op jit(solution)/shard_map/ppermute | solution.py:52
  115.3 9.8 %collective-permute-start.29 = (bf16[384,1024]{1,0:T(8,128)(2,1)S(1)}, bf16[384,1024]{1,0:T(8,128)(2,1)S(1)}, u32[]{:S(2)}, u32[]{:S(2)}) collective-permute-start(bf16[384,1024]{1,0:T(8,128)(2,1)S(1)} %collective-permute-done.16.refs_4_), channel_id=1, source_target_pairs={{0,1},{1,0},{2,3},{3,2},{4,5},{5,4},{6,7},{7,6},{8,9},{9,8},{10,11... | collective-permute-start | bytes 2359304 | tf_op jit(solution)/shard_map/ppermute | solution.py:52
  115.9 10.8 %collective-permute-start.25 = (bf16[192,1024]{1,0:T(8,128)(2,1)S(1)}, bf16[192,1024]{1,0:T(8,128)(2,1)S(1)}, u32[]{:S(2)}, u32[]{:S(2)}) collective-permute-start(bf16[192,1024]{1,0:T(8,128)(2,1)S(1)} %slice.22), channel_id=1, source_target_pairs={{0,16},{1,17},{2,18},{3,19},{4,20},{5,21},{6,22},{7,23},{8,24},{9,... | collective-permute-start | bytes 1179656 | tf_op jit(solution)/shard_map/ppermute | solution.py:52
  116.7 10.4 %collective-permute-start.26 = (bf16[192,1024]{1,0:T(8,128)(2,1)S(1)}, bf16[192,1024]{1,0:T(8,128)(2,1)S(1)}, u32[]{:S(2)}, u32[]{:S(2)}) collective-permute-start(bf16[192,1024]{1,0:T(8,128)(2,1)S(1)} %slice.23), channel_id=1, source_target_pairs={{0,8},{1,9},{2,10},{3,11},{4,12},{5,13},{6,14},{7,15},{8,0},{9,1},... | collective-permute-start | bytes 1179656 | tf_op jit(solution)/shard_map/ppermute | solution.py:52
  117.8 7.3 %collective-permute-start.27 = (bf16[512,256]{1,0:T(8,128)(2,1)S(1)}, bf16[512,256]{1,0:T(8,128)(2,1)S(1)}, u32[]{:S(2)}, u32[]{:S(2)}) collective-permute-start(bf16[512,256]{1,0:T(8,128)(2,1)S(1)} %copy-done.33), channel_id=1, source_target_pairs={{0,6},{1,7},{2,0},{3,1},{4,2},{5,3},{6,4},{7,5},{8,14},{9,15},{10,... | collective-permute-start | bytes 786440 | tf_op jit(solution)/shard_map/ppermute | solution.py:52
  127.0 28.6 %copy-start.30 = (f32[1024]{0:T(1024)S(1)}, f32[1024]{0:T(1024)}, u32[]{:S(2)}) copy-start(f32[1024]{0:T(1024)} %param.21) | copy-start | bytes 12292
  127.0 2.8 %collective-permute-start.30 = (bf16[192,1024]{1,0:T(8,128)(2,1)S(1)}, bf16[192,1024]{1,0:T(8,128)(2,1)S(1)}, u32[]{:S(2)}, u32[]{:S(2)}) collective-permute-start(bf16[192,1024]{1,0:T(8,128)(2,1)S(1)} %collective-permute-done.25.refs_5_), channel_id=1, source_target_pairs={{0,1},{1,0},{2,3},{3,2},{4,5},{5,4},{6,7},{7,6},{8,9},{9,8},{10,11... | collective-permute-start | bytes 1179656 | tf_op jit(solution)/shard_map/ppermute | solution.py:52
  128.2 1.9 %collective-permute-start.31 = (bf16[192,1024]{1,0:T(8,128)(2,1)S(1)}, bf16[192,1024]{1,0:T(8,128)(2,1)S(1)}, u32[]{:S(2)}, u32[]{:S(2)}) collective-permute-start(bf16[192,1024]{1,0:T(8,128)(2,1)S(1)} %collective-permute-done.26.refs_6_), channel_id=1, source_target_pairs={{0,1},{1,0},{2,3},{3,2},{4,5},{5,4},{6,7},{7,6},{8,9},{9,8},{10,11... | collective-permute-start | bytes 1179656 | tf_op jit(solution)/shard_map/ppermute | solution.py:52
  128.2 22.8 %collective-permute-start.34 = (bf16[1536,256]{1,0:T(8,128)(2,1)S(1)}, bf16[1536,256]{1,0:T(8,128)(2,1)S(1)}, u32[]{:S(2)}, u32[]{:S(2)}) collective-permute-start(bf16[1536,256]{1,0:T(8,128)(2,1)S(1)} %pad_maximum_fusion.2.refs_2_), channel_id=1, source_target_pairs={{0,8},{1,9},{2,10},{3,11},{4,12},{5,13},{6,14},{7,15},{8,0},{9,1},... | collective-permute-start | bytes 2359304 | tf_op jit(solution)/shard_map/ppermute | solution.py:52
  129.4 21.6 %collective-permute-start.35 = (bf16[1536,256]{1,0:T(8,128)(2,1)S(1)}, bf16[1536,256]{1,0:T(8,128)(2,1)S(1)}, u32[]{:S(2)}, u32[]{:S(2)}) collective-permute-start(bf16[1536,256]{1,0:T(8,128)(2,1)S(1)} %pad_maximum_fusion.2.refs_2_), channel_id=1, source_target_pairs={{0,16},{1,17},{2,18},{3,19},{4,20},{5,21},{6,22},{7,23},{8,24},{9,... | collective-permute-start | bytes 2359304 | tf_op jit(solution)/shard_map/ppermute | solution.py:52
  130.1 20.9 %collective-permute-start.33 = (bf16[1536,256]{1,0:T(8,128)(2,1)S(1)}, bf16[1536,256]{1,0:T(8,128)(2,1)S(1)}, u32[]{:S(2)}, u32[]{:S(2)}) collective-permute-start(bf16[1536,256]{1,0:T(8,128)(2,1)S(1)} %pad_maximum_fusion.2.refs_2_), channel_id=1, source_target_pairs={{0,1},{1,0},{2,3},{3,2},{4,5},{5,4},{6,7},{7,6},{8,9},{9,8},{10,11... | collective-permute-start | bytes 2359304 | tf_op jit(solution)/shard_map/ppermute | solution.py:52
  130.8 20.1 %collective-permute-start.32 = (bf16[512,256]{1,0:T(8,128)(2,1)S(1)}, bf16[512,256]{1,0:T(8,128)(2,1)S(1)}, u32[]{:S(2)}, u32[]{:S(2)}) collective-permute-start(bf16[512,256]{1,0:T(8,128)(2,1)S(1)} %copy-done.33), channel_id=1, source_target_pairs={{0,4},{1,5},{2,6},{3,7},{4,0},{5,1},{6,2},{7,3},{8,12},{9,13},{10,... | collective-permute-start | bytes 786440 | tf_op jit(solution)/shard_map/ppermute | solution.py:52
  130.9 20.1 %collective-permute-start.36 = (bf16[512,256]{1,0:T(8,128)(2,1)S(1)}, bf16[512,256]{1,0:T(8,128)(2,1)S(1)}, u32[]{:S(2)}, u32[]{:S(2)}) collective-permute-start(bf16[512,256]{1,0:T(8,128)(2,1)S(1)} %copy-done.33), channel_id=1, source_target_pairs={{0,2},{1,3},{2,4},{3,5},{4,6},{5,7},{6,0},{7,1},{8,10},{9,11},{10,... | collective-permute-start | bytes 786440 | tf_op jit(solution)/shard_map/ppermute | solution.py:52
  151.0 4.7 %collective-permute-start.37 = (bf16[1536,256]{1,0:T(8,128)(2,1)S(1)}, bf16[1536,256]{1,0:T(8,128)(2,1)S(1)}, u32[]{:S(2)}, u32[]{:S(2)}) collective-permute-start(bf16[1536,256]{1,0:T(8,128)(2,1)S(1)} %collective-permute-done.34.refs_3_), channel_id=1, source_target_pairs={{0,1},{1,0},{2,3},{3,2},{4,5},{5,4},{6,7},{7,6},{8,9},{9,8},{10,11... | collective-permute-start | bytes 2359304 | tf_op jit(solution)/shard_map/ppermute | solution.py:52
  151.5 4.2 %collective-permute-start.38 = (bf16[1536,256]{1,0:T(8,128)(2,1)S(1)}, bf16[1536,256]{1,0:T(8,128)(2,1)S(1)}, u32[]{:S(2)}, u32[]{:S(2)}) collective-permute-start(bf16[1536,256]{1,0:T(8,128)(2,1)S(1)} %collective-permute-done.35.refs_4_), channel_id=1, source_target_pairs={{0,1},{1,0},{2,3},{3,2},{4,5},{5,4},{6,7},{7,6},{8,9},{9,8},{10,11... | collective-permute-start | bytes 2359304 | tf_op jit(solution)/shard_map/ppermute | solution.py:52
  151.6 3.3 %collective-permute-start.39 = (bf16[512,256]{1,0:T(8,128)(2,1)S(1)}, bf16[512,256]{1,0:T(8,128)(2,1)S(1)}, u32[]{:S(2)}, u32[]{:S(2)}) collective-permute-start(bf16[512,256]{1,0:T(8,128)(2,1)S(1)} %collective-permute-done.27.refs_5_), channel_id=1, source_target_pairs={{0,1},{1,0},{2,3},{3,2},{4,5},{5,4},{6,7},{7,6},{8,9},{9,8},{10,11... | collective-permute-start | bytes 786440 | tf_op jit(solution)/shard_map/ppermute | solution.py:52
  152.0 3.3 %collective-permute-start.40 = (bf16[512,256]{1,0:T(8,128)(2,1)S(1)}, bf16[512,256]{1,0:T(8,128)(2,1)S(1)}, u32[]{:S(2)}, u32[]{:S(2)}) collective-permute-start(bf16[512,256]{1,0:T(8,128)(2,1)S(1)} %collective-permute-done.32.refs_6_), channel_id=1, source_target_pairs={{0,1},{1,0},{2,3},{3,2},{4,5},{5,4},{6,7},{7,6},{8,9},{9,8},{10,11... | collective-permute-start | bytes 786440 | tf_op jit(solution)/shard_map/ppermute | solution.py:52
  152.1 3.6 %collective-permute-start.41 = (bf16[512,256]{1,0:T(8,128)(2,1)S(1)}, bf16[512,256]{1,0:T(8,128)(2,1)S(1)}, u32[]{:S(2)}, u32[]{:S(2)}) collective-permute-start(bf16[512,256]{1,0:T(8,128)(2,1)S(1)} %collective-permute-done.36.refs_7_), channel_id=1, source_target_pairs={{0,1},{1,0},{2,3},{3,2},{4,5},{5,4},{6,7},{7,6},{8,9},{9,8},{10,11... | collective-permute-start | bytes 786440 | tf_op jit(solution)/shard_map/ppermute | solution.py:52
  (14 other events, 32.6 us)

commit v3 on v2

--- a/solution.py
+++ b/solution.py
@@ -412,7 +412,7 @@
     rows, width = table.shape
     every_image, depth = every.shape[0], proj.shape[0]
     blocks = rows // LANES
-    per = 4 if blocks % 4 == 0 else 1
+    per = 8 if blocks % 8 == 0 else 1
     side = max(share, LANES)
     over = (((0,), (0,)), ((), ()))
 

time: 189 us -> 188 us (level)
  no operation moved by 1% of the time
where the time goes in v3:
time: 188 us; the launch traced here: 187 us
  Pallas kernels  51.5 us (27%)
  waiting for transfers between devices  41.6 us (22%)
  starting transfers between devices  38.9 us (21%)
  blocking collectives  23.5 us (12%)
  local copies, waits for them, and re-layouts  17.4 us (9%)
  other arithmetic  7.8 us (4%)
  matrix products  5.26 us (3%)
    ppermute x42, waiting for transfers between devices, moved(): return lax.ppermute(value, BOTH, pairs)  40.4 us
    pallas_call x4, Pallas kernels, call_with_weight(): pl.pallas_call(kernel, out_shape=outs, in_specs=[SMEM] + [ANY] * (weight....  37.5 us
    ppermute x42, starting transfers between devices, moved(): return lax.ppermute(value, BOTH, pairs)  33.9 us
    all_to_all x1, blocking collectives, on_device(): lax.all_to_all(pooled, BOTH, 0, 0, tiled=True).reshape(every_image, -1)  11.8 us
    all_to_all x1, blocking collectives, on_device(): lax.all_to_all(per_device(partial), BOTH, 0, 0, tiled=True)  11.7 us
    pallas_call x1, Pallas kernels, attend(): pl.pallas_call(kernel, grid=(images, blocks), out_shape=jax.ShapeDtypeStr...  7.36 us
    unnamed x71, local copies, waits for them, and re-layouts  7.1 us
    pallas_call x1, Pallas kernels, update(): pl.pallas_call(kernel, grid=(blocks // per,), out_shape=[jax.ShapeDtypeSt...  5.89 us
  transfers between devices with their start and end apart: 43, of which 13 were waited for; matrix products, arithmetic and copies ran while one was open for 11% of the time, Pallas kernels for 17%

profile of v3, /device:TPU:1, one launch (start us, length us, event | category | flops | bytes accessed | tf_op | source)
XLA Modules:
  0.0 187.1 jit_solution(124521222844787648)
XLA Ops:
  0.7 0.9 constant_dynamic-slice_fusion.3
  1.6 0.9 constant_dynamic-slice_fusion.4
  2.7 4.8 %collective-permute-start = (bf16[128,1024]{1,0:T(8,128)(2,1)S(1)}, bf16[128,1024]{1,0:T(8,128)(2,1)}, u32[]{:S(2)}, u32[]{:S(2)}) collective-permute-start(bf16[128,1024]{1,0:T(8,128)(2,1)S(1)} %pad_maximum_fusion.3), channel_id=1, source_target_pairs={{0,6},{1,7},{2,0},{3,1},{4,2},{5,3},{6,4},{7,5},{8,14},{9,15},{10,... | collective-permute-start | bytes 786440 | tf_op jit(solution)/shard_map/ppermute | solution.py:52
  7.9 0.9 collective-permute-start.4
  8.8 0.7 pad_add_fusion
  9.5 0.6 broadcast_in_dim.12
  10.1 4.9 %all-to-all-start = ((s32[32,2,128]{2,1,0:T(2,128)}), s32[32,2,128]{2,1,0:T(2,128)S(1)}, u32[]{:S(2)}, u32[]{:S(2)}) async-start(s32[32,2,128]{2,1,0:T(2,128)} %broadcast_in_dim.12), calls=%async_computation | async-start | bytes 65536 | tf_op jit(solution)/shard_map/all_to_all | solution.py:488
  15.1 1.7 constant_dynamic-slice_fusion.2
  16.8 0.6 fusion.9
  17.6 0.8 prepare.1
  18.4 1.0 copy-done.21
  19.4 1.0 copy-done.22
  20.4 0.9 constant_dynamic-slice_fusion
  21.3 9.0 %collective-permute-done.1 = bf16[128,1024]{1,0:T(8,128)(2,1)} collective-permute-done((bf16[128,1024]{1,0:T(8,128)(2,1)S(1)}, bf16[128,1024]{1,0:T(8,128)(2,1)}, u32[]{:S(2)}, u32[]{:S(2)}) %collective-permute-start.1) | collective-permute-done | bytes 262176 | tf_op jit(solution)/shard_map/ppermute | solution.py:52
  30.3 1.2 pad_maximum_fusion.refs_2_
  31.5 1.3 all-to-all-done
  32.8 0.7 copy-done.25
  33.8 0.6 copy-done.32
  34.8 1.6 collective-permute-start.9
  36.3 2.5 %collective-permute-start.7 = (bf16[128,1024]{1,0:T(8,128)(2,1)}, bf16[128,1024]{1,0:T(8,128)(2,1)}, u32[]{:S(2)}, u32[]{:S(2)}) collective-permute-start(bf16[128,1024]{1,0:T(8,128)(2,1)} %constant_dynamic-slice_fusion.2), channel_id=1, source_target_pairs={{0,6},{1,7},{2,0},{3,1},{4,2},{5,3},{6,4},{7,5},{8,14},{9,15},{10,... | collective-permute-start | bytes 786440 | tf_op jit(solution)/shard_map/ppermute | solution.py:52
  39.0 0.6 compare_reduce_fusion
  39.7 1.6 fusion
  41.4 1.1 convert_bitcast_fusion
  42.5 1.1 copy.23
  43.5 3.6 %fusion.2 = f32[64,256]{1,0:T(8,128)} fusion(f32[8,8,16,128]{3,2,1,0:T(8,128)} %bitcast.17, f32[1,2048,256]{2,1,0:T(8,128)} %param.23), kind=kOutput, calls=%fused_computation.6 | convolution fusion | flops 402653184 | bytes 2686976 | tf_op jit(solution)/shard_map/dot_general | solution.py:501
  47.2 5.3 %collective-permute-done.8 = bf16[128,1024]{1,0:T(8,128)(2,1)} collective-permute-done((bf16[128,1024]{1,0:T(8,128)(2,1)}, bf16[128,1024]{1,0:T(8,128)(2,1)}, u32[]{:S(2)}, u32[]{:S(2)}) %collective-permute-start.8) | collective-permute-done | bytes 262176 | tf_op jit(solution)/shard_map/ppermute | solution.py:52
  52.5 0.6 collective-permute-done.6.refs_4_
  53.1 1.3 collective-permute-start.13
  54.5 2.2 %collective-permute-start.12 = (bf16[128,1024]{1,0:T(8,128)(2,1)}, bf16[128,1024]{1,0:T(8,128)(2,1)}, u32[]{:S(2)}, u32[]{:S(2)}) collective-permute-start(bf16[128,1024]{1,0:T(8,128)(2,1)} %constant_dynamic-slice_fusion.2), channel_id=1, source_target_pairs={{0,4},{1,5},{2,6},{3,7},{4,0},{5,1},{6,2},{7,3},{8,12},{9,13},{10,... | collective-permute-start | bytes 786440 | tf_op jit(solution)/shard_map/ppermute | solution.py:52
  56.8 0.8 slice.20
  57.6 0.8 slice.21
  58.3 0.6 collective-permute-start.10
  58.9 0.6 collective-permute-start.11
  59.6 1.5 reshape.94
  61.1 11.7 %all_to_all.15 = f32[32,2,256]{2,1,0:T(2,128)} all-to-all(f32[32,2,256]{2,1,0:T(2,128)} %reshape.94), channel_id=1, replica_groups=mesh['grp'=4,'fsdp'=8] {'grp','fsdp'}, dimensions={0} | all-to-all | bytes 131072 | tf_op jit(solution)/shard_map/all_to_all | solution.py:559
  72.8 0.9 reduce_sum.19.refs_18_
  73.6 2.0 %pad_maximum_fusion.1.refs_2_ = bf16[384,1024]{1,0:T(8,128)(2,1)} fusion(bf16[128,1024]{1,0:T(8,128)(2,1)} %collective-permute-done.8, bf16[128,1024]{1,0:T(8,128)(2,1)} %collective-permute-done.12, bf16[128,1024]{1,0:T(8,128)(2,1)} %collective-permute-done.7), kind=kLoop, calls=%fused_computation.4 | loop fusion | flops 2359296 | bytes 1572864 | tf_op jit(solution)/shard_map/concatenate | solution.py:523
  76.3 1.8 collective-permute-start.19
  78.1 0.7 pad_add_fusion.1.refs_0_.pos_ref
  78.8 0.7 copy-done.17
  79.5 0.8 copy-done.19
  80.3 9.6 %project_qkv.1 = bf16[544,3072]{1,0:T(8,128)(2,1)} custom-call(s32[4]{0:T(128)} %pad_add_fusion.1.refs_0_.pos_ref, bf16[128,3072]{1,0:T(8,128)(2,1)} %refs_1_.4, bf16[384,1024]{1,0:T(8,128)(2,1)} %copy-done.1, bf16[384,1024]{1,0:T(8,128)(2,1)} %copy-done.3, bf16[384,1024]{1,0:T(8,128)(2,1)} %copy-done.5, bf16[192,1024]{1,0:T(8,128)(2,1)} %copy-done.15, ...), custom_call_target="tpu_custom_call" | custom-call | flops 1 | bytes 1 | tf_op jit(solution)/shard_map/project_qkv/pallas_call | solution.py:212
  90.9 1.9 collective-permute-start.23
  93.3 0.8 collective-permute-start.16
  94.1 10.2 %collective-permute-done.21 = bf16[512,256]{1,0:T(8,128)(2,1)S(1)} collective-permute-done((bf16[512,256]{1,0:T(8,128)(2,1)}, bf16[512,256]{1,0:T(8,128)(2,1)S(1)}, u32[]{:S(2)}, u32[]{:S(2)}) %collective-permute-start.21) | collective-permute-done | bytes 262176 | tf_op jit(solution)/shard_map/ppermute | solution.py:52
  104.3 1.5 collective-permute-start.22
  105.8 1.9 %copy-done = bf16[544,3072]{1,0:T(8,128)(2,1)S(1)} copy-done((bf16[544,3072]{1,0:T(8,128)(2,1)S(1)}, bf16[544,3072]{1,0:T(8,128)(2,1)}, u32[]{:S(2)}) %copy-start) | copy-done | bytes 3342360
  107.8 7.4 %attend.1 = bf16[2,272,1024]{2,1,0:T(8,128)(2,1)S(1)} custom-call(bf16[2,272,3072]{2,1,0:T(8,128)(2,1)S(1)} %bitcast.24, bf16[2,272,3072]{2,1,0:T(8,128)(2,1)S(1)} %bitcast.25, bf16[2,272,3072]{2,1,0:T(8,128)(2,1)S(1)} %bitcast.26), custom_call_target="tpu_custom_call" | custom-call | flops 1 | bytes 1 | tf_op jit(solution)/shard_map/attend/pallas_call | solution.py:308
  115.9 0.8 collective-permute-start.25
  116.7 1.2 collective-permute-start.26
  117.8 1.3 collective-permute-start.27
  119.3 5.8 %project_out.1 = (bf16[544,1024]{1,0:T(8,128)(2,1)S(1)}, bf16[544,1024]{1,0:T(8,128)(2,1)S(1)}) custom-call(s32[4]{0:T(128)S(1)} %copy-done.27, bf16[128,1024]{1,0:T(8,128)(2,1)S(1)} %copy-done.24, bf16[384,1024]{1,0:T(8,128)(2,1)S(1)} %copy-done.2, bf16[384,1024]{1,0:T(8,128)(2,1)S(1)} %copy-done.4, bf16[384,1024]{1,0:T(8,128)(2,1)S(1)} %copy-done.6, ...), custom_call_target="tpu_custom_call" | custom-call | flops 1 | bytes 1 | tf_op jit(solution)/shard_map/project_out/pallas_call | solution.py:212
  125.2 1.5 collective-permute-done.25.refs_5_
  127.0 1.2 collective-permute-start.30
  128.2 1.2 collective-permute-start.34
  130.1 0.7 collective-permute-start.33
  130.9 1.6 collective-permute-start.36
  132.4 9.1 %project_up.1.refs_15_ = bf16[544,4096]{1,0:T(8,128)(2,1)S(1)} custom-call(s32[4]{0:T(128)S(1)} %copy-done.27, bf16[128,4096]{1,0:T(8,128)(2,1)S(1)} %copy-done.14, bf16[384,1024]{1,0:T(8,128)(2,1)S(1)} %copy-done.11, bf16[384,1024]{1,0:T(8,128)(2,1)S(1)} %collective-permute-done.15.refs_3_, bf16[384,1024]{1,0:T(8,128)(2,1)S(1)} %collective-permute-done.16.refs_4_, ...), custom_call_target="tpu_custom_call" | custom-call | flops 1 | bytes 1 | tf_op jit(solution)/shard_map/project_up/pallas_call | solution.py:212
  141.5 9.4 %collective-permute-done.32.refs_6_ = bf16[512,256]{1,0:T(8,128)(2,1)S(1)} collective-permute-done((bf16[512,256]{1,0:T(8,128)(2,1)S(1)}, bf16[512,256]{1,0:T(8,128)(2,1)S(1)}, u32[]{:S(2)}, u32[]{:S(2)}) %collective-permute-start.32) | collective-permute-done | bytes 262176 | tf_op jit(solution)/shard_map/ppermute | solution.py:52
  152.5 2.4 %collective-permute-done.39.refs_12_ = bf16[512,256]{1,0:T(8,128)(2,1)S(1)} collective-permute-done((bf16[512,256]{1,0:T(8,128)(2,1)S(1)}, bf16[512,256]{1,0:T(8,128)(2,1)S(1)}, u32[]{:S(2)}, u32[]{:S(2)}) %collective-permute-start.39) | collective-permute-done | bytes 262176 | tf_op jit(solution)/shard_map/ppermute | solution.py:52
  155.7 13.0 %project_down.1 = bf16[32,2,1792]{2,1,0:T(2,128)(2,1)S(1)} custom-call(s32[4]{0:T(128)S(1)} %copy-done.27, bf16[512,1024]{1,0:T(8,128)(2,1)S(1)} %copy-done.13, bf16[1536,256]{1,0:T(8,128)(2,1)S(1)} %pad_maximum_fusion.2.refs_2_, bf16[1536,256]{1,0:T(8,128)(2,1)S(1)} %collective-permute-done.34.refs_3_, ...), custom_call_target="tpu_custom_call" | custom-call | flops 1 | bytes 1 | tf_op jit(solution)/shard_map/project_down/pallas_call | solution.py:212
  168.7 11.8 %all_to_all.16 = bf16[32,2,1792]{2,1,0:T(2,128)(2,1)S(1)} all-to-all(bf16[32,2,1792]{2,1,0:T(2,128)(2,1)S(1)} %project_down.1), channel_id=1, replica_groups=mesh['grp'=4,'fsdp'=8] {'grp','fsdp'}, dimensions={0} | all-to-all | bytes 458752 | tf_op jit(solution)/shard_map/all_to_all | solution.py:611
  180.5 0.8 reshape.99.every_ref
  181.3 5.9 %update.1 = (f32[2048,256]{1,0:T(8,128)}, f32[2048,256]{1,0:T(8,128)}, f32[2,256]{1,0:T(2,128)}, f32[32,256]{1,0:T(8,128)}) custom-call(s32[4]{0:T(128)} %pad_add_fusion.1.refs_0_.pos_ref, bf16[64,1792]{1,0:T(8,128)(2,1)} %reshape.99.every_ref, bf16[1024,256]{1,0:T(8,128)(2,1)} %proj_ref.1, bf16[2048,64]{1,0:T(8,128)(2,1)} %bitcast.33, ...), custom_call_target="tpu_custom_call" | custom-call | tf_op jit(solution)/shard_map/update/pallas_call | solution.py:463
  (130 shorter events, 8.1 us)
Async XLA Ops:
  0.6 16.1 %copy-start.34 = (s32[32]{0:T(128)S(1)}, s32[32]{0:T(128)}, u32[]{:S(2)}) copy-start(s32[32]{0:T(128)} %param.25) | copy-start | bytes 388
  0.6 16.7 %copy-start.31 = (bf16[2,257,1024]{2,0,1:T(2,128)(2,1)S(1)}, bf16[2,257,1024]{2,0,1:T(2,128)(2,1)}, u32[]{:S(2)}) copy-start(bf16[2,257,1024]{2,0,1:T(2,128)(2,1)} %param.14) | copy-start | bytes 3158020
  2.5 15.1 %copy-start.28 = (f32[1024]{0:T(1024)S(1)}, f32[1024]{0:T(1024)}, u32[]{:S(2)}) copy-start(f32[1024]{0:T(1024)} %param.15) | copy-start | bytes 12292
  2.6 31.0 %collective-permute-start.3 = (bf16[128,3072]{1,0:T(8,128)(2,1)}, bf16[128,3072]{1,0:T(8,128)(2,1)S(1)}, u32[]{:S(2)}, u32[]{:S(2)}) collective-permute-start(bf16[128,3072]{1,0:T(8,128)(2,1)} %refs_1_.4), channel_id=1, source_target_pairs={{0,1},{1,0},{2,3},{3,2},{4,5},{5,4},{6,7},{7,6},{8,9},{9,8},{10,11... | collective-permute-start | bytes 2359304 | tf_op jit(solution)/shard_map/ppermute | solution.py:52
  2.7 18.6 %collective-permute-start = (bf16[128,1024]{1,0:T(8,128)(2,1)S(1)}, bf16[128,1024]{1,0:T(8,128)(2,1)}, u32[]{:S(2)}, u32[]{:S(2)}) collective-permute-start(bf16[128,1024]{1,0:T(8,128)(2,1)S(1)} %pad_maximum_fusion.3), channel_id=1, source_target_pairs={{0,6},{1,7},{2,0},{3,1},{4,2},{5,3},{6,4},{7,5},{8,14},{9,15},{10,... | collective-permute-start | bytes 786440 | tf_op jit(solution)/shard_map/ppermute | solution.py:52
  7.5 22.9 %collective-permute-start.1 = (bf16[128,1024]{1,0:T(8,128)(2,1)S(1)}, bf16[128,1024]{1,0:T(8,128)(2,1)}, u32[]{:S(2)}, u32[]{:S(2)}) collective-permute-start(bf16[128,1024]{1,0:T(8,128)(2,1)S(1)} %pad_maximum_fusion.3), channel_id=1, source_target_pairs={{0,4},{1,5},{2,6},{3,7},{4,0},{5,1},{6,2},{7,3},{8,12},{9,13},{10,... | collective-permute-start | bytes 786440 | tf_op jit(solution)/shard_map/ppermute | solution.py:52
  7.5 22.9 %collective-permute-start.2 = (bf16[128,1024]{1,0:T(8,128)(2,1)S(1)}, bf16[128,1024]{1,0:T(8,128)(2,1)}, u32[]{:S(2)}, u32[]{:S(2)}) collective-permute-start(bf16[128,1024]{1,0:T(8,128)(2,1)S(1)} %pad_maximum_fusion.3), channel_id=1, source_target_pairs={{0,2},{1,3},{2,4},{3,5},{4,6},{5,7},{6,0},{7,1},{8,10},{9,11},{10,... | collective-permute-start | bytes 786440 | tf_op jit(solution)/shard_map/ppermute | solution.py:52
  7.9 24.9 %collective-permute-start.4 = (bf16[128,1024]{1,0:T(8,128)(2,1)}, bf16[128,1024]{1,0:T(8,128)(2,1)S(1)}, u32[]{:S(2)}, u32[]{:S(2)}) collective-permute-start(bf16[128,1024]{1,0:T(8,128)(2,1)} %refs_1_.5), channel_id=1, source_target_pairs={{0,1},{1,0},{2,3},{3,2},{4,5},{5,4},{6,7},{7,6},{8,9},{9,8},{10,11... | collective-permute-start | bytes 786440 | tf_op jit(solution)/shard_map/ppermute | solution.py:52
  10.1 22.7 %all-to-all-start = ((s32[32,2,128]{2,1,0:T(2,128)}), s32[32,2,128]{2,1,0:T(2,128)S(1)}, u32[]{:S(2)}, u32[]{:S(2)}) async-start(s32[32,2,128]{2,1,0:T(2,128)} %broadcast_in_dim.12), calls=%async_computation | async-start | bytes 65536 | tf_op jit(solution)/shard_map/all_to_all | solution.py:488
  31.5 15.7 %copy-start.1 = (bf16[384,1024]{1,0:T(8,128)(2,1)}, bf16[384,1024]{1,0:T(8,128)(2,1)S(1)}, u32[]{:S(2)}) copy-start(bf16[384,1024]{1,0:T(8,128)(2,1)S(1)} %pad_maximum_fusion.refs_2_) | copy-start | bytes 2359300
  33.5 19.0 %collective-permute-start.5 = (bf16[384,1024]{1,0:T(8,128)(2,1)S(1)}, bf16[384,1024]{1,0:T(8,128)(2,1)S(1)}, u32[]{:S(2)}, u32[]{:S(2)}) collective-permute-start(bf16[384,1024]{1,0:T(8,128)(2,1)S(1)} %pad_maximum_fusion.refs_2_), channel_id=1, source_target_pairs={{0,8},{1,9},{2,10},{3,11},{4,12},{5,13},{6,14},{7,15},{8,0},{9,1},... | collective-permute-start | bytes 2359304 | tf_op jit(solution)/shard_map/ppermute | solution.py:52
  34.4 18.7 %collective-permute-start.6 = (bf16[384,1024]{1,0:T(8,128)(2,1)S(1)}, bf16[384,1024]{1,0:T(8,128)(2,1)S(1)}, u32[]{:S(2)}, u32[]{:S(2)}) collective-permute-start(bf16[384,1024]{1,0:T(8,128)(2,1)S(1)} %pad_maximum_fusion.refs_2_), channel_id=1, source_target_pairs={{0,16},{1,17},{2,18},{3,19},{4,20},{5,21},{6,22},{7,23},{8,24},{9,... | collective-permute-start | bytes 2359304 | tf_op jit(solution)/shard_map/ppermute | solution.py:52
  34.8 18.4 %collective-permute-start.9 = (bf16[384,1024]{1,0:T(8,128)(2,1)S(1)}, bf16[384,1024]{1,0:T(8,128)(2,1)S(1)}, u32[]{:S(2)}, u32[]{:S(2)}) collective-permute-start(bf16[384,1024]{1,0:T(8,128)(2,1)S(1)} %pad_maximum_fusion.refs_2_), channel_id=1, source_target_pairs={{0,1},{1,0},{2,3},{3,2},{4,5},{5,4},{6,7},{7,6},{8,9},{9,8},{10,11... | collective-permute-start | bytes 2359304 | tf_op jit(solution)/shard_map/ppermute | solution.py:52
  36.3 10.8 %collective-permute-start.7 = (bf16[128,1024]{1,0:T(8,128)(2,1)}, bf16[128,1024]{1,0:T(8,128)(2,1)}, u32[]{:S(2)}, u32[]{:S(2)}) collective-permute-start(bf16[128,1024]{1,0:T(8,128)(2,1)} %constant_dynamic-slice_fusion.2), channel_id=1, source_target_pairs={{0,6},{1,7},{2,0},{3,1},{4,2},{5,3},{6,4},{7,5},{8,14},{9,15},{10,... | collective-permute-start | bytes 786440 | tf_op jit(solution)/shard_map/ppermute | solution.py:52
  38.9 13.6 %collective-permute-start.8 = (bf16[128,1024]{1,0:T(8,128)(2,1)}, bf16[128,1024]{1,0:T(8,128)(2,1)}, u32[]{:S(2)}, u32[]{:S(2)}) collective-permute-start(bf16[128,1024]{1,0:T(8,128)(2,1)} %constant_dynamic-slice_fusion.2), channel_id=1, source_target_pairs={{0,2},{1,3},{2,4},{3,5},{4,6},{5,7},{6,0},{7,1},{8,10},{9,11},{10,... | collective-permute-start | bytes 786440 | tf_op jit(solution)/shard_map/ppermute | solution.py:52
  52.5 23.2 %copy-start.3 = (bf16[384,1024]{1,0:T(8,128)(2,1)}, bf16[384,1024]{1,0:T(8,128)(2,1)S(1)}, u32[]{:S(2)}) copy-start(bf16[384,1024]{1,0:T(8,128)(2,1)S(1)} %collective-permute-done.5.refs_3_) | copy-start | bytes 2359300
  53.1 22.6 %copy-start.5 = (bf16[384,1024]{1,0:T(8,128)(2,1)}, bf16[384,1024]{1,0:T(8,128)(2,1)S(1)}, u32[]{:S(2)}) copy-start(bf16[384,1024]{1,0:T(8,128)(2,1)S(1)} %collective-permute-done.6.refs_4_) | copy-start | bytes 2359300
  53.1 22.6 %copy-start.7 = (bf16[384,1024]{1,0:T(8,128)(2,1)}, bf16[384,1024]{1,0:T(8,128)(2,1)S(1)}, u32[]{:S(2)}) copy-start(bf16[384,1024]{1,0:T(8,128)(2,1)S(1)} %collective-permute-done.9.refs_8_) | copy-start | bytes 2359300
  53.1 22.6 %collective-permute-start.13 = (bf16[384,1024]{1,0:T(8,128)(2,1)S(1)}, bf16[384,1024]{1,0:T(8,128)(2,1)S(1)}, u32[]{:S(2)}, u32[]{:S(2)}) collective-permute-start(bf16[384,1024]{1,0:T(8,128)(2,1)S(1)} %collective-permute-done.5.refs_3_), channel_id=1, source_target_pairs={{0,1},{1,0},{2,3},{3,2},{4,5},{5,4},{6,7},{7,6},{8,9},{9,8},{10,11... | collective-permute-start | bytes 2359304 | tf_op jit(solution)/shard_map/ppermute | solution.py:52
  54.4 21.3 %collective-permute-start.14 = (bf16[384,1024]{1,0:T(8,128)(2,1)S(1)}, bf16[384,1024]{1,0:T(8,128)(2,1)}, u32[]{:S(2)}, u32[]{:S(2)}) collective-permute-start(bf16[384,1024]{1,0:T(8,128)(2,1)S(1)} %collective-permute-done.6.refs_4_), channel_id=1, source_target_pairs={{0,1},{1,0},{2,3},{3,2},{4,5},{5,4},{6,7},{7,6},{8,9},{9,8},{10,11... | collective-permute-start | bytes 2359304 | tf_op jit(solution)/shard_map/ppermute | solution.py:52
  54.5 19.1 %collective-permute-start.12 = (bf16[128,1024]{1,0:T(8,128)(2,1)}, bf16[128,1024]{1,0:T(8,128)(2,1)}, u32[]{:S(2)}, u32[]{:S(2)}) collective-permute-start(bf16[128,1024]{1,0:T(8,128)(2,1)} %constant_dynamic-slice_fusion.2), channel_id=1, source_target_pairs={{0,4},{1,5},{2,6},{3,7},{4,0},{5,1},{6,2},{7,3},{8,12},{9,13},{10,... | collective-permute-start | bytes 786440 | tf_op jit(solution)/shard_map/ppermute | solution.py:52
  58.3 17.4 %collective-permute-start.10 = (bf16[192,1024]{1,0:T(8,128)(2,1)}, bf16[192,1024]{1,0:T(8,128)(2,1)S(1)}, u32[]{:S(2)}, u32[]{:S(2)}) collective-permute-start(bf16[192,1024]{1,0:T(8,128)(2,1)} %slice.20), channel_id=1, source_target_pairs={{0,16},{1,17},{2,18},{3,19},{4,20},{5,21},{6,22},{7,23},{8,24},{9,... | collective-permute-start | bytes 1179656 | tf_op jit(solution)/shard_map/ppermute | solution.py:52
  58.9 16.8 %collective-permute-start.11 = (bf16[192,1024]{1,0:T(8,128)(2,1)}, bf16[192,1024]{1,0:T(8,128)(2,1)}, u32[]{:S(2)}, u32[]{:S(2)}) collective-permute-start(bf16[192,1024]{1,0:T(8,128)(2,1)} %slice.21), channel_id=1, source_target_pairs={{0,8},{1,9},{2,10},{3,11},{4,12},{5,13},{6,14},{7,15},{8,0},{9,1},... | collective-permute-start | bytes 1179656 | tf_op jit(solution)/shard_map/ppermute | solution.py:52
  75.8 3.0 %collective-permute-start.17 = (bf16[192,1024]{1,0:T(8,128)(2,1)S(1)}, bf16[192,1024]{1,0:T(8,128)(2,1)S(1)}, u32[]{:S(2)}, u32[]{:S(2)}) collective-permute-start(bf16[192,1024]{1,0:T(8,128)(2,1)S(1)} %collective-permute-done.10.refs_5_), channel_id=1, source_target_pairs={{0,1},{1,0},{2,3},{3,2},{4,5},{5,4},{6,7},{7,6},{8,9},{9,8},{10,11... | collective-permute-start | bytes 1179656 | tf_op jit(solution)/shard_map/ppermute | solution.py:52
  76.2 2.6 %collective-permute-start.18 = (bf16[192,1024]{1,0:T(8,128)(2,1)}, bf16[192,1024]{1,0:T(8,128)(2,1)S(1)}, u32[]{:S(2)}, u32[]{:S(2)}) collective-permute-start(bf16[192,1024]{1,0:T(8,128)(2,1)} %collective-permute-done.11.refs_6_), channel_id=1, source_target_pairs={{0,1},{1,0},{2,3},{3,2},{4,5},{5,4},{6,7},{7,6},{8,9},{9,8},{10,11... | collective-permute-start | bytes 1179656 | tf_op jit(solution)/shard_map/ppermute | solution.py:52
  76.3 13.6 %collective-permute-start.19 = (bf16[512,256]{1,0:T(8,128)(2,1)}, bf16[512,256]{1,0:T(8,128)(2,1)S(1)}, u32[]{:S(2)}, u32[]{:S(2)}) collective-permute-start(bf16[512,256]{1,0:T(8,128)(2,1)} %get-tuple-element.83), channel_id=1, source_target_pairs={{0,6},{1,7},{2,0},{3,1},{4,2},{5,3},{6,4},{7,5},{8,14},{9,15},{10,... | collective-permute-start | bytes 786440 | tf_op jit(solution)/shard_map/ppermute | solution.py:52
  78.1 12.2 %collective-permute-start.20 = (bf16[512,256]{1,0:T(8,128)(2,1)}, bf16[512,256]{1,0:T(8,128)(2,1)S(1)}, u32[]{:S(2)}, u32[]{:S(2)}) collective-permute-start(bf16[512,256]{1,0:T(8,128)(2,1)} %get-tuple-element.83), channel_id=1, source_target_pairs={{0,2},{1,3},{2,4},{3,5},{4,6},{5,7},{6,0},{7,1},{8,10},{9,11},{10,... | collective-permute-start | bytes 786440 | tf_op jit(solution)/shard_map/ppermute | solution.py:52
  78.8 12.1 %copy-start.14 = (bf16[128,4096]{1,0:T(8,128)(2,1)S(1)}, bf16[128,4096]{1,0:T(8,128)(2,1)}, u32[]{:S(2)}) copy-start(bf16[128,4096]{1,0:T(8,128)(2,1)} %refs_1_.6) | copy-start | bytes 3145732
  78.8 13.9 %copy-start.13 = (bf16[512,1024]{1,0:T(8,128)(2,1)S(1)}, bf16[512,1024]{1,0:T(8,128)(2,1)}, u32[]{:S(2)}) copy-start(bf16[512,1024]{1,0:T(8,128)(2,1)} %refs_1_.7) | copy-start | bytes 3145732
  78.8 14.0 %copy-start.11 = (bf16[384,1024]{1,0:T(8,128)(2,1)S(1)}, bf16[384,1024]{1,0:T(8,128)(2,1)}, u32[]{:S(2)}) copy-start(bf16[384,1024]{1,0:T(8,128)(2,1)} %pad_maximum_fusion.1.refs_2_) | copy-start | bytes 2359300
  90.3 14.0 %collective-permute-start.21 = (bf16[512,256]{1,0:T(8,128)(2,1)}, bf16[512,256]{1,0:T(8,128)(2,1)S(1)}, u32[]{:S(2)}, u32[]{:S(2)}) collective-permute-start(bf16[512,256]{1,0:T(8,128)(2,1)} %get-tuple-element.83), channel_id=1, source_target_pairs={{0,4},{1,5},{2,6},{3,7},{4,0},{5,1},{6,2},{7,3},{8,12},{9,13},{10,... | collective-permute-start | bytes 786440 | tf_op jit(solution)/shard_map/ppermute | solution.py:52
  90.9 24.4 %collective-permute-start.23 = (bf16[128,4096]{1,0:T(8,128)(2,1)S(1)}, bf16[128,4096]{1,0:T(8,128)(2,1)S(1)}, u32[]{:S(2)}, u32[]{:S(2)}) collective-permute-start(bf16[128,4096]{1,0:T(8,128)(2,1)S(1)} %copy-done.14), channel_id=1, source_target_pairs={{0,1},{1,0},{2,3},{3,2},{4,5},{5,4},{6,7},{7,6},{8,9},{9,8},{10,11... | collective-permute-start | bytes 3145736 | tf_op jit(solution)/shard_map/ppermute | solution.py:52
  92.7 22.5 %collective-permute-start.24 = (bf16[512,1024]{1,0:T(8,128)(2,1)S(1)}, bf16[512,1024]{1,0:T(8,128)(2,1)S(1)}, u32[]{:S(2)}, u32[]{:S(2)}) collective-permute-start(bf16[512,1024]{1,0:T(8,128)(2,1)S(1)} %copy-done.13), channel_id=1, source_target_pairs={{0,1},{1,0},{2,3},{3,2},{4,5},{5,4},{6,7},{7,6},{8,9},{9,8},{10,11... | collective-permute-start | bytes 3145736 | tf_op jit(solution)/shard_map/ppermute | solution.py:52
  92.8 22.4 %collective-permute-start.15 = (bf16[384,1024]{1,0:T(8,128)(2,1)S(1)}, bf16[384,1024]{1,0:T(8,128)(2,1)S(1)}, u32[]{:S(2)}, u32[]{:S(2)}) collective-permute-start(bf16[384,1024]{1,0:T(8,128)(2,1)S(1)} %copy-done.11), channel_id=1, source_target_pairs={{0,8},{1,9},{2,10},{3,11},{4,12},{5,13},{6,14},{7,15},{8,0},{9,1},... | collective-permute-start | bytes 2359304 | tf_op jit(solution)/shard_map/ppermute | solution.py:52
  93.3 21.9 %collective-permute-start.16 = (bf16[384,1024]{1,0:T(8,128)(2,1)S(1)}, bf16[384,1024]{1,0:T(8,128)(2,1)S(1)}, u32[]{:S(2)}, u32[]{:S(2)}) collective-permute-start(bf16[384,1024]{1,0:T(8,128)(2,1)S(1)} %copy-done.11), channel_id=1, source_target_pairs={{0,16},{1,17},{2,18},{3,19},{4,20},{5,21},{6,22},{7,23},{8,24},{9,... | collective-permute-start | bytes 2359304 | tf_op jit(solution)/shard_map/ppermute | solution.py:52
  104.3 10.9 %collective-permute-start.22 = (bf16[384,1024]{1,0:T(8,128)(2,1)S(1)}, bf16[384,1024]{1,0:T(8,128)(2,1)S(1)}, u32[]{:S(2)}, u32[]{:S(2)}) collective-permute-start(bf16[384,1024]{1,0:T(8,128)(2,1)S(1)} %copy-done.11), channel_id=1, source_target_pairs={{0,1},{1,0},{2,3},{3,2},{4,5},{5,4},{6,7},{7,6},{8,9},{9,8},{10,11... | collective-permute-start | bytes 2359304 | tf_op jit(solution)/shard_map/ppermute | solution.py:52
  107.7 10.1 %copy-start.33 = (bf16[512,256]{1,0:T(8,128)(2,1)S(1)}, bf16[512,256]{1,0:T(8,128)(2,1)}, u32[]{:S(2)}) copy-start(bf16[512,256]{1,0:T(8,128)(2,1)} %get-tuple-element.111) | copy-start | bytes 786436
  107.7 11.5 %copy-start.6 = (bf16[384,1024]{1,0:T(8,128)(2,1)S(1)}, bf16[384,1024]{1,0:T(8,128)(2,1)}, u32[]{:S(2)}) copy-start(bf16[384,1024]{1,0:T(8,128)(2,1)} %copy-done.5) | copy-start | bytes 2359300
  107.7 11.5 %copy-start.8 = (bf16[384,1024]{1,0:T(8,128)(2,1)S(1)}, bf16[384,1024]{1,0:T(8,128)(2,1)}, u32[]{:S(2)}) copy-start(bf16[384,1024]{1,0:T(8,128)(2,1)} %copy-done.7) | copy-start | bytes 2359300
  107.7 11.5 %copy-start.10 = (bf16[384,1024]{1,0:T(8,128)(2,1)S(1)}, bf16[384,1024]{1,0:T(8,128)(2,1)}, u32[]{:S(2)}) copy-start(bf16[384,1024]{1,0:T(8,128)(2,1)} %copy-done.9) | copy-start | bytes 2359300
  107.7 11.5 %copy-start.16 = (bf16[192,1024]{1,0:T(8,128)(2,1)S(1)}, bf16[192,1024]{1,0:T(8,128)(2,1)}, u32[]{:S(2)}) copy-start(bf16[192,1024]{1,0:T(8,128)(2,1)} %copy-done.15) | copy-start | bytes 1179652
  107.7 11.4 %copy-start.18 = (bf16[192,1024]{1,0:T(8,128)(2,1)S(1)}, bf16[192,1024]{1,0:T(8,128)(2,1)}, u32[]{:S(2)}) copy-start(bf16[192,1024]{1,0:T(8,128)(2,1)} %copy-done.17) | copy-start | bytes 1179652
  107.7 11.4 %copy-start.20 = (bf16[192,1024]{1,0:T(8,128)(2,1)S(1)}, bf16[192,1024]{1,0:T(8,128)(2,1)}, u32[]{:S(2)}) copy-start(bf16[192,1024]{1,0:T(8,128)(2,1)} %copy-done.19) | copy-start | bytes 1179652
  107.7 11.4 %copy-start.23 = (bf16[544,1024]{1,0:T(8,128)(2,1)S(1)}, bf16[544,1024]{1,0:T(8,128)(2,1)}, u32[]{:S(2)}) copy-start(bf16[544,1024]{1,0:T(8,128)(2,1)} %copy-done.22) | copy-start | bytes 3342340
  107.8 11.4 %copy-start.24 = (bf16[128,1024]{1,0:T(8,128)(2,1)S(1)}, bf16[128,1024]{1,0:T(8,128)(2,1)}, u32[]{:S(2)}) copy-start(bf16[128,1024]{1,0:T(8,128)(2,1)} %refs_1_.5) | copy-start | bytes 786436
  107.8 11.4 %copy-start.26 = (bf16[128,1024]{1,0:T(8,128)(2,1)S(1)}, bf16[128,1024]{1,0:T(8,128)(2,1)}, u32[]{:S(2)}) copy-start(bf16[128,1024]{1,0:T(8,128)(2,1)} %copy-done.25) | copy-start | bytes 786436
  115.2 9.9 %collective-permute-start.28 = (bf16[384,1024]{1,0:T(8,128)(2,1)S(1)}, bf16[384,1024]{1,0:T(8,128)(2,1)S(1)}, u32[]{:S(2)}, u32[]{:S(2)}) collective-permute-start(bf16[384,1024]{1,0:T(8,128)(2,1)S(1)} %collective-permute-done.15.refs_3_), channel_id=1, source_target_pairs={{0,1},{1,0},{2,3},{3,2},{4,5},{5,4},{6,7},{7,6},{8,9},{9,8},{10,11... | collective-permute-start | bytes 2359304 | tf_op jit(solution)/shard_map/ppermute | solution.py:52
  115.3 9.8 %collective-permute-start.29 = (bf16[384,1024]{1,0:T(8,128)(2,1)S(1)}, bf16[384,1024]{1,0:T(8,128)(2,1)S(1)}, u32[]{:S(2)}, u32[]{:S(2)}) collective-permute-start(bf16[384,1024]{1,0:T(8,128)(2,1)S(1)} %collective-permute-done.16.refs_4_), channel_id=1, source_target_pairs={{0,1},{1,0},{2,3},{3,2},{4,5},{5,4},{6,7},{7,6},{8,9},{9,8},{10,11... | collective-permute-start | bytes 2359304 | tf_op jit(solution)/shard_map/ppermute | solution.py:52
  115.9 10.8 %collective-permute-start.25 = (bf16[192,1024]{1,0:T(8,128)(2,1)S(1)}, bf16[192,1024]{1,0:T(8,128)(2,1)S(1)}, u32[]{:S(2)}, u32[]{:S(2)}) collective-permute-start(bf16[192,1024]{1,0:T(8,128)(2,1)S(1)} %slice.22), channel_id=1, source_target_pairs={{0,16},{1,17},{2,18},{3,19},{4,20},{5,21},{6,22},{7,23},{8,24},{9,... | collective-permute-start | bytes 1179656 | tf_op jit(solution)/shard_map/ppermute | solution.py:52
  116.7 10.4 %collective-permute-start.26 = (bf16[192,1024]{1,0:T(8,128)(2,1)S(1)}, bf16[192,1024]{1,0:T(8,128)(2,1)S(1)}, u32[]{:S(2)}, u32[]{:S(2)}) collective-permute-start(bf16[192,1024]{1,0:T(8,128)(2,1)S(1)} %slice.23), channel_id=1, source_target_pairs={{0,8},{1,9},{2,10},{3,11},{4,12},{5,13},{6,14},{7,15},{8,0},{9,1},... | collective-permute-start | bytes 1179656 | tf_op jit(solution)/shard_map/ppermute | solution.py:52
  117.8 7.3 %collective-permute-start.27 = (bf16[512,256]{1,0:T(8,128)(2,1)S(1)}, bf16[512,256]{1,0:T(8,128)(2,1)S(1)}, u32[]{:S(2)}, u32[]{:S(2)}) collective-permute-start(bf16[512,256]{1,0:T(8,128)(2,1)S(1)} %copy-done.33), channel_id=1, source_target_pairs={{0,6},{1,7},{2,0},{3,1},{4,2},{5,3},{6,4},{7,5},{8,14},{9,15},{10,... | collective-permute-start | bytes 786440 | tf_op jit(solution)/shard_map/ppermute | solution.py:52
  127.0 28.6 %copy-start.30 = (f32[1024]{0:T(1024)S(1)}, f32[1024]{0:T(1024)}, u32[]{:S(2)}) copy-start(f32[1024]{0:T(1024)} %param.21) | copy-start | bytes 12292
  127.0 2.8 %collective-permute-start.30 = (bf16[192,1024]{1,0:T(8,128)(2,1)S(1)}, bf16[192,1024]{1,0:T(8,128)(2,1)S(1)}, u32[]{:S(2)}, u32[]{:S(2)}) collective-permute-start(bf16[192,1024]{1,0:T(8,128)(2,1)S(1)} %collective-permute-done.25.refs_5_), channel_id=1, source_target_pairs={{0,1},{1,0},{2,3},{3,2},{4,5},{5,4},{6,7},{7,6},{8,9},{9,8},{10,11... | collective-permute-start | bytes 1179656 | tf_op jit(solution)/shard_map/ppermute | solution.py:52
  128.2 1.9 %collective-permute-start.31 = (bf16[192,1024]{1,0:T(8,128)(2,1)S(1)}, bf16[192,1024]{1,0:T(8,128)(2,1)S(1)}, u32[]{:S(2)}, u32[]{:S(2)}) collective-permute-start(bf16[192,1024]{1,0:T(8,128)(2,1)S(1)} %collective-permute-done.26.refs_6_), channel_id=1, source_target_pairs={{0,1},{1,0},{2,3},{3,2},{4,5},{5,4},{6,7},{7,6},{8,9},{9,8},{10,11... | collective-permute-start | bytes 1179656 | tf_op jit(solution)/shard_map/ppermute | solution.py:52
  128.2 22.8 %collective-permute-start.34 = (bf16[1536,256]{1,0:T(8,128)(2,1)S(1)}, bf16[1536,256]{1,0:T(8,128)(2,1)S(1)}, u32[]{:S(2)}, u32[]{:S(2)}) collective-permute-start(bf16[1536,256]{1,0:T(8,128)(2,1)S(1)} %pad_maximum_fusion.2.refs_2_), channel_id=1, source_target_pairs={{0,8},{1,9},{2,10},{3,11},{4,12},{5,13},{6,14},{7,15},{8,0},{9,1},... | collective-permute-start | bytes 2359304 | tf_op jit(solution)/shard_map/ppermute | solution.py:52
  129.4 21.6 %collective-permute-start.35 = (bf16[1536,256]{1,0:T(8,128)(2,1)S(1)}, bf16[1536,256]{1,0:T(8,128)(2,1)S(1)}, u32[]{:S(2)}, u32[]{:S(2)}) collective-permute-start(bf16[1536,256]{1,0:T(8,128)(2,1)S(1)} %pad_maximum_fusion.2.refs_2_), channel_id=1, source_target_pairs={{0,16},{1,17},{2,18},{3,19},{4,20},{5,21},{6,22},{7,23},{8,24},{9,... | collective-permute-start | bytes 2359304 | tf_op jit(solution)/shard_map/ppermute | solution.py:52
  130.1 20.9 %collective-permute-start.33 = (bf16[1536,256]{1,0:T(8,128)(2,1)S(1)}, bf16[1536,256]{1,0:T(8,128)(2,1)S(1)}, u32[]{:S(2)}, u32[]{:S(2)}) collective-permute-start(bf16[1536,256]{1,0:T(8,128)(2,1)S(1)} %pad_maximum_fusion.2.refs_2_), channel_id=1, source_target_pairs={{0,1},{1,0},{2,3},{3,2},{4,5},{5,4},{6,7},{7,6},{8,9},{9,8},{10,11... | collective-permute-start | bytes 2359304 | tf_op jit(solution)/shard_map/ppermute | solution.py:52
  130.8 20.1 %collective-permute-start.32 = (bf16[512,256]{1,0:T(8,128)(2,1)S(1)}, bf16[512,256]{1,0:T(8,128)(2,1)S(1)}, u32[]{:S(2)}, u32[]{:S(2)}) collective-permute-start(bf16[512,256]{1,0:T(8,128)(2,1)S(1)} %copy-done.33), channel_id=1, source_target_pairs={{0,4},{1,5},{2,6},{3,7},{4,0},{5,1},{6,2},{7,3},{8,12},{9,13},{10,... | collective-permute-start | bytes 786440 | tf_op jit(solution)/shard_map/ppermute | solution.py:52
  130.9 20.1 %collective-permute-start.36 = (bf16[512,256]{1,0:T(8,128)(2,1)S(1)}, bf16[512,256]{1,0:T(8,128)(2,1)S(1)}, u32[]{:S(2)}, u32[]{:S(2)}) collective-permute-start(bf16[512,256]{1,0:T(8,128)(2,1)S(1)} %copy-done.33), channel_id=1, source_target_pairs={{0,2},{1,3},{2,4},{3,5},{4,6},{5,7},{6,0},{7,1},{8,10},{9,11},{10,... | collective-permute-start | bytes 786440 | tf_op jit(solution)/shard_map/ppermute | solution.py:52
  151.0 4.7 %collective-permute-start.37 = (bf16[1536,256]{1,0:T(8,128)(2,1)S(1)}, bf16[1536,256]{1,0:T(8,128)(2,1)S(1)}, u32[]{:S(2)}, u32[]{:S(2)}) collective-permute-start(bf16[1536,256]{1,0:T(8,128)(2,1)S(1)} %collective-permute-done.34.refs_3_), channel_id=1, source_target_pairs={{0,1},{1,0},{2,3},{3,2},{4,5},{5,4},{6,7},{7,6},{8,9},{9,8},{10,11... | collective-permute-start | bytes 2359304 | tf_op jit(solution)/shard_map/ppermute | solution.py:52
  151.5 4.2 %collective-permute-start.38 = (bf16[1536,256]{1,0:T(8,128)(2,1)S(1)}, bf16[1536,256]{1,0:T(8,128)(2,1)S(1)}, u32[]{:S(2)}, u32[]{:S(2)}) collective-permute-start(bf16[1536,256]{1,0:T(8,128)(2,1)S(1)} %collective-permute-done.35.refs_4_), channel_id=1, source_target_pairs={{0,1},{1,0},{2,3},{3,2},{4,5},{5,4},{6,7},{7,6},{8,9},{9,8},{10,11... | collective-permute-start | bytes 2359304 | tf_op jit(solution)/shard_map/ppermute | solution.py:52
  151.6 3.3 %collective-permute-start.39 = (bf16[512,256]{1,0:T(8,128)(2,1)S(1)}, bf16[512,256]{1,0:T(8,128)(2,1)S(1)}, u32[]{:S(2)}, u32[]{:S(2)}) collective-permute-start(bf16[512,256]{1,0:T(8,128)(2,1)S(1)} %collective-permute-done.27.refs_5_), channel_id=1, source_target_pairs={{0,1},{1,0},{2,3},{3,2},{4,5},{5,4},{6,7},{7,6},{8,9},{9,8},{10,11... | collective-permute-start | bytes 786440 | tf_op jit(solution)/shard_map/ppermute | solution.py:52
  152.0 3.3 %collective-permute-start.40 = (bf16[512,256]{1,0:T(8,128)(2,1)S(1)}, bf16[512,256]{1,0:T(8,128)(2,1)S(1)}, u32[]{:S(2)}, u32[]{:S(2)}) collective-permute-start(bf16[512,256]{1,0:T(8,128)(2,1)S(1)} %collective-permute-done.32.refs_6_), channel_id=1, source_target_pairs={{0,1},{1,0},{2,3},{3,2},{4,5},{5,4},{6,7},{7,6},{8,9},{9,8},{10,11... | collective-permute-start | bytes 786440 | tf_op jit(solution)/shard_map/ppermute | solution.py:52
  152.1 3.6 %collective-permute-start.41 = (bf16[512,256]{1,0:T(8,128)(2,1)S(1)}, bf16[512,256]{1,0:T(8,128)(2,1)S(1)}, u32[]{:S(2)}, u32[]{:S(2)}) collective-permute-start(bf16[512,256]{1,0:T(8,128)(2,1)S(1)} %collective-permute-done.36.refs_7_), channel_id=1, source_target_pairs={{0,1},{1,0},{2,3},{3,2},{4,5},{5,4},{6,7},{7,6},{8,9},{9,8},{10,11... | collective-permute-start | bytes 786440 | tf_op jit(solution)/shard_map/ppermute | solution.py:52
  (14 other events, 32.6 us)
